TPU v7x, 32 devices: a whole 2x2x4 slice. The times are simulated.
32 devices in a mesh: req: 4 (over x, core), exp: 8 (over z, y).
Axes of the slice: x: 2, y: 2, z: 4, core: 2. Of those that a mesh axis runs over, the one named last changes fastest.
Arguments:
- tokens: bfloat16 [2048, 2048], P(('req', 'exp')), may hold values from -6 to 6
- routes: int32 [2048, 2], P(('req', 'exp')), may hold values from 0 to 7, all different within a row; in each aligned block of 64 rows (0 to 63, 64 to 127, ...) at most 24 rows name the same one
- router: bfloat16 [2048, 8], replicated, may hold values from -0.26367188 to 0.26367188
- gate_weight: bfloat16 [2048, 90112], P(None, ('req', 'exp')), as said below
- up_weight: bfloat16 [2048, 90112], P(None, ('req', 'exp')), as said below
- down_weight: bfloat16 [90112, 2048], P(('req', 'exp')), as said below
- norm_gain: float32 [2048], replicated, may hold values from 0.5 to 1.5
- head_weight: bfloat16 [2048, 32000], P(None, 'exp'), may hold values from -0.39648438 to 0.39648438
- lengths: int32 [32, 4], P(('req', 'exp')), may hold values from 1 to 32, 64 in all within a row
Outputs:
- hidden_out: bfloat16 [2048, 2048], P(('req', 'exp'))
- request_norm: float32 [128], P(('req', 'exp'))
- request_max: float32 [128], P(('req', 'exp'))
Inputs may be any that keep to these rules, and one draw needn't show every extreme that they name: `routes`: within a row the two experts differ. In each aligned block of 64 rows (the rows of one device) no expert is named by more than 24 rows. Each device's 4 lengths sum to 64. `gate_weight`: the two copies are equal, as the steps say. `up_weight`: the two copies are equal, as the steps say. `down_weight`: the two copies are equal, as the steps say.
All inputs are finite; a program needn't handle non-finite values.
Results may differ from a plain program's by a relative error of at most 0.0036.
Values may be sent and summed in bfloat16 or wider, within the bound.
No kernel may reach another device: no remote copies, remote signals or barrier semaphores. Data moves between devices by JAX's collectives and lax.ppermute only.
A program may use at most 128 MiB of HBM per device.

v0:
```python
import jax
import jax.numpy as jnp
from jax import lax
from jax.sharding import PartitionSpec as P

D = 2048
CAP = 24


norm_eps = 1e-05


def expert_apply(routed_rows, w_gate, w_up, w_down):
    gate_act = jnp.dot(routed_rows, w_gate, preferred_element_type=jnp.float32)
    up_act = jnp.dot(routed_rows, w_up, preferred_element_type=jnp.float32)
    hidden = (jax.nn.silu(gate_act) * up_act).astype(jnp.bfloat16)
    return jnp.dot(hidden, w_down, preferred_element_type=jnp.float32)


def per_device(
    tokens, routes, router, gate_weight, up_weight, down_weight, norm_gain, head_weight, lengths
):
    row_count, model_width = tokens.shape
    experts = router.shape[1]
    capacity = CAP
    half_cap = capacity // 2
    req_count = lax.axis_size("req")
    exp_count = lax.axis_size("exp")
    devices = req_count * exp_count
    half_exp = exp_count // 2
    group_size = devices // (2 * experts)
    chosen_ids = routes.reshape(-1)
    onehot = (chosen_ids[:, None] == jnp.arange(experts, dtype=jnp.int32)[None, :]).astype(
        jnp.int32
    )
    slot_rank = jnp.sum((jnp.cumsum(onehot, axis=0) - 1) * onehot, axis=1)
    row_id = jnp.arange(row_count * 2, dtype=jnp.int32) // 2
    dispatch = (
        jnp.zeros((experts, capacity, model_width), jnp.bfloat16)
        .at[chosen_ids, slot_rank]
        .set(tokens[row_id])
    )
    gating = jax.nn.sigmoid(jnp.dot(tokens, router, preferred_element_type=jnp.float32))
    chosen = jnp.take_along_axis(gating, routes, axis=1)
    split_rows = dispatch.reshape(experts, 2, half_cap, model_width)
    outgoing = jnp.repeat(split_rows, group_size, axis=0)
    outgoing = outgoing.reshape(req_count, half_exp, 2, half_cap, model_width).transpose(
        0, 2, 1, 3, 4
    )
    outgoing = outgoing.reshape(devices, half_cap, model_width)
    arrived = lax.all_to_all(outgoing, ("req", "exp"), split_axis=0, concat_axis=0, tiled=True)
    item_count = arrived.shape[1]
    partial_value = expert_apply(
        arrived.reshape(-1, model_width), gate_weight, up_weight, down_weight
    )
    partial_value = partial_value.reshape(devices, item_count, model_width)
    returned = lax.all_to_all(
        partial_value, ("req", "exp"), split_axis=0, concat_axis=0, tiled=True
    )
    returned = returned.reshape(req_count, 2, half_exp, half_cap, model_width).transpose(
        0, 2, 1, 3, 4
    )
    returned = returned.reshape(experts, group_size, 2, half_cap, model_width)
    results = jnp.sum(returned, axis=1).reshape(experts, capacity, model_width)
    picked = results[chosen_ids, slot_rank].reshape(row_count, 2, model_width)
    branch_sum = jnp.sum(chosen[:, :, None] * picked, axis=1)
    hidden_out = (tokens.astype(jnp.float32) + branch_sum).astype(jnp.bfloat16)
    widened = hidden_out.astype(jnp.float32)
    row_sq = jnp.sum(widened * widened, axis=1)
    normed = (widened * lax.rsqrt(row_sq / D + norm_eps)[:, None] * norm_gain[None, :]).astype(
        jnp.bfloat16
    )
    row_part = jnp.max(
        jnp.dot(
            lax.all_gather(normed, "exp", axis=0, tiled=True),
            head_weight,
            preferred_element_type=jnp.float32,
        ),
        axis=1,
    )
    row_all = lax.pmax(row_part, "exp")
    row_max = lax.dynamic_slice_in_dim(row_all, lax.axis_index("exp") * row_count, row_count)
    request_ends = jnp.cumsum(lengths[0])
    position = jnp.arange(row_count, dtype=jnp.int32)
    request_of = jnp.sum((position[:, None] >= request_ends[None, :]).astype(jnp.int32), axis=1)
    member = request_of[:, None] == jnp.arange(lengths.shape[1], dtype=jnp.int32)[None, :]
    request_sq = jnp.sum(jnp.where(member, row_sq[:, None], jnp.float32(0.0)), axis=0)
    request_norm = jnp.sqrt(request_sq / (lengths[0].astype(jnp.float32) * D))
    request_max = jnp.max(jnp.where(member, row_max[:, None], jnp.float32(-jnp.inf)), axis=0)
    return (hidden_out, request_norm, request_max)


def solution(mesh):
    placed = (
        P(("req", "exp"), None),
        P(("req", "exp"), None),
        P(),
        P(None, ("req", "exp")),
        P(None, ("req", "exp")),
        P(("req", "exp"), None),
        P(),
        P(None, "exp"),
        P(("req", "exp"), None),
    )
    return jax.shard_map(
        per_device,
        mesh=mesh,
        in_specs=placed,
        out_specs=(P(("req", "exp"), None), P(("req", "exp")), P(("req", "exp"))),
        check_vma=False,
    )
```

profile of v0, /device:TPU:0, one launch (start us, length us, event | category | flops | bytes accessed | tf_op | source)
XLA Modules:
  0.0 321.0 jit_solution(3076345492475497243)
XLA Ops:
  7.2 0.8 copy.84
  8.3 0.2 reduce_window_sum.18
  8.7 2.4 gather_fusion
  11.2 12.2 %scatter_fusion = bf16[8,24,2048]{2,1,0:T(8,128)(2,1)S(1)} fusion(bf16[8,24,2048]{2,1,0:T(8,128)(2,1)S(1)} %broadcast_in_dim.46, s32[128]{0:T(128)S(1)} %get-tuple-element.7, bf16[128,2048]{1,0:T(8,128)(2,1)S(1)} %gather_fusion), kind=kCustom, calls=%fused_computation.3 | custom fusion | bytes 1573888 | tf_op jit(solution)/shard_map/scatter | solution.py:41
  23.5 0.4 copy.86
  23.9 0.8 copy.87
  24.7 1.2 broadcast_in_dim.47
  25.9 0.8 copy.93
  26.7 57.2 %all_to_all.10 = bf16[32,12,2048]{2,1,0:T(8,128)(2,1)S(1)} all-to-all(bf16[32,12,2048]{2,1,0:T(8,128)(2,1)S(1)} %bitcast.43), channel_id=1, replica_groups=mesh['req'=4,'exp'=8] {'req','exp'}, dimensions={0} | all-to-all | bytes 3145728 | tf_op jit(solution)/shard_map/all_to_all | solution.py:51
  83.9 1.3 reshape.169
  85.2 11.4 %fusion.15 = f32[384,2816]{1,0:T(8,128)} fusion(bf16[384,2048]{1,0:T(8,128)(2,1)} %reshape.169, bf16[2048,2816]{1,0:T(8,128)(2,1)} %param.12), kind=kOutput, calls=%fused_computation.48 | convolution fusion | flops 4429185024 | bytes 17432576 | tf_op jit(solution)/shard_map/dot_general | solution.py:14
  96.6 18.4 %fusion.4 = f32[384,2048]{1,0:T(8,128)S(1)} fusion(bf16[2816,2048]{1,0:T(8,128)(2,1)} %param.14, bf16[384,2048]{1,0:T(8,128)(2,1)} %reshape.169, bf16[2048,2816]{1,0:T(8,128)(2,1)} %param.13, f32[384,2816]{1,0:T(8,128)} %fusion.15), kind=kOutput, calls=%fused_computation.12 | convolution fusion | flops 8864858112 | bytes 32112640 | tf_op jit(solution)/shard_map/dot_general | solution.py:17
  115.0 2.2 reshape.170
  117.2 3.7 %all-to-all-start.1 = ((f32[32,12,2048]{2,1,0:T(8,128)}), f32[32,12,2048]{2,1,0:T(8,128)}, u32[]{:S(2)}, u32[]{:S(2)}) async-start(f32[32,12,2048]{2,1,0:T(8,128)} %reshape.170), calls=%async_computation.1 | async-start | bytes 8388608 | tf_op jit(solution)/shard_map/all_to_all | solution.py:57
  121.2 0.2 fusion.3
  121.4 1.3 gather_fusion.2
  122.9 93.9 %all-to-all-done.1 = f32[32,12,2048]{2,1,0:T(8,128)} async-done(((f32[32,12,2048]{2,1,0:T(8,128)}), f32[32,12,2048]{2,1,0:T(8,128)}, u32[]{:S(2)}, u32[]{:S(2)}) %all-to-all-start.1) | async-done | bytes 3145760 | tf_op jit(solution)/shard_map/all_to_all | solution.py:57
  216.8 4.6 %copy.90 = f32[4,2,4,12,2048]{4,1,3,2,0:T(2,128)S(1)} copy(f32[4,2,4,12,2048]{4,3,2,1,0:T(8,128)} %bitcast.8) | data formatting | bytes 6291456 | tf_op jit(solution)/shard_map/reshape | solution.py:60
  221.5 4.4 %reduce_sum.58 = f32[8,2,12,2048]{3,1,2,0:T(2,128)} reduce(f32[8,2,2,12,2048]{4,2,3,1,0:T(2,128)S(1)} %bitcast.41, f32[]{:T(128)} %constant.64.clone.1), dimensions={1}, to_apply=%region_3.4 | reduce | flops 393216 | bytes 4718596 | tf_op jit(solution)/shard_map/reduce_sum | solution.py:64
  225.9 2.3 copy.91
  228.2 0.9 copy.92
  229.1 1.9 gather_fusion.1
  231.0 0.6 reshape.174
  231.7 1.6 multiply_reduce_fusion
  233.2 0.2 fusion.5
  233.4 0.9 fusion.7
  234.3 0.2 reduce-window.8
  234.6 46.4 %all-gather.2.cloned.1.call-done = bf16[512,2048]{1,0:T(8,128)(2,1)} async-done(((bf16[64,2048]{1,0:T(8,128)(2,1)}), bf16[512,2048]{1,0:T(8,128)(2,1)}) %all-gather.2.cloned.1.call-update) | async-done | bytes 2097168 | tf_op jit(solution)/shard_map/all_gather | solution.py:75
  281.0 12.9 %convolution_reduce_fusion = f32[512]{0:T(512)S(1)} fusion(bf16[512,2048]{1,0:T(8,128)(2,1)} %all-gather.2.cloned.1.call-done, bf16[2048,4000]{0,1:T(8,128)(2,1)} %param.16), kind=kOutput, calls=%fused_computation.6 | convolution fusion | flops 8390655488 | bytes 18483200 | tf_op jit(solution)/shard_map/dot_general | solution.py:74
  294.0 18.9 %pmax.7 = f32[512]{0:T(512)S(1)} all-reduce(f32[512]{0:T(512)S(1)} %convolution_reduce_fusion), channel_id=1, replica_groups=mesh['req'=4,'exp'=8] {'exp'}, use_global_device_ids=true, to_apply=%region_10.11 | all-reduce | flops 512 | bytes 4096 | tf_op jit(solution)/shard_map/pmax | solution.py:81
  312.9 0.6 select_reduce_fusion.1
  313.6 0.5 fusion.11
  (34 shorter events, 1.4 us)
Async XLA Ops:
  7.2 114.0 %copy-start = (bf16[2048,8]{0,1:T(8,128)(2,1)S(1)}, bf16[2048,8]{0,1:T(8,128)(2,1)}, u32[]{:S(2)}) copy-start(bf16[2048,8]{0,1:T(8,128)(2,1)} %param.11) | copy-start | bytes 98308
  117.1 3.8 %copy-start.4 = (s32[64,2]{0,1:T(2,128)S(1)}, s32[64,2]{0,1:T(2,128)}, u32[]{:S(2)}) copy-start(s32[64,2]{0,1:T(2,128)} %param.10) | copy-start | bytes 1540
  117.1 4.0 %copy-start.2 = (bf16[64,2048]{1,0:T(8,128)(2,1)S(1)}, bf16[64,2048]{1,0:T(8,128)(2,1)}, u32[]{:S(2)}) copy-start(bf16[64,2048]{1,0:T(8,128)(2,1)} %param.9) | copy-start | bytes 786436
  117.2 99.7 %all-to-all-start.1 = ((f32[32,12,2048]{2,1,0:T(8,128)}), f32[32,12,2048]{2,1,0:T(8,128)}, u32[]{:S(2)}, u32[]{:S(2)}) async-start(f32[32,12,2048]{2,1,0:T(8,128)} %reshape.170), calls=%async_computation.1 | async-start | bytes 8388608 | tf_op jit(solution)/shard_map/all_to_all | solution.py:57
  120.9 160.2 %all-gather.2.cloned.1.call-start = ((), (), s32[]{:S(2)}) async-start(), calls=%async_computation.2 | async-start | bytes 2359296 | tf_op jit(solution)/shard_map/all_gather | solution.py:75
  231.0 2.4 copy-start.5
  231.0 3.3 %copy-start.6 = (s32[1,4]{1,0:T(1,128)S(1)}, s32[1,4]{1,0:T(1,128)}, u32[]{:S(2)}) copy-start(s32[1,4]{1,0:T(1,128)} %param.17) | copy-start | bytes 52
  233.4 60.5 %copy-start.3 = (bf16[64,2048]{1,0:T(8,128)(2,1)}, bf16[64,2048]{1,0:T(8,128)(2,1)S(1)}, u32[]{:S(2)}) copy-start(bf16[64,2048]{1,0:T(8,128)(2,1)S(1)} %get-tuple-element.6) | copy-start | bytes 786436
  281.0 33.1 %copy-start.1 = (bf16[2048,8]{0,1:T(8,128)(2,1)S(1)}, bf16[2048,8]{0,1:T(8,128)(2,1)}, u32[]{:S(2)}) copy-start(bf16[2048,8]{0,1:T(8,128)(2,1)} %param.11) | copy-start | bytes 98308
Sparse Core Ops, SparseCore 0:
  234.4 46.5 all-gather.1
where the time goes:
time: 321 us
  waiting for transfers between devices  140 us (44%)
  blocking collectives  76.1 us (24%)
  matrix products  42.8 us (13%)
  local copies, waits for them, and re-layouts  34.8 us (11%)
  between operations  14.3 us (4%)
  other arithmetic  8.88 us (3%)
  starting transfers between devices  3.74 us (1%)
    all_to_all x1, waiting for transfers between devices, per_device(): lax.all_to_all(partial_value, ('req', 'exp'), split_axis=0, concat_axis=0...  93.9 us
    all_to_all x1, blocking collectives, per_device(): lax.all_to_all(outgoing, ('req', 'exp'), split_axis=0, concat_axis=0, til...  57.2 us
    all_gather x1, waiting for transfers between devices, per_device(): lax.all_gather(normed, 'exp', axis=0, tiled=True)  46.4 us
    pmax x1, blocking collectives, per_device(): row_all = lax.pmax(row_part, 'exp')  18.9 us
    dot_general x1, matrix products, expert_apply(): return jnp.dot(hidden, w_down, preferred_element_type=jnp.float32)  18.4 us
    dot_general x1, matrix products, per_device(): jnp.dot(lax.all_gather(normed, 'exp', axis=0, tiled=True), head_weight, p...  12.9 us
    scatter x2, local copies, waits for them, and re-layouts, per_device(): dispatch = jnp.zeros((experts, capacity, model_width), jnp.bfloat16).at[c...  12.7 us
    dot_general x1, matrix products, expert_apply(): gate_act = jnp.dot(routed_rows, w_gate, preferred_element_type=jnp.float32)  11.4 us
  transfers between devices with their start and end apart: 2, of which 2 were waited for; matrix products, arithmetic and copies ran while one was open for 1% of the time, Pallas kernels for 0%

commit v1 on v0

v1 whole, which is shorter than its diff:
```python
import functools

import jax
import jax.numpy as jnp
from jax import lax
from jax.experimental import pallas as pl
from jax.experimental.pallas import tpu as pltpu
from jax.sharding import PartitionSpec as P

CAP = 24
META = 128
VMEM_LIMIT = 60 * 1024 * 1024

norm_eps = 1e-05
AXES = ("req", "exp")
F32 = jnp.float32
BF16 = jnp.bfloat16


def flip_pairs(n_req, n_exp, dim_of_core):
    pairs = []
    for r in range(n_req):
        for e in range(n_exp):
            flips = dim_of_core[r & 1]
            pr, pe = r, e
            for axis, bit in flips:
                if axis == "req":
                    pr ^= bit
                else:
                    pe ^= bit
            pairs.append((r * n_exp + e, pr * n_exp + pe))
    return pairs


def bits_below(n, first=1):
    out = []
    b = first
    while b < n:
        out.append(b)
        b *= 2
    return out


def prepare_kernel(tokens_ref, routes_ref, router_ref, out_ref):
    width = tokens_ref.shape[1]
    rows = tokens_ref.shape[0]
    t = tokens_ref[...]
    out_ref[:, :width] = t
    gating = 1.0 / (1.0 + jnp.exp(-jnp.dot(t, router_ref[...], preferred_element_type=F32)))
    routes = routes_ref[...]
    lane = lax.broadcasted_iota(jnp.int32, (rows, META), 1)
    expert = lax.broadcasted_iota(jnp.int32, gating.shape, 1)
    meta = jnp.zeros((rows, META), F32)
    for k in range(2):
        ids = routes[:, k : k + 1]
        chosen = jnp.sum(jnp.where(expert == ids, gating, 0.0), axis=1, keepdims=True)
        high = chosen.astype(BF16).astype(F32)
        mid = (chosen - high).astype(BF16).astype(F32)
        low = chosen - high - mid
        for j, piece in enumerate((ids.astype(F32), high, mid, low)):
            meta = jnp.where(lane == 4 * k + j, piece, meta)
    out_ref[:, width:] = meta.astype(BF16)


def prepare(tokens, routes, router):
    rows, width = tokens.shape
    return pl.pallas_call(
        prepare_kernel,
        out_shape=jax.ShapeDtypeStruct((rows, width + META), BF16),
        name="prepare",
    )(tokens, routes, router)


def expert_kernel(blocks, slots, expert_ref, *refs):
    block_refs = refs[:blocks]
    gate_ref, up_ref, down_ref = refs[blocks : blocks + 3]
    half = blocks // 2
    own_refs = refs[blocks + 3 : blocks + 3 + half]
    other_ref = refs[blocks + 3 + half]
    table, place, routed, scale, total, sems = refs[blocks + 4 + half :]
    rows = block_refs[0].shape[0]
    width = gate_ref.shape[0]
    count = blocks * rows
    step = pl.program_id(0)

    @pl.when(step == 0)
    def _():
        copies = [
            pltpu.make_async_copy(ref, table.at[pl.ds(i * rows, rows)], sems.at[i])
            for i, ref in enumerate(block_refs)
        ]
        for c in copies:
            c.start()
        for c in copies:
            c.wait()
        meta = table[:, width:].astype(F32)
        own = expert_ref[0].astype(F32)
        lane = lax.broadcasted_iota(jnp.int32, meta.shape, 1)
        first = meta[:, 0:1] == own
        second = meta[:, 4:5] == own
        member = jnp.logical_or(first, second)
        gate = jnp.where(
            first,
            meta[:, 1:2] + meta[:, 2:3] + meta[:, 3:4],
            meta[:, 5:6] + meta[:, 6:7] + meta[:, 7:8],
        )
        flags = jnp.where(jnp.logical_and(lane == 0, member), 1.0, 0.0).astype(BF16)
        before = lax.broadcasted_iota(jnp.int32, (count, count), 0) > lax.broadcasted_iota(
            jnp.int32, (count, count), 1
        )
        rank = jnp.dot(
            jnp.where(before, 1.0, 0.0).astype(BF16), flags, preferred_element_type=F32
        )[:, 0:1].astype(jnp.int32)
        slot = lax.broadcasted_iota(jnp.int32, (count, slots), 1)
        chosen = jnp.logical_and(slot == rank, member)
        place[...] = jnp.where(chosen, 1.0, 0.0).astype(BF16)
        scale[...] = jnp.transpose(
            jnp.broadcast_to(
                jnp.sum(jnp.where(chosen, gate, 0.0), axis=0, keepdims=True), (128, slots)
            )
        )
        routed[...] = lax.dot_general(
            place[...], table[:, :width], (((0,), (0,)), ((), ())), preferred_element_type=F32
        ).astype(BF16)

    x = routed[...]
    g = jnp.dot(x, gate_ref[...], preferred_element_type=F32)
    u = jnp.dot(x, up_ref[...], preferred_element_type=F32)
    hidden = (g / (1.0 + jnp.exp(-g)) * u).astype(BF16)
    y = jnp.dot(hidden, down_ref[...], preferred_element_type=F32)

    @pl.when(step == 0)
    def _():
        total[...] = y

    @pl.when(step > 0)
    def _():
        total[...] += y

    @pl.when(step == pl.num_programs(0) - 1)
    def _():
        weighted = (total[...] * scale[:, 0:1]).astype(BF16)
        for i, ref in enumerate(own_refs):
            ref[...] = jnp.dot(
                place[i * rows : (i + 1) * rows, :], weighted, preferred_element_type=F32
            ).astype(BF16)
        other_ref[...] = jnp.dot(
            place[half * rows :, :], weighted, preferred_element_type=F32
        ).astype(BF16)


def tile_of(size, want):
    for t in range(want, 0, -128):
        if size % t == 0:
            return t
    return size


def run_expert(expert, block_list, gate_weight, up_weight, down_weight, cap):
    blocks = len(block_list)
    rows = block_list[0].shape[0]
    width, hidden = gate_weight.shape
    half = blocks // 2
    slots = blocks * cap
    count = blocks * rows
    tile = tile_of(hidden, 256)
    whole = pl.BlockSpec(memory_space=pl.ANY)
    return pl.pallas_call(
        functools.partial(expert_kernel, blocks, slots),
        grid=(hidden // tile,),
        in_specs=[pl.BlockSpec(memory_space=pltpu.SMEM)]
        + [whole] * blocks
        + [
            pl.BlockSpec((width, tile), lambda i: (0, i)),
            pl.BlockSpec((width, tile), lambda i: (0, i)),
            pl.BlockSpec((tile, width), lambda i: (i, 0)),
        ],
        out_specs=[pl.BlockSpec((rows, width), lambda i: (0, 0))] * half
        + [pl.BlockSpec((half * rows, width), lambda i: (0, 0))],
        out_shape=[jax.ShapeDtypeStruct((rows, width), BF16)] * half
        + [jax.ShapeDtypeStruct((half * rows, width), BF16)],
        scratch_shapes=[
            pltpu.VMEM((count, width + META), BF16),
            pltpu.VMEM((count, slots), BF16),
            pltpu.VMEM((slots, width), BF16),
            pltpu.VMEM((slots, 128), F32),
            pltpu.VMEM((slots, width), F32),
            pltpu.SemaphoreType.DMA((blocks,)),
        ],
        compiler_params=pltpu.CompilerParams(
            vmem_limit_bytes=VMEM_LIMIT, dimension_semantics=("arbitrary",)
        ),
        cost_estimate=pl.CostEstimate(
            flops=6 * slots * width * hidden + 4 * slots * count * width,
            bytes_accessed=6 * width * hidden + 4 * count * width,
            transcendentals=slots * hidden,
        ),
        name="expert",
    )(expert, *block_list, gate_weight, up_weight, down_weight)


def finish_kernel(parts, tokens_ref, gain_ref, *refs):
    hidden_ref, normed_ref, square_ref = refs[parts:]
    total = refs[0][...].astype(F32)
    for ref in refs[1:parts]:
        total = total + ref[...].astype(F32)
    hidden = (tokens_ref[...].astype(F32) + total).astype(BF16)
    hidden_ref[...] = hidden
    wide = hidden.astype(F32)
    square = jnp.sum(wide * wide, axis=1, keepdims=True)
    normed_ref[...] = (
        wide * lax.rsqrt(square / wide.shape[1] + norm_eps) * gain_ref[...]
    ).astype(BF16)
    square_ref[...] = jnp.transpose(jnp.broadcast_to(square, (square.shape[0], 128)))[0:8, :]


def finish(tokens, gain, parts):
    rows, width = tokens.shape
    return pl.pallas_call(
        functools.partial(finish_kernel, len(parts)),
        out_shape=[
            jax.ShapeDtypeStruct((rows, width), BF16),
            jax.ShapeDtypeStruct((rows, width), BF16),
            jax.ShapeDtypeStruct((8, rows), F32),
        ],
        name="finish",
    )(tokens, gain, *parts)


def peak_kernel(blocks, words, places_ref, *refs):
    block_refs = refs[:blocks]
    head_ref, out_ref, table, best, sems = refs[blocks:]
    rows = block_refs[0].shape[0]
    step = pl.program_id(0)
    tile = head_ref.shape[1]

    @pl.when(step == 0)
    def _():
        copies = [
            pltpu.make_async_copy(ref, table.at[pl.ds(i * rows, rows)], sems.at[i])
            for i, ref in enumerate(block_refs)
        ]
        for c in copies:
            c.start()
        for c in copies:
            c.wait()
        best[...] = jnp.full(best.shape, -jnp.inf, F32)

    logits = jnp.dot(table[...], head_ref[...], preferred_element_type=F32)
    word = lax.broadcasted_iota(jnp.int32, logits.shape, 1) + step * tile
    best[...] = jnp.maximum(best[...], jnp.where(word < words, logits, -jnp.inf))

    @pl.when(step == pl.num_programs(0) - 1)
    def _():
        peak = jnp.max(best[...], axis=1, keepdims=True)
        line = jnp.transpose(jnp.broadcast_to(peak, (peak.shape[0], 128)))[0:1, :]
        target = lax.broadcasted_iota(jnp.int32, out_ref.shape, 0)
        out = jnp.full(out_ref.shape, -jnp.inf, F32)
        for i in range(blocks):
            out = jnp.where(target == places_ref[i], line[:, i * rows : (i + 1) * rows], out)
        out_ref[...] = out


def peaks(places, block_list, head_weight, n_exp):
    blocks = len(block_list)
    rows, width = block_list[0].shape
    words = head_weight.shape[1]
    tile = 512
    steps = pl.cdiv(words, tile)
    return pl.pallas_call(
        functools.partial(peak_kernel, blocks, words),
        grid=(steps,),
        in_specs=[pl.BlockSpec(memory_space=pltpu.SMEM)]
        + [pl.BlockSpec(memory_space=pl.ANY)] * blocks
        + [pl.BlockSpec((width, tile), lambda i: (0, i))],
        out_specs=pl.BlockSpec((n_exp, rows), lambda i: (0, 0)),
        out_shape=jax.ShapeDtypeStruct((n_exp, rows), F32),
        scratch_shapes=[
            pltpu.VMEM((blocks * rows, width), BF16),
            pltpu.VMEM((blocks * rows, tile), F32),
            pltpu.SemaphoreType.DMA((blocks,)),
        ],
        compiler_params=pltpu.CompilerParams(
            vmem_limit_bytes=VMEM_LIMIT, dimension_semantics=("arbitrary",)
        ),
        cost_estimate=pl.CostEstimate(
            flops=2 * blocks * rows * width * words,
            bytes_accessed=2 * width * words + 2 * blocks * rows * width,
            transcendentals=0,
        ),
        name="peaks",
    )(places, *block_list, head_weight)


def add(a, b):
    return (a.astype(F32) + b.astype(F32)).astype(BF16)


def per_device(
    n_req,
    n_exp,
    tokens,
    routes,
    router,
    gate_weight,
    up_weight,
    down_weight,
    norm_gain,
    head_weight,
    lengths,
):
    row_count, width = tokens.shape
    experts = router.shape[1]
    half_exp = n_exp // 2
    group_size = n_req * n_exp // (2 * experts)
    r = lax.axis_index("req")
    e = lax.axis_index("exp")
    expert = ((r * half_exp + e % half_exp) // group_size).astype(jnp.int32).reshape(1)

    def send(x, flips0, flips1=None):
        pairs = flip_pairs(n_req, n_exp, (flips0, flips0 if flips1 is None else flips1))
        return lax.ppermute(x, AXES, pairs)

    core = [("req", 1)]
    dims = [("req", b) for b in bits_below(n_req, 2)] + [("exp", b) for b in bits_below(half_exp)]
    extra, dims = dims[3:], dims[:3]
    turned = dims[1:] + dims[:1]

    def hop(x, *js):
        return send(x, [dims[j] for j in js], [turned[j] for j in js])

    block = prepare(tokens, routes, router)
    for d in extra:
        block = jnp.concatenate([block, send(block, [d])], axis=0)
    near = [block]
    near += [hop(b, 0) for b in near]
    near += [hop(b, 1) for b in near]
    far = [hop(b, 2) for b in near]
    near += [send(b, core) for b in near]
    far += [send(b, core) for b in far]
    cap = CAP * block.shape[0] // row_count
    weights = (gate_weight, up_weight, down_weight)

    *near_out, near_other = run_expert(expert, near, *weights, cap)
    *far_out, far_other = run_expert(expert, far, *weights, cap)
    rows = block.shape[0]

    def with_core(own, other):
        got = send(other, core)
        return [add(b, got[i * rows : (i + 1) * rows]) for i, b in enumerate(own)]

    near_sum = with_core(near_out, near_other)
    n3 = hop(near_sum[3], 1)
    n2 = hop(near_sum[2], 1)
    n1 = hop(add(near_sum[1], n3), 0)
    far_sum = with_core(far_out, far_other)
    f3 = hop(far_sum[3], 1)
    f2 = hop(far_sum[2], 1)
    f1 = hop(add(far_sum[1], f3), 0, 2)
    f0 = hop(add(far_sum[0], f2), 2)
    parts = [near_sum[0], n2, n1, f0, f1]
    for d in reversed(extra):
        merged = sum(p.astype(F32) for p in parts).astype(BF16)
        size = merged.shape[0] // 2
        parts = [merged[:size], send(merged[size:], [d])]
    hidden_out, normed, square = finish(tokens, norm_gain.reshape(1, width), parts)

    near_dims = [("exp", b) for b in bits_below(half_exp)]
    near_turn = near_dims[1:] + near_dims[:1]
    across = [("exp", half_exp)]

    def spread(first):
        held, moved = [first], [(0, 0)]
        for a, b in zip(near_dims, near_turn):
            held += [send(x, [a], [b]) for x in held]
            moved += [(p ^ a[1], q ^ b[1]) for p, q in moved]
        return held, moved

    far_first = send(normed, across)
    near_blocks, moved = spread(normed)
    far_blocks, _ = spread(far_first)
    is_second = r % 2 == 1
    places = jnp.stack([jnp.where(is_second, e ^ q, e ^ p) for p, q in moved]).astype(jnp.int32)
    near_peak = peaks(places, near_blocks, head_weight, n_exp)
    far_peak = peaks(places ^ half_exp, far_blocks, head_weight, n_exp)
    got = lax.all_to_all(jnp.maximum(near_peak, far_peak), "exp", 0, 0, tiled=True)
    row_max = jnp.max(got, axis=0)

    request_ends = jnp.cumsum(lengths[0])
    position = jnp.arange(row_count, dtype=jnp.int32)
    request_of = jnp.sum((position[:, None] >= request_ends[None, :]).astype(jnp.int32), axis=1)
    member = request_of[:, None] == jnp.arange(lengths.shape[1], dtype=jnp.int32)[None, :]
    request_sq = jnp.sum(jnp.where(member, square[0][:, None], F32(0.0)), axis=0)
    request_norm = jnp.sqrt(request_sq / (lengths[0].astype(F32) * width))
    request_max = jnp.max(jnp.where(member, row_max[:, None], F32(-jnp.inf)), axis=0)
    return (hidden_out, request_norm, request_max)


def solution(mesh):
    placed = (
        P(AXES, None),
        P(AXES, None),
        P(),
        P(None, AXES),
        P(None, AXES),
        P(AXES, None),
        P(),
        P(None, "exp"),
        P(AXES, None),
    )
    return jax.shard_map(
        functools.partial(per_device, mesh.shape["req"], mesh.shape["exp"]),
        mesh=mesh,
        in_specs=placed,
        out_specs=(P(AXES, None), P(AXES), P(AXES)),
        check_vma=False,
    )
```

time: 321 us -> 197 us (0.61)
  waiting for transfers between devices: 140 us -> 44.7 us
  Pallas kernels: 0 us -> 77.7 us
  blocking collectives: 76.1 us -> 0 us
  matrix products: 42.8 us -> 0 us
  starting transfers between devices: 3.74 us -> 37.4 us
  between operations: 14.3 us -> 0.93 us
  local copies, waits for them, and re-layouts: 34.8 us -> 28.4 us
    all_to_all x1, waiting for transfers between devices: 93.9 us -> 5.78 us  [per_device(): lax.all_to_all(jnp.maximum(near_peak, far_peak), 'exp', 0, 0, tiled=True)]
    pallas_call x0 -> x6, Pallas kernels: none -> 77.7 us  [the longest x2 47.3 us: run_expert(): pl.pallas_call(functools.partial(expert_kernel, blocks, slots), grid=(hid...]
    all_to_all x1 -> x0, blocking collectives: 57.2 us -> none  [per_device(): lax.all_to_all(outgoing, ('req', 'exp'), split_axis=0, concat_axis=0, til...]
    all_gather x1 -> x0, waiting for transfers between devices: 46.4 us -> none  [per_device(): lax.all_gather(normed, 'exp', axis=0, tiled=True)]
    dot_general x4 -> x0, matrix products: 42.8 us -> none  [the longest x1 18.4 us: expert_apply(): return jnp.dot(hidden, w_down, preferred_element_type=jnp.float32)]
    ppermute x0 -> x31, waiting for transfers between devices: none -> 38.9 us  [send(): return lax.ppermute(x, AXES, pairs)]
    ppermute x0 -> x31, starting transfers between devices: none -> 31.4 us  [send(): return lax.ppermute(x, AXES, pairs)]
    unnamed x15 -> x61, local copies, waits for them, and re-layouts: 0.81 us -> 27.7 us
  transfers between devices with their start and end apart: 2 -> 32, of which waited for: 2 -> 14; matrix products, arithmetic and copies ran while one was open for 1% -> 13% of each run, Pallas kernels for 0% -> 31%
where the time goes in v1:
time: 197 us; the launch traced here: 196 us
  Pallas kernels  77.7 us (39%)
  waiting for transfers between devices  44.7 us (23%)
  starting transfers between devices  37.4 us (19%)
  local copies, waits for them, and re-layouts  28.4 us (14%)
  other arithmetic  6.86 us (3%)
    pallas_call x2, Pallas kernels, run_expert(): pl.pallas_call(functools.partial(expert_kernel, blocks, slots), grid=(hid...  47.3 us
    ppermute x31, waiting for transfers between devices, send(): return lax.ppermute(x, AXES, pairs)  38.9 us
    ppermute x31, starting transfers between devices, send(): return lax.ppermute(x, AXES, pairs)  31.4 us
    unnamed x61, local copies, waits for them, and re-layouts  27.7 us
    pallas_call x2, Pallas kernels, peaks(): pl.pallas_call(functools.partial(peak_kernel, blocks, words), grid=(steps...  25.8 us
    all_to_all x1, starting transfers between devices, per_device(): lax.all_to_all(jnp.maximum(near_peak, far_peak), 'exp', 0, 0, tiled=True)  6.01 us
    all_to_all x1, waiting for transfers between devices, per_device(): lax.all_to_all(jnp.maximum(near_peak, far_peak), 'exp', 0, 0, tiled=True)  5.78 us
  transfers between devices with their start and end apart: 32, of which 14 were waited for; matrix products, arithmetic and copies ran while one was open for 13% of the time, Pallas kernels for 31%

profile of v1, /device:TPU:0, one launch (start us, length us, event | category | flops | bytes accessed | tf_op | source)
XLA Modules:
  0.0 196.0 jit_solution(12858788347042314569)
XLA Ops:
  0.6 1.4 copy.21.routes_ref
  2.0 1.8 copy.22.router_ref
  3.8 2.2 %prepare.1.refs_0_ = bf16[64,2176]{1,0:T(8,128)(2,1)} custom-call(bf16[64,2048]{1,0:T(8,128)(2,1)} %tokens_ref.3, s32[64,2]{1,0:T(8,128)} %copy.21.routes_ref, bf16[2048,8]{1,0:T(8,128)(2,1)} %copy.22.router_ref), custom_call_target="tpu_custom_call" | custom-call | tf_op jit(solution)/shard_map/prepare/pallas_call | solution.py:67
  6.0 2.9 %collective-permute-start = (bf16[64,2176]{1,0:T(8,128)(2,1)}, bf16[64,2176]{1,0:T(8,128)(2,1)S(1)}, u32[]{:S(2)}, u32[]{:S(2)}) collective-permute-start(bf16[64,2176]{1,0:T(8,128)(2,1)} %prepare.1.refs_0_), channel_id=1, source_target_pairs={{0,16},{1,17},{2,18},{3,19},{4,20},{5,21},{6,22},{7,23},{8,9},{9,8... | collective-permute-start | bytes 835592 | tf_op jit(solution)/shard_map/ppermute | solution.py:322
  8.9 1.5 collective-permute-start.1
  10.4 3.2 %collective-permute-done.refs_1_ = bf16[64,2176]{1,0:T(8,128)(2,1)S(1)} collective-permute-done((bf16[64,2176]{1,0:T(8,128)(2,1)}, bf16[64,2176]{1,0:T(8,128)(2,1)S(1)}, u32[]{:S(2)}, u32[]{:S(2)}) %collective-permute-start) | collective-permute-done | bytes 278560 | tf_op jit(solution)/shard_map/ppermute | solution.py:322
  13.6 2.1 %collective-permute-start.2 = (bf16[64,2176]{1,0:T(8,128)(2,1)S(1)}, bf16[64,2176]{1,0:T(8,128)(2,1)S(1)}, u32[]{:S(2)}, u32[]{:S(2)}) collective-permute-start(bf16[64,2176]{1,0:T(8,128)(2,1)S(1)} %collective-permute-done.refs_1_), channel_id=1, source_target_pairs={{0,1},{1,0},{2,3},{3,2},{4,5},{5,4},{6,7},{7,6},{8,10},{9,11},{10,... | collective-permute-start | bytes 835592 | tf_op jit(solution)/shard_map/ppermute | solution.py:322
  15.7 1.6 collective-permute-start.11
  17.7 1.6 collective-permute-start.13
  20.2 2.1 %collective-permute-start.14 = (bf16[64,2176]{1,0:T(8,128)(2,1)S(1)}, bf16[64,2176]{1,0:T(8,128)(2,1)S(1)}, u32[]{:S(2)}, u32[]{:S(2)}) collective-permute-start(bf16[64,2176]{1,0:T(8,128)(2,1)S(1)} %collective-permute-done.2.refs_3_), channel_id=1, source_target_pairs={{0,2},{1,3},{2,0},{3,1},{4,6},{5,7},{6,4},{7,5},{8,24},{9,25},{10,... | collective-permute-start | bytes 835592 | tf_op jit(solution)/shard_map/ppermute | solution.py:322
  22.8 2.7 %collective-permute-done.12.refs_1_ = bf16[64,2176]{1,0:T(8,128)(2,1)S(1)} collective-permute-done((bf16[64,2176]{1,0:T(8,128)(2,1)S(1)}, bf16[64,2176]{1,0:T(8,128)(2,1)S(1)}, u32[]{:S(2)}, u32[]{:S(2)}) %collective-permute-start.12) | collective-permute-done | bytes 278560 | tf_op jit(solution)/shard_map/ppermute | solution.py:322
  25.4 3.0 %collective-permute-done.13.refs_2_ = bf16[64,2176]{1,0:T(8,128)(2,1)S(1)} collective-permute-done((bf16[64,2176]{1,0:T(8,128)(2,1)S(1)}, bf16[64,2176]{1,0:T(8,128)(2,1)S(1)}, u32[]{:S(2)}, u32[]{:S(2)}) %collective-permute-start.13) | collective-permute-done | bytes 278560 | tf_op jit(solution)/shard_map/ppermute | solution.py:322
  28.4 3.0 %collective-permute-done.14.refs_3_ = bf16[64,2176]{1,0:T(8,128)(2,1)S(1)} collective-permute-done((bf16[64,2176]{1,0:T(8,128)(2,1)S(1)}, bf16[64,2176]{1,0:T(8,128)(2,1)S(1)}, u32[]{:S(2)}, u32[]{:S(2)}) %collective-permute-start.14) | collective-permute-done | bytes 278560 | tf_op jit(solution)/shard_map/ppermute | solution.py:322
  34.1 23.7 %expert.3 = (bf16[64,2048]{1,0:T(8,128)(2,1)}, bf16[64,2048]{1,0:T(8,128)(2,1)}, bf16[64,2048]{1,0:T(8,128)(2,1)}, bf16[64,2048]{1,0:T(8,128)(2,1)}, bf16[256,2048]{1,0:T(8,128)(2,1)}) custom-call(s32[1]{0:T(128)} %bitcast.1.expert_ref, bf16[64,2176]{1,0:T(8,128)(2,1)} %copy-done.3, bf16[64,2176]{1,0:T(8,128)(2,1)} %copy-done.4, bf16[64,2176]{1,0:T(8,128)(2,1)} %copy-done.5, ...), custom_call_target="tpu_custom_call" | custom-call | flops 7449083904 | bytes 38797312 | tf_op jit(solution)/shard_map/expert/pallas_call | solution.py:168
  58.7 23.6 %expert.2 = (bf16[64,2048]{1,0:T(8,128)(2,1)}, bf16[64,2048]{1,0:T(8,128)(2,1)}, bf16[64,2048]{1,0:T(8,128)(2,1)}, bf16[64,2048]{1,0:T(8,128)(2,1)}, bf16[256,2048]{1,0:T(8,128)(2,1)}) custom-call(s32[1]{0:T(128)} %bitcast.1.expert_ref, bf16[64,2176]{1,0:T(8,128)(2,1)} %prepare.1.refs_0_, bf16[64,2176]{1,0:T(8,128)(2,1)} %copy-done, ...), custom_call_target="tpu_custom_call" | custom-call | flops 7449083904 | bytes 38797312 | tf_op jit(solution)/shard_map/expert/pallas_call | solution.py:168
  84.0 1.3 collective-permute-done.7
  87.5 1.9 collective-permute-done.22
  90.7 2.1 %collective-permute-done.9 = bf16[64,2048]{1,0:T(8,128)(2,1)S(1)} collective-permute-done((bf16[64,2048]{1,0:T(8,128)(2,1)S(1)}, bf16[64,2048]{1,0:T(8,128)(2,1)S(1)}, u32[]{:S(2)}, u32[]{:S(2)}) %collective-permute-start.9) | collective-permute-done | bytes 262176 | tf_op jit(solution)/shard_map/ppermute | solution.py:322
  92.8 2.1 %add_convert_fusion.6 = (bf16[64,2048]{1,0:T(8,128)(2,1)S(1)}, bf16[64,2048]{1,0:T(8,128)(2,1)S(1)}, bf16[64,2048]{1,0:T(8,128)(2,1)}) fusion(bf16[64,2048]{1,0:T(8,128)(2,1)S(1)} %collective-permute-done.9, bf16[64,2048]{1,0:T(8,128)(2,1)} %get-tuple-element.19, bf16[256,2048]{1,0:T(8,128)(2,1)S(1)} %collective-permute-done.7, ...), kind=kLoop, calls=%fused_computation.6 | loop fusion | flops 2097152 | bytes 2621440 | tf_op jit(solution)/shard_map/convert_element_type | solution.py:296
  96.0 2.4 %collective-permute-start.10 = (bf16[64,2048]{1,0:T(8,128)(2,1)S(1)}, bf16[64,2048]{1,0:T(8,128)(2,1)S(1)}, u32[]{:S(2)}, u32[]{:S(2)}) collective-permute-start(bf16[64,2048]{1,0:T(8,128)(2,1)S(1)} %get-tuple-element.35), channel_id=1, source_target_pairs={{0,16},{1,17},{2,18},{3,19},{4,20},{5,21},{6,22},{7,23},{8,9},{9,8... | collective-permute-start | bytes 786440 | tf_op jit(solution)/shard_map/ppermute | solution.py:322
  100.2 5.6 %collective-permute-done.8.refs_1_ = bf16[64,2048]{1,0:T(8,128)(2,1)S(1)} collective-permute-done((bf16[64,2048]{1,0:T(8,128)(2,1)S(1)}, bf16[64,2048]{1,0:T(8,128)(2,1)S(1)}, u32[]{:S(2)}, u32[]{:S(2)}) %collective-permute-start.8) | collective-permute-done | bytes 262176 | tf_op jit(solution)/shard_map/ppermute | solution.py:322
  105.8 2.6 %collective-permute-done.10.refs_2_ = bf16[64,2048]{1,0:T(8,128)(2,1)S(1)} collective-permute-done((bf16[64,2048]{1,0:T(8,128)(2,1)S(1)}, bf16[64,2048]{1,0:T(8,128)(2,1)S(1)}, u32[]{:S(2)}, u32[]{:S(2)}) %collective-permute-start.10) | collective-permute-done | bytes 262176 | tf_op jit(solution)/shard_map/ppermute | solution.py:322
  109.3 2.4 %finish.1 = (bf16[64,2048]{1,0:T(8,128)(2,1)}, bf16[64,2048]{1,0:T(8,128)(2,1)}, f32[8,64]{1,0:T(8,128)}) custom-call(bf16[64,2048]{1,0:T(8,128)(2,1)} %tokens_ref.3, f32[1,2048]{1,0:T(1,128)} %bitcast.17, bf16[64,2048]{1,0:T(8,128)(2,1)} %get-tuple-element.37.refs_0_, bf16[64,2048]{1,0:T(8,128)(2,1)} %copy-done.23, bf16[64,2048]{1,0:T(8,128)(2,1)} %copy-done.24, ...), custom_call_target="tpu_custom_call" | custom-call | tf_op jit(solution)/shard_map/finish/pallas_call | solution.py:219
  111.7 2.6 %collective-permute-start.27 = (bf16[64,2048]{1,0:T(8,128)(2,1)}, bf16[64,2048]{1,0:T(8,128)(2,1)S(1)}, u32[]{:S(2)}, u32[]{:S(2)}) collective-permute-start(bf16[64,2048]{1,0:T(8,128)(2,1)} %get-tuple-element.28.refs_0_), channel_id=1, source_target_pairs={{0,4},{1,5},{2,6},{3,7},{4,0},{5,1},{6,2},{7,3},{8,12},{9,13},{10,... | collective-permute-start | bytes 786440 | tf_op jit(solution)/shard_map/ppermute | solution.py:322
  114.7 11.7 %collective-permute-done.27.refs_0_ = bf16[64,2048]{1,0:T(8,128)(2,1)S(1)} collective-permute-done((bf16[64,2048]{1,0:T(8,128)(2,1)}, bf16[64,2048]{1,0:T(8,128)(2,1)S(1)}, u32[]{:S(2)}, u32[]{:S(2)}) %collective-permute-start.27) | collective-permute-done | bytes 262176 | tf_op jit(solution)/shard_map/ppermute | solution.py:322
  126.4 1.4 collective-permute-start.28
  129.9 20.7 %copy.23.refs_4_ = bf16[2048,4000]{1,0:T(8,128)(2,1)} copy(bf16[2048,4000]{0,1:T(8,128)(2,1)} %param.16) | data formatting | bytes 32768000 | tf_op args[7]
  154.4 12.9 %peaks.2 = f32[8,64]{1,0:T(8,128)} custom-call(s32[4]{0:T(128)} %get-tuple-element.32.places_ref, bf16[64,2048]{1,0:T(8,128)(2,1)} %get-tuple-element.28.refs_0_, bf16[64,2048]{1,0:T(8,128)(2,1)} %copy-done.14, bf16[64,2048]{1,0:T(8,128)(2,1)} %copy-done.15, bf16[64,2048]{1,0:T(8,128)(2,1)} %copy-done.16, bf16[2048,4000]{1,0:T(8,128)(2,1)} %copy.23.refs_4_), custom_call_target="tpu_custom_call" | custom-call | flops 4194304000 | bytes 17432576 | tf_op jit(solution)/shard_map/peaks/pallas_call | solution.py:270
  168.2 12.9 %peaks.3 = f32[8,64]{1,0:T(8,128)} custom-call(s32[4]{0:T(128)} %get-tuple-element.31.places_ref, bf16[64,2048]{1,0:T(8,128)(2,1)} %copy-done.12, bf16[64,2048]{1,0:T(8,128)(2,1)} %copy-done.13, bf16[64,2048]{1,0:T(8,128)(2,1)} %copy-done.17, bf16[64,2048]{1,0:T(8,128)(2,1)} %copy-done.18, bf16[2048,4000]{1,0:T(8,128)(2,1)} %copy.23.refs_4_), custom_call_target="tpu_custom_call" | custom-call | flops 4194304000 | bytes 17432576 | tf_op jit(solution)/shard_map/peaks/pallas_call | solution.py:270
  181.1 1.3 max.3
  182.4 6.0 %all-to-all-start = ((f32[8,1,64]{2,1,0:T(1,128)}), f32[8,1,64]{2,1,0:T(1,128)S(1)}, u32[]{:S(2)}, u32[]{:S(2)}) async-start(f32[8,1,64]{2,1,0:T(1,128)} %bitcast.11), calls=%async_computation | async-start | bytes 8192 | tf_op jit(solution)/shard_map/all_to_all | solution.py:386
  189.1 5.8 %all-to-all-done = f32[8,1,64]{2,1,0:T(1,128)S(1)} async-done(((f32[8,1,64]{2,1,0:T(1,128)}), f32[8,1,64]{2,1,0:T(1,128)S(1)}, u32[]{:S(2)}, u32[]{:S(2)}) %all-to-all-start) | async-done | bytes 2080 | tf_op jit(solution)/shard_map/all_to_all | solution.py:386
  (112 shorter events, 23.1 us)
Async XLA Ops:
  6.0 7.7 %collective-permute-start = (bf16[64,2176]{1,0:T(8,128)(2,1)}, bf16[64,2176]{1,0:T(8,128)(2,1)S(1)}, u32[]{:S(2)}, u32[]{:S(2)}) collective-permute-start(bf16[64,2176]{1,0:T(8,128)(2,1)} %prepare.1.refs_0_), channel_id=1, source_target_pairs={{0,16},{1,17},{2,18},{3,19},{4,20},{5,21},{6,22},{7,23},{8,9},{9,8... | collective-permute-start | bytes 835592 | tf_op jit(solution)/shard_map/ppermute | solution.py:322
  8.9 8.8 %collective-permute-start.1 = (bf16[64,2176]{1,0:T(8,128)(2,1)}, bf16[64,2176]{1,0:T(8,128)(2,1)S(1)}, u32[]{:S(2)}, u32[]{:S(2)}) collective-permute-start(bf16[64,2176]{1,0:T(8,128)(2,1)} %prepare.1.refs_0_), channel_id=1, source_target_pairs={{0,1},{1,0},{2,3},{3,2},{4,5},{5,4},{6,7},{7,6},{8,10},{9,11},{10,... | collective-permute-start | bytes 835592 | tf_op jit(solution)/shard_map/ppermute | solution.py:322
  13.6 6.6 %collective-permute-start.2 = (bf16[64,2176]{1,0:T(8,128)(2,1)S(1)}, bf16[64,2176]{1,0:T(8,128)(2,1)S(1)}, u32[]{:S(2)}, u32[]{:S(2)}) collective-permute-start(bf16[64,2176]{1,0:T(8,128)(2,1)S(1)} %collective-permute-done.refs_1_), channel_id=1, source_target_pairs={{0,1},{1,0},{2,3},{3,2},{4,5},{5,4},{6,7},{7,6},{8,10},{9,11},{10,... | collective-permute-start | bytes 835592 | tf_op jit(solution)/shard_map/ppermute | solution.py:322
  15.7 6.8 %collective-permute-start.11 = (bf16[64,2176]{1,0:T(8,128)(2,1)}, bf16[64,2176]{1,0:T(8,128)(2,1)S(1)}, u32[]{:S(2)}, u32[]{:S(2)}) collective-permute-start(bf16[64,2176]{1,0:T(8,128)(2,1)} %prepare.1.refs_0_), channel_id=1, source_target_pairs={{0,2},{1,3},{2,0},{3,1},{4,6},{5,7},{6,4},{7,5},{8,24},{9,25},{10,... | collective-permute-start | bytes 835592 | tf_op jit(solution)/shard_map/ppermute | solution.py:322
  17.3 8.2 %collective-permute-start.12 = (bf16[64,2176]{1,0:T(8,128)(2,1)S(1)}, bf16[64,2176]{1,0:T(8,128)(2,1)S(1)}, u32[]{:S(2)}, u32[]{:S(2)}) collective-permute-start(bf16[64,2176]{1,0:T(8,128)(2,1)S(1)} %collective-permute-done.refs_1_), channel_id=1, source_target_pairs={{0,2},{1,3},{2,0},{3,1},{4,6},{5,7},{6,4},{7,5},{8,24},{9,25},{10,... | collective-permute-start | bytes 835592 | tf_op jit(solution)/shard_map/ppermute | solution.py:322
  17.7 10.7 %collective-permute-start.13 = (bf16[64,2176]{1,0:T(8,128)(2,1)S(1)}, bf16[64,2176]{1,0:T(8,128)(2,1)S(1)}, u32[]{:S(2)}, u32[]{:S(2)}) collective-permute-start(bf16[64,2176]{1,0:T(8,128)(2,1)S(1)} %collective-permute-done.1.refs_2_), channel_id=1, source_target_pairs={{0,2},{1,3},{2,0},{3,1},{4,6},{5,7},{6,4},{7,5},{8,24},{9,25},{10,... | collective-permute-start | bytes 835592 | tf_op jit(solution)/shard_map/ppermute | solution.py:322
  20.2 11.2 %collective-permute-start.14 = (bf16[64,2176]{1,0:T(8,128)(2,1)S(1)}, bf16[64,2176]{1,0:T(8,128)(2,1)S(1)}, u32[]{:S(2)}, u32[]{:S(2)}) collective-permute-start(bf16[64,2176]{1,0:T(8,128)(2,1)S(1)} %collective-permute-done.2.refs_3_), channel_id=1, source_target_pairs={{0,2},{1,3},{2,0},{3,1},{4,6},{5,7},{6,4},{7,5},{8,24},{9,25},{10,... | collective-permute-start | bytes 835592 | tf_op jit(solution)/shard_map/ppermute | solution.py:322
  22.5 9.5 %collective-permute-start.15 = (bf16[64,2176]{1,0:T(8,128)(2,1)S(1)}, bf16[64,2176]{1,0:T(8,128)(2,1)S(1)}, u32[]{:S(2)}, u32[]{:S(2)}) collective-permute-start(bf16[64,2176]{1,0:T(8,128)(2,1)S(1)} %collective-permute-done.11.refs_0_), channel_id=1, source_target_pairs={{0,8},{1,9},{2,10},{3,11},{4,12},{5,13},{6,14},{7,15},{8,0},{9,1},... | collective-permute-start | bytes 835592 | tf_op jit(solution)/shard_map/ppermute | solution.py:322
  25.4 6.6 %collective-permute-start.16 = (bf16[64,2176]{1,0:T(8,128)(2,1)S(1)}, bf16[64,2176]{1,0:T(8,128)(2,1)S(1)}, u32[]{:S(2)}, u32[]{:S(2)}) collective-permute-start(bf16[64,2176]{1,0:T(8,128)(2,1)S(1)} %collective-permute-done.12.refs_1_), channel_id=1, source_target_pairs={{0,8},{1,9},{2,10},{3,11},{4,12},{5,13},{6,14},{7,15},{8,0},{9,1},... | collective-permute-start | bytes 835592 | tf_op jit(solution)/shard_map/ppermute | solution.py:322
  28.4 4.0 %collective-permute-start.17 = (bf16[64,2176]{1,0:T(8,128)(2,1)S(1)}, bf16[64,2176]{1,0:T(8,128)(2,1)S(1)}, u32[]{:S(2)}, u32[]{:S(2)}) collective-permute-start(bf16[64,2176]{1,0:T(8,128)(2,1)S(1)} %collective-permute-done.13.refs_2_), channel_id=1, source_target_pairs={{0,8},{1,9},{2,10},{3,11},{4,12},{5,13},{6,14},{7,15},{8,0},{9,1},... | collective-permute-start | bytes 835592 | tf_op jit(solution)/shard_map/ppermute | solution.py:322
  31.4 1.9 collective-permute-start.18
  31.4 26.6 %collective-permute-start.3 = (bf16[64,2176]{1,0:T(8,128)(2,1)}, bf16[64,2176]{1,0:T(8,128)(2,1)S(1)}, u32[]{:S(2)}, u32[]{:S(2)}) collective-permute-start(bf16[64,2176]{1,0:T(8,128)(2,1)} %prepare.1.refs_0_), channel_id=1, source_target_pairs={{0,8},{1,9},{2,10},{3,11},{4,12},{5,13},{6,14},{7,15},{8,0},{9,1},... | collective-permute-start | bytes 835592 | tf_op jit(solution)/shard_map/ppermute | solution.py:322
  31.9 26.1 %collective-permute-start.4 = (bf16[64,2176]{1,0:T(8,128)(2,1)S(1)}, bf16[64,2176]{1,0:T(8,128)(2,1)}, u32[]{:S(2)}, u32[]{:S(2)}) collective-permute-start(bf16[64,2176]{1,0:T(8,128)(2,1)S(1)} %collective-permute-done.refs_1_), channel_id=1, source_target_pairs={{0,8},{1,9},{2,10},{3,11},{4,12},{5,13},{6,14},{7,15},{8,0},{9,1},... | collective-permute-start | bytes 835592 | tf_op jit(solution)/shard_map/ppermute | solution.py:322
  32.0 26.0 %collective-permute-start.5 = (bf16[64,2176]{1,0:T(8,128)(2,1)S(1)}, bf16[64,2176]{1,0:T(8,128)(2,1)}, u32[]{:S(2)}, u32[]{:S(2)}) collective-permute-start(bf16[64,2176]{1,0:T(8,128)(2,1)S(1)} %collective-permute-done.1.refs_2_), channel_id=1, source_target_pairs={{0,8},{1,9},{2,10},{3,11},{4,12},{5,13},{6,14},{7,15},{8,0},{9,1},... | collective-permute-start | bytes 835592 | tf_op jit(solution)/shard_map/ppermute | solution.py:322
  32.5 25.6 %collective-permute-start.6 = (bf16[64,2176]{1,0:T(8,128)(2,1)S(1)}, bf16[64,2176]{1,0:T(8,128)(2,1)}, u32[]{:S(2)}, u32[]{:S(2)}) collective-permute-start(bf16[64,2176]{1,0:T(8,128)(2,1)S(1)} %collective-permute-done.2.refs_3_), channel_id=1, source_target_pairs={{0,8},{1,9},{2,10},{3,11},{4,12},{5,13},{6,14},{7,15},{8,0},{9,1},... | collective-permute-start | bytes 835592 | tf_op jit(solution)/shard_map/ppermute | solution.py:322
  57.8 25.0 %collective-permute-start.19 = (bf16[256,2048]{1,0:T(8,128)(2,1)}, bf16[256,2048]{1,0:T(8,128)(2,1)S(1)}, u32[]{:S(2)}, u32[]{:S(2)}) collective-permute-start(bf16[256,2048]{1,0:T(8,128)(2,1)} %get-tuple-element.22), channel_id=1, source_target_pairs={{0,8},{1,9},{2,10},{3,11},{4,12},{5,13},{6,14},{7,15},{8,0},{9,1},... | collective-permute-start | bytes 3145736 | tf_op jit(solution)/shard_map/ppermute | solution.py:322
  82.4 3.0 %collective-permute-start.7 = (bf16[256,2048]{1,0:T(8,128)(2,1)}, bf16[256,2048]{1,0:T(8,128)(2,1)S(1)}, u32[]{:S(2)}, u32[]{:S(2)}) collective-permute-start(bf16[256,2048]{1,0:T(8,128)(2,1)} %get-tuple-element.17), channel_id=1, source_target_pairs={{0,8},{1,9},{2,10},{3,11},{4,12},{5,13},{6,14},{7,15},{8,0},{9,1},... | collective-permute-start | bytes 3145736 | tf_op jit(solution)/shard_map/ppermute | solution.py:322
  82.9 6.4 %collective-permute-start.22 = (bf16[64,2048]{1,0:T(8,128)(2,1)S(1)}, bf16[64,2048]{1,0:T(8,128)(2,1)S(1)}, u32[]{:S(2)}, u32[]{:S(2)}) collective-permute-start(bf16[64,2048]{1,0:T(8,128)(2,1)S(1)} %add_convert_fusion.1), channel_id=1, source_target_pairs={{0,1},{1,0},{2,3},{3,2},{4,5},{5,4},{6,7},{7,6},{8,10},{9,11},{10,... | collective-permute-start | bytes 786440 | tf_op jit(solution)/shard_map/ppermute | solution.py:322
  86.3 6.4 %collective-permute-start.9 = (bf16[64,2048]{1,0:T(8,128)(2,1)S(1)}, bf16[64,2048]{1,0:T(8,128)(2,1)S(1)}, u32[]{:S(2)}, u32[]{:S(2)}) collective-permute-start(bf16[64,2048]{1,0:T(8,128)(2,1)S(1)} %add_convert_fusion.7), channel_id=1, source_target_pairs={{0,1},{1,0},{2,3},{3,2},{4,5},{5,4},{6,7},{7,6},{8,10},{9,11},{10,... | collective-permute-start | bytes 786440 | tf_op jit(solution)/shard_map/ppermute | solution.py:322
  89.5 9.9 %collective-permute-start.20 = (bf16[64,2048]{1,0:T(8,128)(2,1)S(1)}, bf16[64,2048]{1,0:T(8,128)(2,1)S(1)}, u32[]{:S(2)}, u32[]{:S(2)}) collective-permute-start(bf16[64,2048]{1,0:T(8,128)(2,1)S(1)} %get-tuple-element.34), channel_id=1, source_target_pairs={{0,1},{1,0},{2,3},{3,2},{4,5},{5,4},{6,7},{7,6},{8,10},{9,11},{10,... | collective-permute-start | bytes 786440 | tf_op jit(solution)/shard_map/ppermute | solution.py:322
  94.9 10.9 %collective-permute-start.8 = (bf16[64,2048]{1,0:T(8,128)(2,1)S(1)}, bf16[64,2048]{1,0:T(8,128)(2,1)S(1)}, u32[]{:S(2)}, u32[]{:S(2)}) collective-permute-start(bf16[64,2048]{1,0:T(8,128)(2,1)S(1)} %get-tuple-element.36), channel_id=1, source_target_pairs={{0,1},{1,0},{2,3},{3,2},{4,5},{5,4},{6,7},{7,6},{8,10},{9,11},{10,... | collective-permute-start | bytes 786440 | tf_op jit(solution)/shard_map/ppermute | solution.py:322
  96.0 12.4 %collective-permute-start.10 = (bf16[64,2048]{1,0:T(8,128)(2,1)S(1)}, bf16[64,2048]{1,0:T(8,128)(2,1)S(1)}, u32[]{:S(2)}, u32[]{:S(2)}) collective-permute-start(bf16[64,2048]{1,0:T(8,128)(2,1)S(1)} %get-tuple-element.35), channel_id=1, source_target_pairs={{0,16},{1,17},{2,18},{3,19},{4,20},{5,21},{6,22},{7,23},{8,9},{9,8... | collective-permute-start | bytes 786440 | tf_op jit(solution)/shard_map/ppermute | solution.py:322
  98.4 10.0 %collective-permute-start.23 = (bf16[64,2048]{1,0:T(8,128)(2,1)S(1)}, bf16[64,2048]{1,0:T(8,128)(2,1)S(1)}, u32[]{:S(2)}, u32[]{:S(2)}) collective-permute-start(bf16[64,2048]{1,0:T(8,128)(2,1)S(1)} %get-tuple-element.33), channel_id=1, source_target_pairs={{0,18},{1,19},{2,16},{3,17},{4,22},{5,23},{6,20},{7,21},{8,25},{9,... | collective-permute-start | bytes 786440 | tf_op jit(solution)/shard_map/ppermute | solution.py:322
  99.6 8.8 %collective-permute-start.21 = (bf16[64,2048]{1,0:T(8,128)(2,1)S(1)}, bf16[64,2048]{1,0:T(8,128)(2,1)S(1)}, u32[]{:S(2)}, u32[]{:S(2)}) collective-permute-start(bf16[64,2048]{1,0:T(8,128)(2,1)S(1)} %add_convert_fusion.3), channel_id=1, source_target_pairs={{0,2},{1,3},{2,0},{3,1},{4,6},{5,7},{6,4},{7,5},{8,24},{9,25},{10,... | collective-permute-start | bytes 786440 | tf_op jit(solution)/shard_map/ppermute | solution.py:322
  111.7 14.7 %collective-permute-start.27 = (bf16[64,2048]{1,0:T(8,128)(2,1)}, bf16[64,2048]{1,0:T(8,128)(2,1)S(1)}, u32[]{:S(2)}, u32[]{:S(2)}) collective-permute-start(bf16[64,2048]{1,0:T(8,128)(2,1)} %get-tuple-element.28.refs_0_), channel_id=1, source_target_pairs={{0,4},{1,5},{2,6},{3,7},{4,0},{5,1},{6,2},{7,3},{8,12},{9,13},{10,... | collective-permute-start | bytes 786440 | tf_op jit(solution)/shard_map/ppermute | solution.py:322
  114.3 14.5 %collective-permute-start.24 = (bf16[64,2048]{1,0:T(8,128)(2,1)}, bf16[64,2048]{1,0:T(8,128)(2,1)S(1)}, u32[]{:S(2)}, u32[]{:S(2)}) collective-permute-start(bf16[64,2048]{1,0:T(8,128)(2,1)} %get-tuple-element.28.refs_0_), channel_id=1, source_target_pairs={{0,1},{1,0},{2,3},{3,2},{4,5},{5,4},{6,7},{7,6},{8,10},{9,11},{10,... | collective-permute-start | bytes 786440 | tf_op jit(solution)/shard_map/ppermute | solution.py:322
  126.4 26.1 %collective-permute-start.28 = (bf16[64,2048]{1,0:T(8,128)(2,1)S(1)}, bf16[64,2048]{1,0:T(8,128)(2,1)S(1)}, u32[]{:S(2)}, u32[]{:S(2)}) collective-permute-start(bf16[64,2048]{1,0:T(8,128)(2,1)S(1)} %collective-permute-done.27.refs_0_), channel_id=1, source_target_pairs={{0,1},{1,0},{2,3},{3,2},{4,5},{5,4},{6,7},{7,6},{8,10},{9,11},{10,... | collective-permute-start | bytes 786440 | tf_op jit(solution)/shard_map/ppermute | solution.py:322
  127.8 25.8 %collective-permute-start.25 = (bf16[64,2048]{1,0:T(8,128)(2,1)}, bf16[64,2048]{1,0:T(8,128)(2,1)S(1)}, u32[]{:S(2)}, u32[]{:S(2)}) collective-permute-start(bf16[64,2048]{1,0:T(8,128)(2,1)} %get-tuple-element.28.refs_0_), channel_id=1, source_target_pairs={{0,2},{1,3},{2,0},{3,1},{4,6},{5,7},{6,4},{7,5},{8,9},{9,8},{10,11... | collective-permute-start | bytes 786440 | tf_op jit(solution)/shard_map/ppermute | solution.py:322
  128.8 24.8 %collective-permute-start.26 = (bf16[64,2048]{1,0:T(8,128)(2,1)S(1)}, bf16[64,2048]{1,0:T(8,128)(2,1)S(1)}, u32[]{:S(2)}, u32[]{:S(2)}) collective-permute-start(bf16[64,2048]{1,0:T(8,128)(2,1)S(1)} %collective-permute-done.24.refs_1_), channel_id=1, source_target_pairs={{0,2},{1,3},{2,0},{3,1},{4,6},{5,7},{6,4},{7,5},{8,9},{9,8},{10,11... | collective-permute-start | bytes 786440 | tf_op jit(solution)/shard_map/ppermute | solution.py:322
  151.5 15.8 %collective-permute-start.29 = (bf16[64,2048]{1,0:T(8,128)(2,1)S(1)}, bf16[64,2048]{1,0:T(8,128)(2,1)S(1)}, u32[]{:S(2)}, u32[]{:S(2)}) collective-permute-start(bf16[64,2048]{1,0:T(8,128)(2,1)S(1)} %collective-permute-done.27.refs_0_), channel_id=1, source_target_pairs={{0,2},{1,3},{2,0},{3,1},{4,6},{5,7},{6,4},{7,5},{8,9},{9,8},{10,11... | collective-permute-start | bytes 786440 | tf_op jit(solution)/shard_map/ppermute | solution.py:322
  152.5 14.8 %collective-permute-start.30 = (bf16[64,2048]{1,0:T(8,128)(2,1)S(1)}, bf16[64,2048]{1,0:T(8,128)(2,1)S(1)}, u32[]{:S(2)}, u32[]{:S(2)}) collective-permute-start(bf16[64,2048]{1,0:T(8,128)(2,1)S(1)} %collective-permute-done.28.refs_1_), channel_id=1, source_target_pairs={{0,2},{1,3},{2,0},{3,1},{4,6},{5,7},{6,4},{7,5},{8,9},{9,8},{10,11... | collective-permute-start | bytes 786440 | tf_op jit(solution)/shard_map/ppermute | solution.py:322
  182.4 12.5 %all-to-all-start = ((f32[8,1,64]{2,1,0:T(1,128)}), f32[8,1,64]{2,1,0:T(1,128)S(1)}, u32[]{:S(2)}, u32[]{:S(2)}) async-start(f32[8,1,64]{2,1,0:T(1,128)} %bitcast.11), calls=%async_computation | async-start | bytes 8192 | tf_op jit(solution)/shard_map/all_to_all | solution.py:386
  (29 other events, 386.5 us)

commit v2 on v1

v2 whole, which is shorter than its diff:
```python
import functools

import jax
import jax.numpy as jnp
from jax import lax
from jax.experimental import pallas as pl
from jax.experimental.pallas import tpu as pltpu
from jax.sharding import PartitionSpec as P

CAP = 24
META = 128
CUT = 768
HAND_ON = 0
VMEM_LIMIT = 60 * 1024 * 1024

norm_eps = 1e-05
AXES = ("req", "exp")
F32 = jnp.float32
BF16 = jnp.bfloat16


def flip_pairs(n_req, n_exp, dim_of_core):
    pairs = []
    for r in range(n_req):
        for e in range(n_exp):
            flips = dim_of_core[r & 1]
            pr, pe = r, e
            for axis, bit in flips:
                if axis == "req":
                    pr ^= bit
                else:
                    pe ^= bit
            pairs.append((r * n_exp + e, pr * n_exp + pe))
    return pairs


def bits_below(n, first=1):
    out = []
    b = first
    while b < n:
        out.append(b)
        b *= 2
    return out


def prepare_kernel(tokens_ref, routes_ref, router_ref, out_ref):
    width = tokens_ref.shape[1]
    rows = tokens_ref.shape[0]
    t = tokens_ref[...]
    out_ref[:, :width] = t
    logits = lax.dot_general(
        t, router_ref[...], (((1,), (1,)), ((), ())), preferred_element_type=F32
    )
    gating = 1.0 / (1.0 + jnp.exp(-logits))
    routes = jnp.transpose(
        jnp.concatenate([routes_ref[...].astype(F32), jnp.zeros((6, rows), F32)], axis=0)
    )
    lane = lax.broadcasted_iota(jnp.int32, (rows, META), 1)
    expert = lax.broadcasted_iota(jnp.int32, gating.shape, 1).astype(F32)
    meta = jnp.zeros((rows, META), F32)
    for k in range(2):
        ids = routes[:, k : k + 1]
        chosen = jnp.sum(jnp.where(expert == ids, gating, 0.0), axis=1, keepdims=True)
        high = chosen.astype(BF16).astype(F32)
        mid = (chosen - high).astype(BF16).astype(F32)
        low = chosen - high - mid
        for j, piece in enumerate((ids, high, mid, low)):
            meta = jnp.where(lane == 4 * k + j, piece, meta)
    out_ref[:, width:] = meta.astype(BF16)


def prepare(tokens, routes, router):
    rows, width = tokens.shape
    return pl.pallas_call(
        prepare_kernel,
        out_shape=jax.ShapeDtypeStruct((rows, width + META), BF16),
        compiler_params=params(8 * 1024 * 1024),
        name="prepare",
    )(tokens, routes.T, router.T)


def near_core(x):
    return pltpu.with_memory_space_constraint(x, pltpu.VMEM)


LOCAL = pl.BlockSpec(memory_space=pltpu.VMEM)


def params(limit):
    return pltpu.CompilerParams(vmem_limit_bytes=limit)


def fetch_kernel(parts, from_ref, after_ref, to_ref, sems):
    rows = to_ref.shape[0] // parts
    copies = [
        pltpu.make_async_copy(
            from_ref.at[pl.ds(i * rows, rows)], to_ref.at[pl.ds(i * rows, rows)], sems.at[i]
        )
        for i in range(parts)
    ]
    for c in copies:
        c.start()
    for c in copies:
        c.wait()


def fetch(x, after):
    parts = max(p for p in range(1, 9) if x.shape[0] % (16 * p) == 0)
    size = x.size * x.dtype.itemsize
    return pl.pallas_call(
        functools.partial(fetch_kernel, parts),
        in_specs=[pl.BlockSpec(memory_space=pl.ANY)] * 2,
        out_specs=LOCAL,
        out_shape=pltpu.VMEM(x.shape, x.dtype),
        scratch_shapes=[pltpu.SemaphoreType.DMA((parts,))],
        compiler_params=params(1024 * 1024),
        cost_estimate=pl.CostEstimate(flops=0, bytes_accessed=size, transcendentals=0),
        name="fetch",
    )(pltpu.with_memory_space_constraint(x, pltpu.HBM), after)


def pieces(size, want):
    return size // want if size % want == 0 else 1


def spans(size, want):
    return [(at, min(want, size - at)) for at in range(0, size, want)]


def expert_kernel(blocks, slots, held, hand_on, expert_ref, *refs):
    half = blocks // 2
    block_refs, refs = refs[:blocks], refs[blocks:]
    weight_refs, refs = refs[:3], refs[3:]
    own_refs, other_ref, refs = refs[:half], refs[half], refs[half + 1 :]
    kept, refs = refs[:hand_on], refs[hand_on:]
    table, hidden, weighted, refs = refs[0], refs[1], refs[2], refs[3:]
    loaded, sems = list(kept) + list(refs[:-1]), refs[-1]
    rows = block_refs[0].shape[0]
    width, units = weight_refs[0].shape
    count = blocks * rows
    weights = list(weight_refs[:held]) + loaded
    cuts = [spans(units, CUT), spans(units, CUT), spans(width, CUT)]
    waits = [[] for _ in range(3)]

    def load(w, j):
        if w >= held:
            at, size = cuts[w][j]
            c = pltpu.make_async_copy(
                weight_refs[w].at[:, pl.ds(at, size)],
                weights[w].at[:, pl.ds(at, size)],
                sems.at[w, j],
            )
            c.start()
            waits[w].append(c)

    def arrive(w, j):
        if w >= held:
            waits[w][j].wait()

    for j in range(len(cuts[0])):
        load(0, j)
        load(1, j)
    for j in range(len(cuts[2])):
        load(2, j)
    for i, ref in enumerate(block_refs):
        table[i * rows : (i + 1) * rows, :] = ref[...]
    own = expert_ref[0].astype(F32)
    meta = jnp.transpose(table[:, width:].astype(F32))
    first = meta[0:1] == own
    second = meta[4:5] == own
    member = jnp.logical_or(first, second)
    weight = jnp.where(first, meta[1:2] + meta[2:3] + meta[3:4], meta[5:6] + meta[6:7] + meta[7:8])
    flag = jnp.where(member, 1.0, 0.0)
    part = min(count, 512)
    before = lax.broadcasted_iota(jnp.int32, (part, part), 0) < lax.broadcasted_iota(
        jnp.int32, (part, part), 1
    )
    before = jnp.where(before, 1.0, 0.0).astype(BF16)
    ranks, base = [], jnp.zeros((1, 1), F32)
    for at in range(0, count, part):
        some = flag[:, at : at + part]
        rank = jnp.dot(
            jnp.broadcast_to(some, (8, part)).astype(BF16), before, preferred_element_type=F32
        )
        ranks.append(rank[0:1] + base)
        base = base + jnp.sum(some, axis=1, keepdims=True)
    rank = jnp.where(member, jnp.concatenate(ranks, axis=1), -1.0).astype(jnp.int32)
    chosen = lax.broadcasted_iota(jnp.int32, (slots, count), 0) == rank
    place = jnp.where(chosen, 1.0, 0.0).astype(BF16)
    scale = jnp.sum(jnp.where(chosen, weight, 0.0), axis=1, keepdims=True)
    x = jnp.dot(place, table[:, :width], preferred_element_type=F32).astype(BF16)
    back = jnp.transpose(place)
    for j, (start, size) in enumerate(cuts[0]):
        arrive(0, j)
        arrive(1, j)
        for at, some in spans(size, 256):
            at = slice(start + at, start + at + some)
            g = jnp.dot(x, weights[0][:, at], preferred_element_type=F32)
            u = jnp.dot(x, weights[1][:, at], preferred_element_type=F32)
            hidden[:, at] = (g / (1.0 + jnp.exp(-g)) * u).astype(BF16)
    for j, (start, size) in enumerate(cuts[2]):
        arrive(2, j)
        for at, some in spans(size, 256):
            at = slice(start + at, start + at + some)
            y = jnp.dot(hidden[...], weights[2][:, at], preferred_element_type=F32)
            weighted[:, at] = (y * scale).astype(BF16)
    for start, size in spans(width, 1024):
        at = slice(start, start + size)
        spread = jnp.dot(back, weighted[:, at], preferred_element_type=F32).astype(BF16)
        for i, ref in enumerate(own_refs):
            ref[:, at] = spread[i * rows : (i + 1) * rows]
        other_ref[:, at] = spread[half * rows :]


def run_expert(expert, block_list, weights, cap, held, hand_on):
    blocks = len(block_list)
    rows = block_list[0].shape[0]
    width, units = weights[0].shape
    slots = blocks * cap
    count = blocks * rows
    half = blocks // 2
    loads = [pltpu.VMEM(w.shape, BF16) for w in weights]
    cuts = len(spans(max(units, width), CUT))
    scoped = sum(2 * width * units for _ in weights[max(held, hand_on) :])
    return pl.pallas_call(
        functools.partial(expert_kernel, blocks, slots, held, hand_on),
        in_specs=[pl.BlockSpec(memory_space=pltpu.SMEM)]
        + [LOCAL] * (blocks + held)
        + [pl.BlockSpec(memory_space=pl.ANY)] * (3 - held),
        out_specs=[LOCAL] * (half + 1 + hand_on),
        out_shape=[jax.ShapeDtypeStruct((rows, width), BF16)] * half
        + [jax.ShapeDtypeStruct((half * rows, width), BF16)]
        + loads[:hand_on],
        scratch_shapes=[
            pltpu.VMEM((count, width + META), BF16),
            pltpu.VMEM((slots, units), BF16),
            pltpu.VMEM((slots, width), BF16),
            *loads[max(held, hand_on) :],
            pltpu.SemaphoreType.DMA((3, cuts)),
        ],
        compiler_params=params(scoped + 10 * count * (width + META)),
        cost_estimate=pl.CostEstimate(
            flops=10 * slots * width * units + 4 * slots * count * width,
            bytes_accessed=6 * width * units,
            transcendentals=slots * units,
        ),
        name="expert",
    )(
        expert,
        *map(near_core, block_list),
        *map(near_core, weights[:held]),
        *(pltpu.with_memory_space_constraint(w, pltpu.HBM) for w in weights[held:]),
    )


def add_kernel(count, rows, *refs):
    own, other, out = refs[:count], refs[count:-count], refs[-count:]
    for i in range(count):
        got = other[0][i * rows : (i + 1) * rows] if len(other) == 1 else other[i][...]
        out[i][...] = (own[i][...].astype(F32) + got.astype(F32)).astype(BF16)


def add_blocks(own, other):
    count = len(own)
    rows, width = own[0].shape
    return pl.pallas_call(
        functools.partial(add_kernel, count, rows),
        in_specs=[LOCAL] * (count + len(other)),
        out_specs=[LOCAL] * count,
        out_shape=[jax.ShapeDtypeStruct((rows, width), BF16)] * count,
        compiler_params=params(12 * count * rows * width),
        cost_estimate=pl.CostEstimate(
            flops=count * rows * width, bytes_accessed=6 * count * rows * width, transcendentals=0
        ),
        name="add_blocks",
    )(*own, *other)


def finish_kernel(parts, lengths_ref, tokens_ref, gain_ref, *refs):
    hidden_ref, normed_ref, norm_ref = refs[parts:]
    total = refs[0][...].astype(F32)
    for ref in refs[1:parts]:
        total = total + ref[...].astype(F32)
    hidden = (tokens_ref[...].astype(F32) + total).astype(BF16)
    hidden_ref[...] = hidden
    wide = hidden.astype(F32)
    width = wide.shape[1]
    square = jnp.sum(wide * wide, axis=1, keepdims=True)
    normed_ref[...] = (wide * lax.rsqrt(square / width + norm_eps) * gain_ref[...]).astype(BF16)
    row = lax.broadcasted_iota(jnp.int32, square.shape, 0)
    lane = lax.broadcasted_iota(jnp.int32, norm_ref.shape, 1)
    out, start = jnp.zeros(norm_ref.shape, F32), 0
    for j in range(norm_ref.shape[1]):
        end = start + lengths_ref[0, j]
        member = jnp.logical_and(row >= start, row < end)
        mean = jnp.sum(jnp.where(member, square, 0.0), axis=0, keepdims=True) / (
            lengths_ref[0, j].astype(F32) * width
        )
        out = jnp.where(lane == j, jnp.sqrt(mean), out)
        start = end
    norm_ref[...] = out


def finish(lengths, tokens, gain, parts):
    rows, width = tokens.shape
    return pl.pallas_call(
        functools.partial(finish_kernel, len(parts)),
        in_specs=[pl.BlockSpec(memory_space=pltpu.SMEM)] + [LOCAL] * (2 + len(parts)),
        out_specs=[LOCAL] * 3,
        out_shape=[
            jax.ShapeDtypeStruct((rows, width), BF16),
            jax.ShapeDtypeStruct((rows, width), BF16),
            jax.ShapeDtypeStruct(lengths.shape, F32),
        ],
        compiler_params=params(8 * 1024 * 1024),
        name="finish",
    )(lengths, tokens, gain, *parts)


def request_kernel(lengths_ref, *refs):
    out_ref = refs[-1]
    peak = refs[0][...]
    for ref in refs[1:-1]:
        peak = jnp.maximum(peak, ref[...])
    row = lax.broadcasted_iota(jnp.int32, peak.shape, 1)
    lane = lax.broadcasted_iota(jnp.int32, out_ref.shape, 1)
    out, start = jnp.zeros(out_ref.shape, F32), 0
    for j in range(out_ref.shape[1]):
        end = start + lengths_ref[0, j]
        member = jnp.logical_and(row >= start, row < end)
        best = jnp.max(jnp.where(member, peak, -jnp.inf), axis=1, keepdims=True)
        out = jnp.where(lane == j, best, out)
        start = end
    out_ref[...] = out


def request_peaks(lengths, found):
    return pl.pallas_call(
        request_kernel,
        in_specs=[pl.BlockSpec(memory_space=pltpu.SMEM)] + [LOCAL] * len(found),
        out_specs=LOCAL,
        out_shape=jax.ShapeDtypeStruct(lengths.shape, F32),
        compiler_params=params(1024 * 1024),
        name="request_peaks",
    )(lengths, *found)


def peak_kernel(blocks, *refs):
    block_refs = refs[:blocks]
    head_ref, out_ref, table = refs[blocks:]
    rows = block_refs[0].shape[0]
    words = head_ref.shape[0]
    for i, ref in enumerate(block_refs):
        table[i * rows : (i + 1) * rows, :] = ref[...]
    tile = max(t for t in range(16, 513, 16) if words % t == 0)
    best = None
    for j in range(words // tile):
        logits = lax.dot_general(
            head_ref[j * tile : (j + 1) * tile, :],
            table[...],
            (((1,), (1,)), ((), ())),
            preferred_element_type=F32,
        )
        peak = jnp.max(logits, axis=0, keepdims=True)
        best = peak if best is None else jnp.maximum(best, peak)
    for i in range(blocks):
        out_ref[i : i + 1, :] = best[:, i * rows : (i + 1) * rows]


def peaks(block_list, words_first):
    blocks = len(block_list)
    rows, width = block_list[0].shape
    words = words_first.shape[0]
    return pl.pallas_call(
        functools.partial(peak_kernel, blocks),
        in_specs=[LOCAL] * (blocks + 1),
        out_specs=LOCAL,
        out_shape=jax.ShapeDtypeStruct((blocks, rows), F32),
        scratch_shapes=[pltpu.VMEM((blocks * rows, width), BF16)],
        compiler_params=params(12 * 1024 * 1024),
        cost_estimate=pl.CostEstimate(
            flops=2 * blocks * rows * width * words,
            bytes_accessed=2 * blocks * rows * width,
            transcendentals=0,
        ),
        name="peaks",
    )(*map(near_core, block_list), near_core(words_first))


def per_device(
    n_req,
    n_exp,
    tokens,
    routes,
    router,
    gate_weight,
    up_weight,
    down_weight,
    norm_gain,
    head_weight,
    lengths,
):
    row_count, width = tokens.shape
    experts = router.shape[1]
    half_exp = n_exp // 2
    group_size = n_req * n_exp // (2 * experts)
    r = lax.axis_index("req")
    e = lax.axis_index("exp")
    expert = ((r * half_exp + e % half_exp) // group_size).astype(jnp.int32).reshape(1)

    def send(x, flips0, flips1=None):
        pairs = flip_pairs(n_req, n_exp, (flips0, flips0 if flips1 is None else flips1))
        return lax.ppermute(x, AXES, pairs)

    core = [("req", 1)]
    dims = [("req", b) for b in bits_below(n_req, 2)] + [("exp", b) for b in bits_below(half_exp)]
    extra, dims = dims[3:], dims[:3]
    turned = dims[1:] + dims[:1]

    def hop(x, *js):
        return send(x, [dims[j] for j in js], [turned[j] for j in js])

    block = prepare(tokens, routes, router)
    for d in extra:
        block = jnp.concatenate([block, send(block, [d])], axis=0)
    near = [block, hop(block, 0)]
    near += [hop(b, 1) for b in near]
    far = [hop(b, 2) for b in near]
    near += [send(b, core) for b in near]
    cap = CAP * block.shape[0] // row_count
    rows = block.shape[0]
    blocks = len(near)

    weights = [gate_weight, up_weight, down_weight]
    out = run_expert(expert, near, weights, cap, 0, HAND_ON)
    half = blocks // 2
    near_out, near_other, weights[:HAND_ON] = out[:half], out[half], out[half + 1 :]
    far, near_out = lax.optimization_barrier((far, near_out))
    far += [send(b, core) for b in far]
    out = run_expert(expert, far, weights, cap, HAND_ON, 0)
    far_out, far_other = out[:half], out[half]
    near_sum = add_blocks(near_out, [send(near_other, core)])
    n3 = hop(near_sum[3], 1)
    n2 = hop(near_sum[2], 1)
    n1 = hop(add_blocks([near_sum[1]], [n3])[0], 0)
    words_first = fetch(head_weight.T, far_other)
    far_sum = add_blocks(far_out, [send(far_other, core)])
    f3 = hop(far_sum[3], 1)
    f2 = hop(far_sum[2], 1)
    f1 = hop(add_blocks([far_sum[1]], [f3])[0], 0, 2)
    f0 = hop(add_blocks([far_sum[0]], [f2])[0], 2)
    parts = [near_sum[0], n2, n1, f0, f1]
    for d in reversed(extra):
        merged = sum(p.astype(F32) for p in parts).astype(BF16)
        size = merged.shape[0] // 2
        parts = [merged[:size], send(merged[size:], [d])]
    parts, words_first = lax.optimization_barrier((parts, words_first))
    hidden_out, normed, request_norm = finish(lengths, tokens, norm_gain.reshape(1, width), parts)

    near_dims = [("exp", b) for b in bits_below(half_exp)]
    near_turn = near_dims[1:] + near_dims[:1]
    across = ("exp", half_exp)
    ways = [([], [])]
    for p, q in zip(near_dims, near_turn):
        ways += [(a + [p], b + [q]) for a, b in ways]
    far_first = send(normed, [across])
    near_blocks = [normed] + [send(normed, *w) for w in ways[1:]]
    far_blocks = [far_first] + [send(far_first, *w) for w in ways[1:]]
    near_blocks, far_first = lax.optimization_barrier((near_blocks, far_first))
    near_peak = peaks(near_blocks, words_first)
    far_first, near_peak = lax.optimization_barrier((far_first, near_peak))
    first_peak = peaks([far_first], words_first)
    far_peak = peaks(far_blocks[1:], words_first)
    found = [near_peak[0:1]]
    found += [send(near_peak[i : i + 1], *w) for i, w in enumerate(ways) if i > 0]
    found += [send(first_peak, [across])]
    found += [
        send(far_peak[i : i + 1], p + [across], q + [across])
        for i, (p, q) in enumerate(ways[1:])
    ]
    request_max = request_peaks(lengths, found)
    return (hidden_out, request_norm[0], request_max[0])


def solution(mesh):
    placed = (
        P(AXES, None),
        P(AXES, None),
        P(),
        P(None, AXES),
        P(None, AXES),
        P(AXES, None),
        P(),
        P(None, "exp"),
        P(AXES, None),
    )
    return jax.shard_map(
        functools.partial(per_device, mesh.shape["req"], mesh.shape["exp"]),
        mesh=mesh,
        in_specs=placed,
        out_specs=(P(AXES, None), P(AXES), P(AXES)),
        check_vma=False,
    )
```

time: 197 us -> 128 us (0.65)
  Pallas kernels: 77.7 us -> 50.1 us
  local copies, waits for them, and re-layouts: 28.4 us -> 2.4 us
  waiting for transfers between devices: 44.7 us -> 29.3 us
  starting transfers between devices: 37.4 us -> 44.6 us
  other arithmetic: 6.86 us -> 0 us
    pallas_call x5 -> x13, Pallas kernels: 75.5 us -> 49.8 us  [the longest x2 27.3 us: run_expert(): pl.pallas_call(functools.partial(expert_kernel, blocks, slots, held, hand...]
    unnamed x61 -> x12, local copies, waits for them, and re-layouts: 27.7 us -> 2.39 us
    ppermute x31 -> x38, starting transfers between devices: 31.4 us -> 44.6 us  [send(): return lax.ppermute(x, AXES, pairs)]
    ppermute x31 -> x38, waiting for transfers between devices: 38.9 us -> 29.3 us  [send(): return lax.ppermute(x, AXES, pairs)]
    all_to_all x1 -> x0, starting transfers between devices: 6.01 us -> none  [per_device(): lax.all_to_all(jnp.maximum(near_peak, far_peak), 'exp', 0, 0, tiled=True)]
    all_to_all x1 -> x0, waiting for transfers between devices: 5.78 us -> none  [per_device(): lax.all_to_all(jnp.maximum(near_peak, far_peak), 'exp', 0, 0, tiled=True)]
    convert_element_type x5 -> x0, other arithmetic: 3.48 us -> none  [add(): return (a.astype(F32) + b.astype(F32)).astype(BF16)]
  transfers between devices with their start and end apart: 32 -> 38, of which waited for: 14 -> 17; matrix products, arithmetic and copies ran while one was open for 13% -> 0% of each run, Pallas kernels for 31% -> 34%
where the time goes in v2:
time: 128 us; the launch traced here: 127 us
  Pallas kernels  50.1 us (39%)
  starting transfers between devices  44.6 us (35%)
  waiting for transfers between devices  29.3 us (23%)
  local copies, waits for them, and re-layouts  2.4 us (2%)
    ppermute x38, starting transfers between devices, send(): return lax.ppermute(x, AXES, pairs)  44.6 us
    ppermute x38, waiting for transfers between devices, send(): return lax.ppermute(x, AXES, pairs)  29.3 us
    pallas_call x2, Pallas kernels, run_expert(): pl.pallas_call(functools.partial(expert_kernel, blocks, slots, held, hand...  27.3 us
    pallas_call x3, Pallas kernels, peaks(): pl.pallas_call(functools.partial(peak_kernel, blocks), in_specs=[LOCAL] *...  13.4 us
    pallas_call x1, Pallas kernels, fetch(): pl.pallas_call(functools.partial(fetch_kernel, parts), in_specs=[pl.Block...  5.8 us
  transfers between devices with their start and end apart: 38, of which 17 were waited for; matrix products, arithmetic and copies ran while one was open for 0% of the time, Pallas kernels for 34%

profile of v2, /device:TPU:0, one launch (start us, length us, event | category | flops | bytes accessed | tf_op | source)
XLA Modules:
  0.0 127.3 jit_solution(12333997534951662039)
XLA Ops:
  3.3 3.0 %collective-permute-start.1 = (bf16[64,2176]{1,0:T(8,128)(2,1)S(1)}, bf16[64,2176]{1,0:T(8,128)(2,1)S(1)}, u32[]{:S(2)}, u32[]{:S(2)}) collective-permute-start(bf16[64,2176]{1,0:T(8,128)(2,1)S(1)} %prepare.1.refs_0_), channel_id=1, source_target_pairs={{0,16},{1,17},{2,18},{3,19},{4,20},{5,21},{6,22},{7,23},{8,9},{9,8... | collective-permute-start | bytes 835592 | tf_op jit(solution)/shard_map/ppermute | solution.py:413
  6.3 1.5 %collective-permute-start.3 = (bf16[64,2176]{1,0:T(8,128)(2,1)S(1)}, bf16[64,2176]{1,0:T(8,128)(2,1)S(1)}, u32[]{:S(2)}, u32[]{:S(2)}) collective-permute-start(bf16[64,2176]{1,0:T(8,128)(2,1)S(1)} %prepare.1.refs_0_), channel_id=1, source_target_pairs={{0,1},{1,0},{2,3},{3,2},{4,5},{5,4},{6,7},{7,6},{8,10},{9,11},{10,... | collective-permute-start | bytes 835592 | tf_op jit(solution)/shard_map/ppermute | solution.py:413
  7.9 3.0 %collective-permute-done.1.refs_1_ = bf16[64,2176]{1,0:T(8,128)(2,1)S(1)} collective-permute-done((bf16[64,2176]{1,0:T(8,128)(2,1)S(1)}, bf16[64,2176]{1,0:T(8,128)(2,1)S(1)}, u32[]{:S(2)}, u32[]{:S(2)}) %collective-permute-start.1) | collective-permute-done | bytes 278560 | tf_op jit(solution)/shard_map/ppermute | solution.py:413
  10.9 2.0 %collective-permute-start.5 = (bf16[64,2176]{1,0:T(8,128)(2,1)S(1)}, bf16[64,2176]{1,0:T(8,128)(2,1)S(1)}, u32[]{:S(2)}, u32[]{:S(2)}) collective-permute-start(bf16[64,2176]{1,0:T(8,128)(2,1)S(1)} %collective-permute-done.1.refs_1_), channel_id=1, source_target_pairs={{0,1},{1,0},{2,3},{3,2},{4,5},{5,4},{6,7},{7,6},{8,10},{9,11},{10,... | collective-permute-start | bytes 835592 | tf_op jit(solution)/shard_map/ppermute | solution.py:413
  13.5 3.9 %collective-permute-done.5.refs_3_ = bf16[64,2176]{1,0:T(8,128)(2,1)S(1)} collective-permute-done((bf16[64,2176]{1,0:T(8,128)(2,1)S(1)}, bf16[64,2176]{1,0:T(8,128)(2,1)S(1)}, u32[]{:S(2)}, u32[]{:S(2)}) %collective-permute-start.5) | collective-permute-done | bytes 278560 | tf_op jit(solution)/shard_map/ppermute | solution.py:413
  17.4 2.1 %collective-permute-start = (bf16[64,2176]{1,0:T(8,128)(2,1)S(1)}, bf16[64,2176]{1,0:T(8,128)(2,1)S(1)}, u32[]{:S(2)}, u32[]{:S(2)}) collective-permute-start(bf16[64,2176]{1,0:T(8,128)(2,1)S(1)} %prepare.1.refs_0_), channel_id=1, source_target_pairs={{0,2},{1,3},{2,0},{3,1},{4,6},{5,7},{6,4},{7,5},{8,24},{9,25},{10,... | collective-permute-start | bytes 835592 | tf_op jit(solution)/shard_map/ppermute | solution.py:413
  19.6 2.0 %collective-permute-start.2 = (bf16[64,2176]{1,0:T(8,128)(2,1)S(1)}, bf16[64,2176]{1,0:T(8,128)(2,1)S(1)}, u32[]{:S(2)}, u32[]{:S(2)}) collective-permute-start(bf16[64,2176]{1,0:T(8,128)(2,1)S(1)} %collective-permute-done.1.refs_1_), channel_id=1, source_target_pairs={{0,2},{1,3},{2,0},{3,1},{4,6},{5,7},{6,4},{7,5},{8,24},{9,25},{10,... | collective-permute-start | bytes 835592 | tf_op jit(solution)/shard_map/ppermute | solution.py:413
  21.6 13.6 %expert.2 = (bf16[64,2048]{1,0:T(8,128)(2,1)S(1)}, bf16[64,2048]{1,0:T(8,128)(2,1)S(1)}, bf16[64,2048]{1,0:T(8,128)(2,1)S(1)}, bf16[64,2048]{1,0:T(8,128)(2,1)S(1)}, bf16[256,2048]{1,0:T(8,128)(2,1)S(1)}) custom-call(s32[1]{0:T(128)} %bitcast.3.expert_ref, bf16[64,2176]{1,0:T(8,128)(2,1)S(1)} %prepare.1.refs_0_, ...), custom_call_target="tpu_custom_call" | custom-call | flops 11878268928 | bytes 34603008 | tf_op jit(solution)/shard_map/expert/pallas_call | solution.py:225
  38.1 13.8 %expert.3 = (bf16[64,2048]{1,0:T(8,128)(2,1)S(1)}, bf16[64,2048]{1,0:T(8,128)(2,1)S(1)}, bf16[64,2048]{1,0:T(8,128)(2,1)S(1)}, bf16[64,2048]{1,0:T(8,128)(2,1)S(1)}, bf16[256,2048]{1,0:T(8,128)(2,1)S(1)}) custom-call(s32[1]{0:T(128)} %bitcast.3.expert_ref, bf16[64,2176]{1,0:T(8,128)(2,1)S(1)} %collective-permute-done.refs_0_, ...), custom_call_target="tpu_custom_call" | custom-call | flops 11878268928 | bytes 34603008 | tf_op jit(solution)/shard_map/expert/pallas_call | solution.py:225
  52.3 2.0 %collective-permute-start.13 = (bf16[64,2048]{1,0:T(8,128)(2,1)S(1)}, bf16[64,2048]{1,0:T(8,128)(2,1)S(1)}, u32[]{:S(2)}, u32[]{:S(2)}) collective-permute-start(bf16[64,2048]{1,0:T(8,128)(2,1)S(1)} %get-tuple-element.57), channel_id=1, source_target_pairs={{0,1},{1,0},{2,3},{3,2},{4,5},{5,4},{6,7},{7,6},{8,10},{9,11},{10,... | collective-permute-start | bytes 786440 | tf_op jit(solution)/shard_map/ppermute | solution.py:413
  54.8 2.0 %collective-permute-start.20 = (bf16[64,2048]{1,0:T(8,128)(2,1)S(1)}, bf16[64,2048]{1,0:T(8,128)(2,1)S(1)}, u32[]{:S(2)}, u32[]{:S(2)}) collective-permute-start(bf16[64,2048]{1,0:T(8,128)(2,1)S(1)} %get-tuple-element.68), channel_id=1, source_target_pairs={{0,1},{1,0},{2,3},{3,2},{4,5},{5,4},{6,7},{7,6},{8,10},{9,11},{10,... | collective-permute-start | bytes 786440 | tf_op jit(solution)/shard_map/ppermute | solution.py:413
  56.9 1.9 %collective-permute-start.12 = (bf16[64,2048]{1,0:T(8,128)(2,1)S(1)}, bf16[64,2048]{1,0:T(8,128)(2,1)S(1)}, u32[]{:S(2)}, u32[]{:S(2)}) collective-permute-start(bf16[64,2048]{1,0:T(8,128)(2,1)S(1)} %get-tuple-element.55), channel_id=1, source_target_pairs={{0,1},{1,0},{2,3},{3,2},{4,5},{5,4},{6,7},{7,6},{8,10},{9,11},{10,... | collective-permute-start | bytes 786440 | tf_op jit(solution)/shard_map/ppermute | solution.py:413
  58.9 1.8 %collective-permute-start.14 = (bf16[64,2048]{1,0:T(8,128)(2,1)S(1)}, bf16[64,2048]{1,0:T(8,128)(2,1)S(1)}, u32[]{:S(2)}, u32[]{:S(2)}) collective-permute-start(bf16[64,2048]{1,0:T(8,128)(2,1)S(1)} %add_blocks.6), channel_id=1, source_target_pairs={{0,16},{1,17},{2,18},{3,19},{4,20},{5,21},{6,22},{7,23},{8,9},{9,8... | collective-permute-start | bytes 786440 | tf_op jit(solution)/shard_map/ppermute | solution.py:413
  61.9 2.2 %collective-permute-start.21 = (bf16[64,2048]{1,0:T(8,128)(2,1)S(1)}, bf16[64,2048]{1,0:T(8,128)(2,1)S(1)}, u32[]{:S(2)}, u32[]{:S(2)}) collective-permute-start(bf16[64,2048]{1,0:T(8,128)(2,1)S(1)} %add_blocks.8), channel_id=1, source_target_pairs={{0,2},{1,3},{2,0},{3,1},{4,6},{5,7},{6,4},{7,5},{8,24},{9,25},{10,... | collective-permute-start | bytes 786440 | tf_op jit(solution)/shard_map/ppermute | solution.py:413
  64.1 3.0 %collective-permute-done.22.refs_1_ = bf16[64,2048]{1,0:T(8,128)(2,1)S(1)} collective-permute-done((bf16[64,2048]{1,0:T(8,128)(2,1)S(1)}, bf16[64,2048]{1,0:T(8,128)(2,1)S(1)}, u32[]{:S(2)}, u32[]{:S(2)}) %collective-permute-start.22) | collective-permute-done | bytes 262176 | tf_op jit(solution)/shard_map/ppermute | solution.py:413
  67.2 3.0 %collective-permute-start.23 = (bf16[64,2048]{1,0:T(8,128)(2,1)S(1)}, bf16[64,2048]{1,0:T(8,128)(2,1)S(1)}, u32[]{:S(2)}, u32[]{:S(2)}) collective-permute-start(bf16[64,2048]{1,0:T(8,128)(2,1)S(1)} %add_blocks.9), channel_id=1, source_target_pairs={{0,18},{1,19},{2,16},{3,17},{4,22},{5,23},{6,20},{7,21},{8,25},{9,... | collective-permute-start | bytes 786440 | tf_op jit(solution)/shard_map/ppermute | solution.py:413
  70.2 5.8 %fetch.1.refs_4_.refs_1_.refs_3_ = bf16[4000,2048]{1,0:T(8,128)(2,1)S(1)} custom-call(bf16[4000,2048]{1,0:T(8,128)(2,1)} %bitcast.10, bf16[256,2048]{1,0:T(8,128)(2,1)S(1)} %get-tuple-element.66.after_ref), custom_call_target="tpu_custom_call" | custom-call | bytes 16384000 | tf_op jit(solution)/shard_map/fetch/pallas_call | solution.py:110
  77.6 2.6 %collective-permute-start.27 = (bf16[64,2048]{1,0:T(8,128)(2,1)S(1)}, bf16[64,2048]{1,0:T(8,128)(2,1)S(1)}, u32[]{:S(2)}, u32[]{:S(2)}) collective-permute-start(bf16[64,2048]{1,0:T(8,128)(2,1)S(1)} %get-tuple-element.80.refs_0_), channel_id=1, source_target_pairs={{0,4},{1,5},{2,6},{3,7},{4,0},{5,1},{6,2},{7,3},{8,12},{9,13},{10,... | collective-permute-start | bytes 786440 | tf_op jit(solution)/shard_map/ppermute | solution.py:413
  81.5 1.6 %collective-permute-start.25 = (bf16[64,2048]{1,0:T(8,128)(2,1)S(1)}, bf16[64,2048]{1,0:T(8,128)(2,1)S(1)}, u32[]{:S(2)}, u32[]{:S(2)}) collective-permute-start(bf16[64,2048]{1,0:T(8,128)(2,1)S(1)} %get-tuple-element.80.refs_0_), channel_id=1, source_target_pairs={{0,2},{1,3},{2,0},{3,1},{4,6},{5,7},{6,4},{7,5},{8,9},{9,8},{10,11... | collective-permute-start | bytes 786440 | tf_op jit(solution)/shard_map/ppermute | solution.py:413
  83.6 5.0 %collective-permute-done.27.refs_0_ = bf16[64,2048]{1,0:T(8,128)(2,1)S(1)} collective-permute-done((bf16[64,2048]{1,0:T(8,128)(2,1)S(1)}, bf16[64,2048]{1,0:T(8,128)(2,1)S(1)}, u32[]{:S(2)}, u32[]{:S(2)}) %collective-permute-start.27) | collective-permute-done | bytes 262176 | tf_op jit(solution)/shard_map/ppermute | solution.py:413
  88.6 3.7 %collective-permute-done.26.refs_3_ = bf16[64,2048]{1,0:T(8,128)(2,1)S(1)} collective-permute-done((bf16[64,2048]{1,0:T(8,128)(2,1)S(1)}, bf16[64,2048]{1,0:T(8,128)(2,1)S(1)}, u32[]{:S(2)}, u32[]{:S(2)}) %collective-permute-start.26) | collective-permute-done | bytes 262176 | tf_op jit(solution)/shard_map/ppermute | solution.py:413
  92.3 2.2 %collective-permute-done.25.refs_2_ = bf16[64,2048]{1,0:T(8,128)(2,1)S(1)} collective-permute-done((bf16[64,2048]{1,0:T(8,128)(2,1)S(1)}, bf16[64,2048]{1,0:T(8,128)(2,1)S(1)}, u32[]{:S(2)}, u32[]{:S(2)}) %collective-permute-start.25) | collective-permute-done | bytes 262176 | tf_op jit(solution)/shard_map/ppermute | solution.py:413
  94.5 4.5 %peaks.3 = f32[4,64]{1,0:T(4,128)S(1)} custom-call(bf16[64,2048]{1,0:T(8,128)(2,1)S(1)} %get-tuple-element.80.refs_0_, bf16[64,2048]{1,0:T(8,128)(2,1)S(1)} %collective-permute-done.24.refs_1_, bf16[64,2048]{1,0:T(8,128)(2,1)S(1)} %collective-permute-done.25.refs_2_, bf16[64,2048]{1,0:T(8,128)(2,1)S(1)} %collective-permute-done.26.refs_3_, ...), custom_call_target="tpu_custom_call" | custom-call | flops 4194304000 | bytes 1048576 | tf_op jit(solution)/shard_map/peaks/pallas_call | solution.py:374
  99.0 1.5 %collective-permute-start.34 = (bf16[64,2048]{1,0:T(8,128)(2,1)S(1)}, bf16[64,2048]{1,0:T(8,128)(2,1)S(1)}, u32[]{:S(2)}, u32[]{:S(2)}) collective-permute-start(bf16[64,2048]{1,0:T(8,128)(2,1)S(1)} %collective-permute-done.27.refs_0_), channel_id=1, source_target_pairs={{0,3},{1,2},{2,1},{3,0},{4,7},{5,6},{6,5},{7,4},{8,11},{9,10},{10,... | collective-permute-start | bytes 786440 | tf_op jit(solution)/shard_map/ppermute | solution.py:413
  100.5 1.5 %collective-permute-start.33 = (bf16[64,2048]{1,0:T(8,128)(2,1)S(1)}, bf16[64,2048]{1,0:T(8,128)(2,1)S(1)}, u32[]{:S(2)}, u32[]{:S(2)}) collective-permute-start(bf16[64,2048]{1,0:T(8,128)(2,1)S(1)} %collective-permute-done.27.refs_0_), channel_id=1, source_target_pairs={{0,2},{1,3},{2,0},{3,1},{4,6},{5,7},{6,4},{7,5},{8,9},{9,8},{10,11... | collective-permute-start | bytes 786440 | tf_op jit(solution)/shard_map/ppermute | solution.py:413
  104.0 1.5 %collective-permute-start.29 = (f32[1,64]{1,0:T(1,128)S(1)}, f32[1,64]{1,0:T(1,128)S(1)}, u32[]{:S(2)}, u32[]{:S(2)}) collective-permute-start(f32[1,64]{1,0:T(1,128)S(1)} %get-tuple-element.91), channel_id=1, source_target_pairs={{0,2},{1,3},{2,0},{3,1},{4,6},{5,7},{6,4},{7,5},{8,9},{9,8},{10,11... | collective-permute-start | bytes 776 | tf_op jit(solution)/shard_map/ppermute | solution.py:413
  105.5 4.4 %peaks.4 = f32[1,64]{1,0:T(1,128)S(1)} custom-call(bf16[64,2048]{1,0:T(8,128)(2,1)S(1)} %collective-permute-done.27.refs_0_, bf16[4000,2048]{1,0:T(8,128)(2,1)S(1)} %fetch.1.refs_4_.refs_1_.refs_3_), custom_call_target="tpu_custom_call" | custom-call | flops 1048576000 | bytes 262144 | tf_op jit(solution)/shard_map/peaks/pallas_call | solution.py:374
  111.9 4.5 %peaks.5 = f32[3,64]{1,0:T(4,128)S(1)} custom-call(bf16[64,2048]{1,0:T(8,128)(2,1)S(1)} %collective-permute-done.32.refs_0_, bf16[64,2048]{1,0:T(8,128)(2,1)S(1)} %collective-permute-done.33.refs_1_, bf16[64,2048]{1,0:T(8,128)(2,1)S(1)} %collective-permute-done.34.refs_2_, bf16[4000,2048]{1,0:T(8,128)(2,1)S(1)} %fetch.1.refs_4_.refs_1_.refs_3_), custom_call_target="tpu_custom_call" | custom-call | flops 3145728000 | bytes 786432 | tf_op jit(solution)/shard_map/peaks/pallas_call | solution.py:374
  116.3 2.5 %collective-permute-start.37 = (f32[1,64]{1,0:T(1,128)S(1)}, f32[1,64]{1,0:T(1,128)S(1)}, u32[]{:S(2)}, u32[]{:S(2)}) collective-permute-start(f32[1,64]{1,0:T(1,128)S(1)} %get-tuple-element.87), channel_id=1, source_target_pairs={{0,7},{1,6},{2,5},{3,4},{4,3},{5,2},{6,1},{7,0},{8,15},{9,14},{10,... | collective-permute-start | bytes 776 | tf_op jit(solution)/shard_map/ppermute | solution.py:413
  118.8 2.0 %collective-permute-start.36 = (f32[1,64]{1,0:T(1,128)S(1)}, f32[1,64]{1,0:T(1,128)S(1)}, u32[]{:S(2)}, u32[]{:S(2)}) collective-permute-start(f32[1,64]{1,0:T(1,128)S(1)} %get-tuple-element.88), channel_id=1, source_target_pairs={{0,6},{1,7},{2,4},{3,5},{4,2},{5,3},{6,0},{7,1},{8,13},{9,12},{10,... | collective-permute-start | bytes 776 | tf_op jit(solution)/shard_map/ppermute | solution.py:413
  122.6 1.6 %collective-permute-done.36.refs_6_ = f32[1,64]{1,0:T(1,128)S(1)} collective-permute-done((f32[1,64]{1,0:T(1,128)S(1)}, f32[1,64]{1,0:T(1,128)S(1)}, u32[]{:S(2)}, u32[]{:S(2)}) %collective-permute-start.36) | collective-permute-done | bytes 288 | tf_op jit(solution)/shard_map/ppermute | solution.py:413
  124.2 2.0 %collective-permute-done.35.refs_5_ = f32[1,64]{1,0:T(1,128)S(1)} collective-permute-done((f32[1,64]{1,0:T(1,128)S(1)}, f32[1,64]{1,0:T(1,128)S(1)}, u32[]{:S(2)}, u32[]{:S(2)}) %collective-permute-start.35) | collective-permute-done | bytes 288 | tf_op jit(solution)/shard_map/ppermute | solution.py:413
  (72 shorter events, 19.0 us)
Async XLA Ops:
  3.3 7.5 %collective-permute-start.1 = (bf16[64,2176]{1,0:T(8,128)(2,1)S(1)}, bf16[64,2176]{1,0:T(8,128)(2,1)S(1)}, u32[]{:S(2)}, u32[]{:S(2)}) collective-permute-start(bf16[64,2176]{1,0:T(8,128)(2,1)S(1)} %prepare.1.refs_0_), channel_id=1, source_target_pairs={{0,16},{1,17},{2,18},{3,19},{4,20},{5,21},{6,22},{7,23},{8,9},{9,8... | collective-permute-start | bytes 835592 | tf_op jit(solution)/shard_map/ppermute | solution.py:413
  6.3 6.7 %collective-permute-start.3 = (bf16[64,2176]{1,0:T(8,128)(2,1)S(1)}, bf16[64,2176]{1,0:T(8,128)(2,1)S(1)}, u32[]{:S(2)}, u32[]{:S(2)}) collective-permute-start(bf16[64,2176]{1,0:T(8,128)(2,1)S(1)} %prepare.1.refs_0_), channel_id=1, source_target_pairs={{0,1},{1,0},{2,3},{3,2},{4,5},{5,4},{6,7},{7,6},{8,10},{9,11},{10,... | collective-permute-start | bytes 835592 | tf_op jit(solution)/shard_map/ppermute | solution.py:413
  10.9 6.6 %collective-permute-start.5 = (bf16[64,2176]{1,0:T(8,128)(2,1)S(1)}, bf16[64,2176]{1,0:T(8,128)(2,1)S(1)}, u32[]{:S(2)}, u32[]{:S(2)}) collective-permute-start(bf16[64,2176]{1,0:T(8,128)(2,1)S(1)} %collective-permute-done.1.refs_1_), channel_id=1, source_target_pairs={{0,1},{1,0},{2,3},{3,2},{4,5},{5,4},{6,7},{7,6},{8,10},{9,11},{10,... | collective-permute-start | bytes 835592 | tf_op jit(solution)/shard_map/ppermute | solution.py:413
  12.9 6.6 %collective-permute-start.7 = (bf16[64,2176]{1,0:T(8,128)(2,1)S(1)}, bf16[64,2176]{1,0:T(8,128)(2,1)S(1)}, u32[]{:S(2)}, u32[]{:S(2)}) collective-permute-start(bf16[64,2176]{1,0:T(8,128)(2,1)S(1)} %prepare.1.refs_0_), channel_id=1, source_target_pairs={{0,8},{1,9},{2,10},{3,11},{4,12},{5,13},{6,14},{7,15},{8,0},{9,1},... | collective-permute-start | bytes 835592 | tf_op jit(solution)/shard_map/ppermute | solution.py:413
  13.0 6.6 %collective-permute-start.9 = (bf16[64,2176]{1,0:T(8,128)(2,1)S(1)}, bf16[64,2176]{1,0:T(8,128)(2,1)S(1)}, u32[]{:S(2)}, u32[]{:S(2)}) collective-permute-start(bf16[64,2176]{1,0:T(8,128)(2,1)S(1)} %collective-permute-done.3.refs_2_), channel_id=1, source_target_pairs={{0,8},{1,9},{2,10},{3,11},{4,12},{5,13},{6,14},{7,15},{8,0},{9,1},... | collective-permute-start | bytes 835592 | tf_op jit(solution)/shard_map/ppermute | solution.py:413
  13.4 8.1 %collective-permute-start.8 = (bf16[64,2176]{1,0:T(8,128)(2,1)S(1)}, bf16[64,2176]{1,0:T(8,128)(2,1)S(1)}, u32[]{:S(2)}, u32[]{:S(2)}) collective-permute-start(bf16[64,2176]{1,0:T(8,128)(2,1)S(1)} %collective-permute-done.1.refs_1_), channel_id=1, source_target_pairs={{0,8},{1,9},{2,10},{3,11},{4,12},{5,13},{6,14},{7,15},{8,0},{9,1},... | collective-permute-start | bytes 835592 | tf_op jit(solution)/shard_map/ppermute | solution.py:413
  17.4 17.8 %collective-permute-start = (bf16[64,2176]{1,0:T(8,128)(2,1)S(1)}, bf16[64,2176]{1,0:T(8,128)(2,1)S(1)}, u32[]{:S(2)}, u32[]{:S(2)}) collective-permute-start(bf16[64,2176]{1,0:T(8,128)(2,1)S(1)} %prepare.1.refs_0_), channel_id=1, source_target_pairs={{0,2},{1,3},{2,0},{3,1},{4,6},{5,7},{6,4},{7,5},{8,24},{9,25},{10,... | collective-permute-start | bytes 835592 | tf_op jit(solution)/shard_map/ppermute | solution.py:413
  19.5 15.7 %collective-permute-start.4 = (bf16[64,2176]{1,0:T(8,128)(2,1)S(1)}, bf16[64,2176]{1,0:T(8,128)(2,1)S(1)}, u32[]{:S(2)}, u32[]{:S(2)}) collective-permute-start(bf16[64,2176]{1,0:T(8,128)(2,1)S(1)} %collective-permute-done.3.refs_2_), channel_id=1, source_target_pairs={{0,2},{1,3},{2,0},{3,1},{4,6},{5,7},{6,4},{7,5},{8,24},{9,25},{10,... | collective-permute-start | bytes 835592 | tf_op jit(solution)/shard_map/ppermute | solution.py:413
  19.6 15.6 %collective-permute-start.2 = (bf16[64,2176]{1,0:T(8,128)(2,1)S(1)}, bf16[64,2176]{1,0:T(8,128)(2,1)S(1)}, u32[]{:S(2)}, u32[]{:S(2)}) collective-permute-start(bf16[64,2176]{1,0:T(8,128)(2,1)S(1)} %collective-permute-done.1.refs_1_), channel_id=1, source_target_pairs={{0,2},{1,3},{2,0},{3,1},{4,6},{5,7},{6,4},{7,5},{8,24},{9,25},{10,... | collective-permute-start | bytes 835592 | tf_op jit(solution)/shard_map/ppermute | solution.py:413
  21.6 13.7 %collective-permute-start.6 = (bf16[64,2176]{1,0:T(8,128)(2,1)S(1)}, bf16[64,2176]{1,0:T(8,128)(2,1)S(1)}, u32[]{:S(2)}, u32[]{:S(2)}) collective-permute-start(bf16[64,2176]{1,0:T(8,128)(2,1)S(1)} %collective-permute-done.5.refs_3_), channel_id=1, source_target_pairs={{0,2},{1,3},{2,0},{3,1},{4,6},{5,7},{6,4},{7,5},{8,24},{9,25},{10,... | collective-permute-start | bytes 835592 | tf_op jit(solution)/shard_map/ppermute | solution.py:413
  36.3 15.7 %collective-permute-start.11 = (bf16[256,2048]{1,0:T(8,128)(2,1)S(1)}, bf16[256,2048]{1,0:T(8,128)(2,1)S(1)}, u32[]{:S(2)}, u32[]{:S(2)}) collective-permute-start(bf16[256,2048]{1,0:T(8,128)(2,1)S(1)} %get-tuple-element.53), channel_id=1, source_target_pairs={{0,8},{1,9},{2,10},{3,11},{4,12},{5,13},{6,14},{7,15},{8,0},{9,1},... | collective-permute-start | bytes 3145736 | tf_op jit(solution)/shard_map/ppermute | solution.py:413
  52.3 6.5 %collective-permute-start.13 = (bf16[64,2048]{1,0:T(8,128)(2,1)S(1)}, bf16[64,2048]{1,0:T(8,128)(2,1)S(1)}, u32[]{:S(2)}, u32[]{:S(2)}) collective-permute-start(bf16[64,2048]{1,0:T(8,128)(2,1)S(1)} %get-tuple-element.57), channel_id=1, source_target_pairs={{0,1},{1,0},{2,3},{3,2},{4,5},{5,4},{6,7},{7,6},{8,10},{9,11},{10,... | collective-permute-start | bytes 786440 | tf_op jit(solution)/shard_map/ppermute | solution.py:413
  54.8 7.0 %collective-permute-start.20 = (bf16[64,2048]{1,0:T(8,128)(2,1)S(1)}, bf16[64,2048]{1,0:T(8,128)(2,1)S(1)}, u32[]{:S(2)}, u32[]{:S(2)}) collective-permute-start(bf16[64,2048]{1,0:T(8,128)(2,1)S(1)} %get-tuple-element.68), channel_id=1, source_target_pairs={{0,1},{1,0},{2,3},{3,2},{4,5},{5,4},{6,7},{7,6},{8,10},{9,11},{10,... | collective-permute-start | bytes 786440 | tf_op jit(solution)/shard_map/ppermute | solution.py:413
  56.8 10.4 %collective-permute-start.22 = (bf16[64,2048]{1,0:T(8,128)(2,1)S(1)}, bf16[64,2048]{1,0:T(8,128)(2,1)S(1)}, u32[]{:S(2)}, u32[]{:S(2)}) collective-permute-start(bf16[64,2048]{1,0:T(8,128)(2,1)S(1)} %get-tuple-element.70), channel_id=1, source_target_pairs={{0,1},{1,0},{2,3},{3,2},{4,5},{5,4},{6,7},{7,6},{8,10},{9,11},{10,... | collective-permute-start | bytes 786440 | tf_op jit(solution)/shard_map/ppermute | solution.py:413
  56.9 19.1 %collective-permute-start.12 = (bf16[64,2048]{1,0:T(8,128)(2,1)S(1)}, bf16[64,2048]{1,0:T(8,128)(2,1)S(1)}, u32[]{:S(2)}, u32[]{:S(2)}) collective-permute-start(bf16[64,2048]{1,0:T(8,128)(2,1)S(1)} %get-tuple-element.55), channel_id=1, source_target_pairs={{0,1},{1,0},{2,3},{3,2},{4,5},{5,4},{6,7},{7,6},{8,10},{9,11},{10,... | collective-permute-start | bytes 786440 | tf_op jit(solution)/shard_map/ppermute | solution.py:413
  58.9 17.1 %collective-permute-start.14 = (bf16[64,2048]{1,0:T(8,128)(2,1)S(1)}, bf16[64,2048]{1,0:T(8,128)(2,1)S(1)}, u32[]{:S(2)}, u32[]{:S(2)}) collective-permute-start(bf16[64,2048]{1,0:T(8,128)(2,1)S(1)} %add_blocks.6), channel_id=1, source_target_pairs={{0,16},{1,17},{2,18},{3,19},{4,20},{5,21},{6,22},{7,23},{8,9},{9,8... | collective-permute-start | bytes 786440 | tf_op jit(solution)/shard_map/ppermute | solution.py:413
  61.9 14.1 %collective-permute-start.21 = (bf16[64,2048]{1,0:T(8,128)(2,1)S(1)}, bf16[64,2048]{1,0:T(8,128)(2,1)S(1)}, u32[]{:S(2)}, u32[]{:S(2)}) collective-permute-start(bf16[64,2048]{1,0:T(8,128)(2,1)S(1)} %add_blocks.8), channel_id=1, source_target_pairs={{0,2},{1,3},{2,0},{3,1},{4,6},{5,7},{6,4},{7,5},{8,24},{9,25},{10,... | collective-permute-start | bytes 786440 | tf_op jit(solution)/shard_map/ppermute | solution.py:413
  67.2 8.8 %collective-permute-start.23 = (bf16[64,2048]{1,0:T(8,128)(2,1)S(1)}, bf16[64,2048]{1,0:T(8,128)(2,1)S(1)}, u32[]{:S(2)}, u32[]{:S(2)}) collective-permute-start(bf16[64,2048]{1,0:T(8,128)(2,1)S(1)} %add_blocks.9), channel_id=1, source_target_pairs={{0,18},{1,19},{2,16},{3,17},{4,22},{5,23},{6,20},{7,21},{8,25},{9,... | collective-permute-start | bytes 786440 | tf_op jit(solution)/shard_map/ppermute | solution.py:413
  77.6 11.1 %collective-permute-start.27 = (bf16[64,2048]{1,0:T(8,128)(2,1)S(1)}, bf16[64,2048]{1,0:T(8,128)(2,1)S(1)}, u32[]{:S(2)}, u32[]{:S(2)}) collective-permute-start(bf16[64,2048]{1,0:T(8,128)(2,1)S(1)} %get-tuple-element.80.refs_0_), channel_id=1, source_target_pairs={{0,4},{1,5},{2,6},{3,7},{4,0},{5,1},{6,2},{7,3},{8,12},{9,13},{10,... | collective-permute-start | bytes 786440 | tf_op jit(solution)/shard_map/ppermute | solution.py:413
  80.1 12.2 %collective-permute-start.26 = (bf16[64,2048]{1,0:T(8,128)(2,1)S(1)}, bf16[64,2048]{1,0:T(8,128)(2,1)S(1)}, u32[]{:S(2)}, u32[]{:S(2)}) collective-permute-start(bf16[64,2048]{1,0:T(8,128)(2,1)S(1)} %get-tuple-element.80.refs_0_), channel_id=1, source_target_pairs={{0,3},{1,2},{2,1},{3,0},{4,7},{5,6},{6,5},{7,4},{8,11},{9,10},{10,... | collective-permute-start | bytes 786440 | tf_op jit(solution)/shard_map/ppermute | solution.py:413
  81.5 12.9 %collective-permute-start.25 = (bf16[64,2048]{1,0:T(8,128)(2,1)S(1)}, bf16[64,2048]{1,0:T(8,128)(2,1)S(1)}, u32[]{:S(2)}, u32[]{:S(2)}) collective-permute-start(bf16[64,2048]{1,0:T(8,128)(2,1)S(1)} %get-tuple-element.80.refs_0_), channel_id=1, source_target_pairs={{0,2},{1,3},{2,0},{3,1},{4,6},{5,7},{6,4},{7,5},{8,9},{9,8},{10,11... | collective-permute-start | bytes 786440 | tf_op jit(solution)/shard_map/ppermute | solution.py:413
  83.1 11.4 %collective-permute-start.24 = (bf16[64,2048]{1,0:T(8,128)(2,1)S(1)}, bf16[64,2048]{1,0:T(8,128)(2,1)S(1)}, u32[]{:S(2)}, u32[]{:S(2)}) collective-permute-start(bf16[64,2048]{1,0:T(8,128)(2,1)S(1)} %get-tuple-element.80.refs_0_), channel_id=1, source_target_pairs={{0,1},{1,0},{2,3},{3,2},{4,5},{5,4},{6,7},{7,6},{8,10},{9,11},{10,... | collective-permute-start | bytes 786440 | tf_op jit(solution)/shard_map/ppermute | solution.py:413
  99.0 10.9 %collective-permute-start.34 = (bf16[64,2048]{1,0:T(8,128)(2,1)S(1)}, bf16[64,2048]{1,0:T(8,128)(2,1)S(1)}, u32[]{:S(2)}, u32[]{:S(2)}) collective-permute-start(bf16[64,2048]{1,0:T(8,128)(2,1)S(1)} %collective-permute-done.27.refs_0_), channel_id=1, source_target_pairs={{0,3},{1,2},{2,1},{3,0},{4,7},{5,6},{6,5},{7,4},{8,11},{9,10},{10,... | collective-permute-start | bytes 786440 | tf_op jit(solution)/shard_map/ppermute | solution.py:413
  100.5 11.0 %collective-permute-start.33 = (bf16[64,2048]{1,0:T(8,128)(2,1)S(1)}, bf16[64,2048]{1,0:T(8,128)(2,1)S(1)}, u32[]{:S(2)}, u32[]{:S(2)}) collective-permute-start(bf16[64,2048]{1,0:T(8,128)(2,1)S(1)} %collective-permute-done.27.refs_0_), channel_id=1, source_target_pairs={{0,2},{1,3},{2,0},{3,1},{4,6},{5,7},{6,4},{7,5},{8,9},{9,8},{10,11... | collective-permute-start | bytes 786440 | tf_op jit(solution)/shard_map/ppermute | solution.py:413
  102.0 9.8 %collective-permute-start.32 = (bf16[64,2048]{1,0:T(8,128)(2,1)S(1)}, bf16[64,2048]{1,0:T(8,128)(2,1)S(1)}, u32[]{:S(2)}, u32[]{:S(2)}) collective-permute-start(bf16[64,2048]{1,0:T(8,128)(2,1)S(1)} %collective-permute-done.27.refs_0_), channel_id=1, source_target_pairs={{0,1},{1,0},{2,3},{3,2},{4,5},{5,4},{6,7},{7,6},{8,10},{9,11},{10,... | collective-permute-start | bytes 786440 | tf_op jit(solution)/shard_map/ppermute | solution.py:413
  102.5 16.3 %collective-permute-start.30 = (f32[1,64]{1,0:T(1,128)S(1)}, f32[1,64]{1,0:T(1,128)S(1)}, u32[]{:S(2)}, u32[]{:S(2)}) collective-permute-start(f32[1,64]{1,0:T(1,128)S(1)} %get-tuple-element.90), channel_id=1, source_target_pairs={{0,3},{1,2},{2,1},{3,0},{4,7},{5,6},{6,5},{7,4},{8,11},{9,10},{10,... | collective-permute-start | bytes 776 | tf_op jit(solution)/shard_map/ppermute | solution.py:413
  104.0 16.8 %collective-permute-start.29 = (f32[1,64]{1,0:T(1,128)S(1)}, f32[1,64]{1,0:T(1,128)S(1)}, u32[]{:S(2)}, u32[]{:S(2)}) collective-permute-start(f32[1,64]{1,0:T(1,128)S(1)} %get-tuple-element.91), channel_id=1, source_target_pairs={{0,2},{1,3},{2,0},{3,1},{4,6},{5,7},{6,4},{7,5},{8,9},{9,8},{10,11... | collective-permute-start | bytes 776 | tf_op jit(solution)/shard_map/ppermute | solution.py:413
  109.9 12.0 %collective-permute-start.28 = (f32[1,64]{1,0:T(1,128)S(1)}, f32[1,64]{1,0:T(1,128)S(1)}, u32[]{:S(2)}, u32[]{:S(2)}) collective-permute-start(f32[1,64]{1,0:T(1,128)S(1)} %get-tuple-element.92), channel_id=1, source_target_pairs={{0,1},{1,0},{2,3},{3,2},{4,5},{5,4},{6,7},{7,6},{8,10},{9,11},{10,... | collective-permute-start | bytes 776 | tf_op jit(solution)/shard_map/ppermute | solution.py:413
  111.5 10.4 %collective-permute-start.31 = (f32[1,64]{1,0:T(1,128)S(1)}, f32[1,64]{1,0:T(1,128)S(1)}, u32[]{:S(2)}, u32[]{:S(2)}) collective-permute-start(f32[1,64]{1,0:T(1,128)S(1)} %peaks.4), channel_id=1, source_target_pairs={{0,4},{1,5},{2,6},{3,7},{4,0},{5,1},{6,2},{7,3},{8,12},{9,13},{10,... | collective-permute-start | bytes 776 | tf_op jit(solution)/shard_map/ppermute | solution.py:413
  116.3 6.2 %collective-permute-start.37 = (f32[1,64]{1,0:T(1,128)S(1)}, f32[1,64]{1,0:T(1,128)S(1)}, u32[]{:S(2)}, u32[]{:S(2)}) collective-permute-start(f32[1,64]{1,0:T(1,128)S(1)} %get-tuple-element.87), channel_id=1, source_target_pairs={{0,7},{1,6},{2,5},{3,4},{4,3},{5,2},{6,1},{7,0},{8,15},{9,14},{10,... | collective-permute-start | bytes 776 | tf_op jit(solution)/shard_map/ppermute | solution.py:413
  118.8 5.3 %collective-permute-start.36 = (f32[1,64]{1,0:T(1,128)S(1)}, f32[1,64]{1,0:T(1,128)S(1)}, u32[]{:S(2)}, u32[]{:S(2)}) collective-permute-start(f32[1,64]{1,0:T(1,128)S(1)} %get-tuple-element.88), channel_id=1, source_target_pairs={{0,6},{1,7},{2,4},{3,5},{4,2},{5,3},{6,0},{7,1},{8,13},{9,12},{10,... | collective-permute-start | bytes 776 | tf_op jit(solution)/shard_map/ppermute | solution.py:413
  120.8 5.3 %collective-permute-start.35 = (f32[1,64]{1,0:T(1,128)S(1)}, f32[1,64]{1,0:T(1,128)S(1)}, u32[]{:S(2)}, u32[]{:S(2)}) collective-permute-start(f32[1,64]{1,0:T(1,128)S(1)} %get-tuple-element.89), channel_id=1, source_target_pairs={{0,5},{1,4},{2,7},{3,6},{4,1},{5,0},{6,3},{7,2},{8,14},{9,15},{10,... | collective-permute-start | bytes 776 | tf_op jit(solution)/shard_map/ppermute | solution.py:413
  (12 other events, 34.5 us)

commit v3 on v2

--- a/solution.py
+++ b/solution.py
@@ -10,13 +10,15 @@
 CAP = 24
 META = 128
 CUT = 768
-HAND_ON = 0
+DOWN_CUT = 512
+SPREAD = 1024
 VMEM_LIMIT = 60 * 1024 * 1024
 
 norm_eps = 1e-05
 AXES = ("req", "exp")
 F32 = jnp.float32
 BF16 = jnp.bfloat16
+SHORT = pl.CostEstimate(flops=1, bytes_accessed=1, transcendentals=0)
 
 
 def flip_pairs(n_req, n_exp, dim_of_core):
@@ -43,13 +45,19 @@
     return out
 
 
-def prepare_kernel(tokens_ref, routes_ref, router_ref, out_ref):
-    width = tokens_ref.shape[1]
-    rows = tokens_ref.shape[0]
-    t = tokens_ref[...]
-    out_ref[:, :width] = t
+def prepare_kernel(tokens_hbm, routes_hbm, router_hbm, out_ref, routes_ref, router_ref, sems):
+    rows, width = tokens_hbm.shape
+    copies = [
+        pltpu.make_async_copy(tokens_hbm, out_ref.at[:, pl.ds(0, width)], sems.at[0]),
+        pltpu.make_async_copy(router_hbm, router_ref, sems.at[1]),
+        pltpu.make_async_copy(routes_hbm, routes_ref, sems.at[2]),
+    ]
+    for c in copies:
+        c.start()
+    for c in copies:
+        c.wait()
     logits = lax.dot_general(
-        t, router_ref[...], (((1,), (1,)), ((), ())), preferred_element_type=F32
+        out_ref[:, :width], router_ref[...], (((1,), (1,)), ((), ())), preferred_element_type=F32
     )
     gating = 1.0 / (1.0 + jnp.exp(-logits))
     routes = jnp.transpose(
@@ -69,14 +77,25 @@
     out_ref[:, width:] = meta.astype(BF16)
 
 
+def in_hbm(x):
+    return pltpu.with_memory_space_constraint(x, pltpu.HBM)
+
+
 def prepare(tokens, routes, router):
     rows, width = tokens.shape
     return pl.pallas_call(
         prepare_kernel,
+        in_specs=[pl.BlockSpec(memory_space=pl.ANY)] * 3,
+        out_specs=pl.BlockSpec(memory_space=pltpu.VMEM),
         out_shape=jax.ShapeDtypeStruct((rows, width + META), BF16),
+        scratch_shapes=[
+            pltpu.VMEM(routes.shape[::-1], jnp.int32),
+            pltpu.VMEM(router.shape[::-1], BF16),
+            pltpu.SemaphoreType.DMA((3,)),
+        ],
         compiler_params=params(8 * 1024 * 1024),
         name="prepare",
-    )(tokens, routes.T, router.T)
+    )(in_hbm(tokens), in_hbm(routes.T), in_hbm(router.T))
 
 
 def near_core(x):
@@ -114,48 +133,36 @@
         out_shape=pltpu.VMEM(x.shape, x.dtype),
         scratch_shapes=[pltpu.SemaphoreType.DMA((parts,))],
         compiler_params=params(1024 * 1024),
-        cost_estimate=pl.CostEstimate(flops=0, bytes_accessed=size, transcendentals=0),
+        cost_estimate=SHORT,
         name="fetch",
     )(pltpu.with_memory_space_constraint(x, pltpu.HBM), after)
 
 
-def pieces(size, want):
-    return size // want if size % want == 0 else 1
-
-
 def spans(size, want):
     return [(at, min(want, size - at)) for at in range(0, size, want)]
 
 
-def expert_kernel(blocks, slots, held, hand_on, expert_ref, *refs):
+def expert_kernel(blocks, slots, expert_ref, *refs):
     half = blocks // 2
     block_refs, refs = refs[:blocks], refs[blocks:]
     weight_refs, refs = refs[:3], refs[3:]
     own_refs, other_ref, refs = refs[:half], refs[half], refs[half + 1 :]
-    kept, refs = refs[:hand_on], refs[hand_on:]
-    table, hidden, weighted, refs = refs[0], refs[1], refs[2], refs[3:]
-    loaded, sems = list(kept) + list(refs[:-1]), refs[-1]
+    table, hidden, weighted, *weights, sems = refs
     rows = block_refs[0].shape[0]
     width, units = weight_refs[0].shape
     count = blocks * rows
-    weights = list(weight_refs[:held]) + loaded
-    cuts = [spans(units, CUT), spans(units, CUT), spans(width, CUT)]
+    cuts = [spans(units, CUT), spans(units, CUT), spans(width, DOWN_CUT)]
     waits = [[] for _ in range(3)]
 
     def load(w, j):
-        if w >= held:
-            at, size = cuts[w][j]
-            c = pltpu.make_async_copy(
-                weight_refs[w].at[:, pl.ds(at, size)],
-                weights[w].at[:, pl.ds(at, size)],
-                sems.at[w, j],
-            )
-            c.start()
-            waits[w].append(c)
-
-    def arrive(w, j):
-        if w >= held:
-            waits[w][j].wait()
+        at, size = cuts[w][j]
+        c = pltpu.make_async_copy(
+            weight_refs[w].at[:, pl.ds(at, size)],
+            weights[w].at[:, pl.ds(at, size)],
+            sems.at[w, j],
+        )
+        c.start()
+        waits[w].append(c)
 
     for j in range(len(cuts[0])):
         load(0, j)
@@ -191,66 +198,58 @@
     x = jnp.dot(place, table[:, :width], preferred_element_type=F32).astype(BF16)
     back = jnp.transpose(place)
     for j, (start, size) in enumerate(cuts[0]):
-        arrive(0, j)
-        arrive(1, j)
+        waits[0][j].wait()
+        waits[1][j].wait()
         for at, some in spans(size, 256):
             at = slice(start + at, start + at + some)
             g = jnp.dot(x, weights[0][:, at], preferred_element_type=F32)
             u = jnp.dot(x, weights[1][:, at], preferred_element_type=F32)
             hidden[:, at] = (g / (1.0 + jnp.exp(-g)) * u).astype(BF16)
+    ready = 0
     for j, (start, size) in enumerate(cuts[2]):
-        arrive(2, j)
+        waits[2][j].wait()
         for at, some in spans(size, 256):
             at = slice(start + at, start + at + some)
             y = jnp.dot(hidden[...], weights[2][:, at], preferred_element_type=F32)
             weighted[:, at] = (y * scale).astype(BF16)
-    for start, size in spans(width, 1024):
-        at = slice(start, start + size)
+        end = start + size
+        if end - ready < SPREAD and end < width:
+            continue
+        at = slice(ready, end)
         spread = jnp.dot(back, weighted[:, at], preferred_element_type=F32).astype(BF16)
         for i, ref in enumerate(own_refs):
             ref[:, at] = spread[i * rows : (i + 1) * rows]
         other_ref[:, at] = spread[half * rows :]
-
-
-def run_expert(expert, block_list, weights, cap, held, hand_on):
+        ready = end
+
+
+def run_expert(expert, block_list, weights, cap):
     blocks = len(block_list)
     rows = block_list[0].shape[0]
     width, units = weights[0].shape
     slots = blocks * cap
     count = blocks * rows
     half = blocks // 2
-    loads = [pltpu.VMEM(w.shape, BF16) for w in weights]
-    cuts = len(spans(max(units, width), CUT))
-    scoped = sum(2 * width * units for _ in weights[max(held, hand_on) :])
-    return pl.pallas_call(
-        functools.partial(expert_kernel, blocks, slots, held, hand_on),
+    cuts = max(len(spans(units, CUT)), len(spans(width, DOWN_CUT)))
+    return pl.pallas_call(
+        functools.partial(expert_kernel, blocks, slots),
         in_specs=[pl.BlockSpec(memory_space=pltpu.SMEM)]
-        + [LOCAL] * (blocks + held)
-        + [pl.BlockSpec(memory_space=pl.ANY)] * (3 - held),
-        out_specs=[LOCAL] * (half + 1 + hand_on),
+        + [LOCAL] * blocks
+        + [pl.BlockSpec(memory_space=pl.ANY)] * 3,
+        out_specs=[LOCAL] * (half + 1),
         out_shape=[jax.ShapeDtypeStruct((rows, width), BF16)] * half
-        + [jax.ShapeDtypeStruct((half * rows, width), BF16)]
-        + loads[:hand_on],
+        + [jax.ShapeDtypeStruct((half * rows, width), BF16)],
         scratch_shapes=[
             pltpu.VMEM((count, width + META), BF16),
             pltpu.VMEM((slots, units), BF16),
             pltpu.VMEM((slots, width), BF16),
-            *loads[max(held, hand_on) :],
+            *(pltpu.VMEM(w.shape, BF16) for w in weights),
             pltpu.SemaphoreType.DMA((3, cuts)),
         ],
-        compiler_params=params(scoped + 10 * count * (width + META)),
-        cost_estimate=pl.CostEstimate(
-            flops=10 * slots * width * units + 4 * slots * count * width,
-            bytes_accessed=6 * width * units,
-            transcendentals=slots * units,
-        ),
+        compiler_params=params(6 * width * units + 10 * count * (width + META)),
+        cost_estimate=SHORT,
         name="expert",
-    )(
-        expert,
-        *map(near_core, block_list),
-        *map(near_core, weights[:held]),
-        *(pltpu.with_memory_space_constraint(w, pltpu.HBM) for w in weights[held:]),
-    )
+    )(expert, *map(near_core, block_list), *map(in_hbm, weights))
 
 
 def add_kernel(count, rows, *refs):
@@ -269,9 +268,7 @@
         out_specs=[LOCAL] * count,
         out_shape=[jax.ShapeDtypeStruct((rows, width), BF16)] * count,
         compiler_params=params(12 * count * rows * width),
-        cost_estimate=pl.CostEstimate(
-            flops=count * rows * width, bytes_accessed=6 * count * rows * width, transcendentals=0
-        ),
+        cost_estimate=SHORT,
         name="add_blocks",
     )(*own, *other)
 
@@ -378,11 +375,7 @@
         out_shape=jax.ShapeDtypeStruct((blocks, rows), F32),
         scratch_shapes=[pltpu.VMEM((blocks * rows, width), BF16)],
         compiler_params=params(12 * 1024 * 1024),
-        cost_estimate=pl.CostEstimate(
-            flops=2 * blocks * rows * width * words,
-            bytes_accessed=2 * blocks * rows * width,
-            transcendentals=0,
-        ),
+        cost_estimate=SHORT,
         name="peaks",
     )(*map(near_core, block_list), near_core(words_first))
 
@@ -429,16 +422,12 @@
     near += [send(b, core) for b in near]
     cap = CAP * block.shape[0] // row_count
     rows = block.shape[0]
-    blocks = len(near)
 
     weights = [gate_weight, up_weight, down_weight]
-    out = run_expert(expert, near, weights, cap, 0, HAND_ON)
-    half = blocks // 2
-    near_out, near_other, weights[:HAND_ON] = out[:half], out[half], out[half + 1 :]
+    *near_out, near_other = run_expert(expert, near, weights, cap)
     far, near_out = lax.optimization_barrier((far, near_out))
     far += [send(b, core) for b in far]
-    out = run_expert(expert, far, weights, cap, HAND_ON, 0)
-    far_out, far_other = out[:half], out[half]
+    *far_out, far_other = run_expert(expert, far, weights, cap)
     near_sum = add_blocks(near_out, [send(near_other, core)])
     n3 = hop(near_sum[3], 1)
     n2 = hop(near_sum[2], 1)
@@ -457,27 +446,48 @@
     parts, words_first = lax.optimization_barrier((parts, words_first))
     hidden_out, normed, request_norm = finish(lengths, tokens, norm_gain.reshape(1, width), parts)
 
-    near_dims = [("exp", b) for b in bits_below(half_exp)]
-    near_turn = near_dims[1:] + near_dims[:1]
+    exp_dims = [("exp", b) for b in bits_below(half_exp)]
     across = ("exp", half_exp)
-    ways = [([], [])]
-    for p, q in zip(near_dims, near_turn):
-        ways += [(a + [p], b + [q]) for a, b in ways]
-    far_first = send(normed, [across])
-    near_blocks = [normed] + [send(normed, *w) for w in ways[1:]]
-    far_blocks = [far_first] + [send(far_first, *w) for w in ways[1:]]
-    near_blocks, far_first = lax.optimization_barrier((near_blocks, far_first))
-    near_peak = peaks(near_blocks, words_first)
-    far_first, near_peak = lax.optimization_barrier((far_first, near_peak))
-    first_peak = peaks([far_first], words_first)
-    far_peak = peaks(far_blocks[1:], words_first)
-    found = [near_peak[0:1]]
-    found += [send(near_peak[i : i + 1], *w) for i, w in enumerate(ways) if i > 0]
-    found += [send(first_peak, [across])]
-    found += [
-        send(far_peak[i : i + 1], p + [across], q + [across])
-        for i, (p, q) in enumerate(ways[1:])
-    ]
+
+    def tree(dims0, dims1):
+        ways = [([], [])]
+        for p, q in zip(dims0, dims1):
+            ways += [(a + [p], b + [q]) for a, b in ways]
+        return ways
+
+    def peak_back(group):
+        peak = peaks([held[k] for k in group], words_first)
+        out = []
+        for n, (side, i) in enumerate(group):
+            p, q = trees[side][i]
+            one = peak[n : n + 1]
+            if side:
+                one = send(one, p + [across], q + [across])
+            elif p:
+                one = send(one, p, q)
+            out.append(one)
+        return out, peak
+
+    trees = tree(exp_dims[::-1], exp_dims[::-1]), tree(exp_dims, exp_dims[1:] + exp_dims[:1])
+    singles = [i for i, (p, _) in enumerate(trees[0]) if len(p) == 1]
+    first = send(normed, [across])
+    first, *near_singles = lax.optimization_barrier(
+        (first, *(send(normed, *trees[0][i]) for i in singles))
+    )
+    held = {(0, 0): normed, (1, 0): first}
+    for i, x in zip(singles, near_singles):
+        held[0, i] = x
+        held[1, i] = send(first, *trees[1][i])
+    early = sorted(k for k in held if k == (1, 0) or k[0] == 0)
+    found, peak = peak_back(early)
+    for i in singles:
+        held[1, i], peak = lax.optimization_barrier((held[1, i], peak))
+    for side in (1, 0):
+        for i, (p, q) in enumerate(trees[side]):
+            if len(p) > 1:
+                before = trees[side].index((p[:-1], q[:-1]))
+                held[side, i] = send(held[side, before], p[-1:], q[-1:])
+    found += peak_back(sorted(k for k in held if k not in early))[0]
     request_max = request_peaks(lengths, found)
     return (hidden_out, request_norm[0], request_max[0])
 

time: 128 us -> 119 us (0.930)
  waiting for transfers between devices: 29.3 us -> 23.4 us
  Pallas kernels: 50.1 us -> 45.9 us
  starting transfers between devices: 44.6 us -> 48.8 us
  local copies, waits for them, and re-layouts: 2.4 us -> 0.02 us
    ppermute x38, waiting for transfers between devices: 29.3 us -> 23.4 us  [send(): return lax.ppermute(x, AXES, pairs)]
    pallas_call x3 -> x2, Pallas kernels: 13.4 us -> 9.02 us  [peaks(): pl.pallas_call(functools.partial(peak_kernel, blocks), in_specs=[LOCAL] *...]
    ppermute x38, starting transfers between devices: 44.6 us -> 48.8 us  [send(): return lax.ppermute(x, AXES, pairs)]
    unnamed x12 -> x6, local copies, waits for them, and re-layouts: 2.39 us -> 0.01 us
  transfers between devices with their start and end apart: 38 -> 38, of which waited for: 17 -> 15; matrix products, arithmetic and copies ran while one was open for 0% -> 0% of each run, Pallas kernels for 34% -> 35%
where the time goes in v3:
time: 119 us
  starting transfers between devices  48.8 us (41%)
  Pallas kernels  45.9 us (39%)
  waiting for transfers between devices  23.4 us (20%)
    ppermute x38, starting transfers between devices, send(): return lax.ppermute(x, AXES, pairs)  48.8 us
    pallas_call x2, Pallas kernels, run_expert(): pl.pallas_call(functools.partial(expert_kernel, blocks, slots), in_specs=...  26.5 us
    ppermute x38, waiting for transfers between devices, send(): return lax.ppermute(x, AXES, pairs)  23.4 us
    pallas_call x2, Pallas kernels, peaks(): pl.pallas_call(functools.partial(peak_kernel, blocks), in_specs=[LOCAL] *...  9.02 us
    pallas_call x1, Pallas kernels, fetch(): pl.pallas_call(functools.partial(fetch_kernel, parts), in_specs=[pl.Block...  5.8 us
  transfers between devices with their start and end apart: 38, of which 15 were waited for; matrix products, arithmetic and copies ran while one was open for 0% of the time, Pallas kernels for 35%

profile of v3, /device:TPU:0, one launch (start us, length us, event | category | flops | bytes accessed | tf_op | source)
XLA Modules:
  0.0 118.9 jit_solution(8393217570466186675)
XLA Ops:
  0.6 1.3 %prepare.1.refs_0_ = bf16[64,2176]{1,0:T(8,128)(2,1)S(1)} custom-call(bf16[64,2048]{1,0:T(8,128)(2,1)} %tokens_ref.1, s32[2,64]{1,0:T(2,128)} %bitcast.10, bf16[8,2048]{1,0:T(8,128)(2,1)} %bitcast.9), custom_call_target="tpu_custom_call" | custom-call | tf_op jit(solution)/shard_map/prepare/pallas_call | solution.py:86
  1.9 3.0 %collective-permute-start.1 = (bf16[64,2176]{1,0:T(8,128)(2,1)S(1)}, bf16[64,2176]{1,0:T(8,128)(2,1)S(1)}, u32[]{:S(2)}, u32[]{:S(2)}) collective-permute-start(bf16[64,2176]{1,0:T(8,128)(2,1)S(1)} %prepare.1.refs_0_), channel_id=1, source_target_pairs={{0,16},{1,17},{2,18},{3,19},{4,20},{5,21},{6,22},{7,23},{8,9},{9,8... | collective-permute-start | bytes 835592 | tf_op jit(solution)/shard_map/ppermute | solution.py:406
  4.9 1.5 %collective-permute-start.3 = (bf16[64,2176]{1,0:T(8,128)(2,1)S(1)}, bf16[64,2176]{1,0:T(8,128)(2,1)S(1)}, u32[]{:S(2)}, u32[]{:S(2)}) collective-permute-start(bf16[64,2176]{1,0:T(8,128)(2,1)S(1)} %prepare.1.refs_0_), channel_id=1, source_target_pairs={{0,1},{1,0},{2,3},{3,2},{4,5},{5,4},{6,7},{7,6},{8,10},{9,11},{10,... | collective-permute-start | bytes 835592 | tf_op jit(solution)/shard_map/ppermute | solution.py:406
  6.4 3.0 %collective-permute-done.1.refs_1_ = bf16[64,2176]{1,0:T(8,128)(2,1)S(1)} collective-permute-done((bf16[64,2176]{1,0:T(8,128)(2,1)S(1)}, bf16[64,2176]{1,0:T(8,128)(2,1)S(1)}, u32[]{:S(2)}, u32[]{:S(2)}) %collective-permute-start.1) | collective-permute-done | bytes 278560 | tf_op jit(solution)/shard_map/ppermute | solution.py:406
  9.5 2.0 %collective-permute-start.5 = (bf16[64,2176]{1,0:T(8,128)(2,1)S(1)}, bf16[64,2176]{1,0:T(8,128)(2,1)S(1)}, u32[]{:S(2)}, u32[]{:S(2)}) collective-permute-start(bf16[64,2176]{1,0:T(8,128)(2,1)S(1)} %collective-permute-done.1.refs_1_), channel_id=1, source_target_pairs={{0,1},{1,0},{2,3},{3,2},{4,5},{5,4},{6,7},{7,6},{8,10},{9,11},{10,... | collective-permute-start | bytes 835592 | tf_op jit(solution)/shard_map/ppermute | solution.py:406
  12.1 3.9 %collective-permute-done.5.refs_3_ = bf16[64,2176]{1,0:T(8,128)(2,1)S(1)} collective-permute-done((bf16[64,2176]{1,0:T(8,128)(2,1)S(1)}, bf16[64,2176]{1,0:T(8,128)(2,1)S(1)}, u32[]{:S(2)}, u32[]{:S(2)}) %collective-permute-start.5) | collective-permute-done | bytes 278560 | tf_op jit(solution)/shard_map/ppermute | solution.py:406
  16.0 2.1 %collective-permute-start = (bf16[64,2176]{1,0:T(8,128)(2,1)S(1)}, bf16[64,2176]{1,0:T(8,128)(2,1)S(1)}, u32[]{:S(2)}, u32[]{:S(2)}) collective-permute-start(bf16[64,2176]{1,0:T(8,128)(2,1)S(1)} %prepare.1.refs_0_), channel_id=1, source_target_pairs={{0,2},{1,3},{2,0},{3,1},{4,6},{5,7},{6,4},{7,5},{8,24},{9,25},{10,... | collective-permute-start | bytes 835592 | tf_op jit(solution)/shard_map/ppermute | solution.py:406
  18.2 2.0 %collective-permute-start.2 = (bf16[64,2176]{1,0:T(8,128)(2,1)S(1)}, bf16[64,2176]{1,0:T(8,128)(2,1)S(1)}, u32[]{:S(2)}, u32[]{:S(2)}) collective-permute-start(bf16[64,2176]{1,0:T(8,128)(2,1)S(1)} %collective-permute-done.1.refs_1_), channel_id=1, source_target_pairs={{0,2},{1,3},{2,0},{3,1},{4,6},{5,7},{6,4},{7,5},{8,24},{9,25},{10,... | collective-permute-start | bytes 835592 | tf_op jit(solution)/shard_map/ppermute | solution.py:406
  20.2 13.1 %expert.2 = (bf16[64,2048]{1,0:T(8,128)(2,1)S(1)}, bf16[64,2048]{1,0:T(8,128)(2,1)S(1)}, bf16[64,2048]{1,0:T(8,128)(2,1)S(1)}, bf16[64,2048]{1,0:T(8,128)(2,1)S(1)}, bf16[256,2048]{1,0:T(8,128)(2,1)S(1)}) custom-call(s32[1]{0:T(128)} %bitcast.3.expert_ref, bf16[64,2176]{1,0:T(8,128)(2,1)S(1)} %prepare.1.refs_0_, ...), custom_call_target="tpu_custom_call" | custom-call | flops 1 | bytes 1 | tf_op jit(solution)/shard_map/expert/pallas_call | solution.py:234
  36.2 13.3 %expert.3 = (bf16[64,2048]{1,0:T(8,128)(2,1)S(1)}, bf16[64,2048]{1,0:T(8,128)(2,1)S(1)}, bf16[64,2048]{1,0:T(8,128)(2,1)S(1)}, bf16[64,2048]{1,0:T(8,128)(2,1)S(1)}, bf16[256,2048]{1,0:T(8,128)(2,1)S(1)}) custom-call(s32[1]{0:T(128)} %bitcast.3.expert_ref, bf16[64,2176]{1,0:T(8,128)(2,1)S(1)} %collective-permute-done.refs_0_, ...), custom_call_target="tpu_custom_call" | custom-call | flops 1 | bytes 1 | tf_op jit(solution)/shard_map/expert/pallas_call | solution.py:234
  50.0 2.0 %collective-permute-start.13 = (bf16[64,2048]{1,0:T(8,128)(2,1)S(1)}, bf16[64,2048]{1,0:T(8,128)(2,1)S(1)}, u32[]{:S(2)}, u32[]{:S(2)}) collective-permute-start(bf16[64,2048]{1,0:T(8,128)(2,1)S(1)} %get-tuple-element.54), channel_id=1, source_target_pairs={{0,1},{1,0},{2,3},{3,2},{4,5},{5,4},{6,7},{7,6},{8,10},{9,11},{10,... | collective-permute-start | bytes 786440 | tf_op jit(solution)/shard_map/ppermute | solution.py:406
  52.6 2.0 %collective-permute-start.20 = (bf16[64,2048]{1,0:T(8,128)(2,1)S(1)}, bf16[64,2048]{1,0:T(8,128)(2,1)S(1)}, u32[]{:S(2)}, u32[]{:S(2)}) collective-permute-start(bf16[64,2048]{1,0:T(8,128)(2,1)S(1)} %get-tuple-element.65), channel_id=1, source_target_pairs={{0,1},{1,0},{2,3},{3,2},{4,5},{5,4},{6,7},{7,6},{8,10},{9,11},{10,... | collective-permute-start | bytes 786440 | tf_op jit(solution)/shard_map/ppermute | solution.py:406
  54.6 1.9 %collective-permute-start.12 = (bf16[64,2048]{1,0:T(8,128)(2,1)S(1)}, bf16[64,2048]{1,0:T(8,128)(2,1)S(1)}, u32[]{:S(2)}, u32[]{:S(2)}) collective-permute-start(bf16[64,2048]{1,0:T(8,128)(2,1)S(1)} %get-tuple-element.52), channel_id=1, source_target_pairs={{0,1},{1,0},{2,3},{3,2},{4,5},{5,4},{6,7},{7,6},{8,10},{9,11},{10,... | collective-permute-start | bytes 786440 | tf_op jit(solution)/shard_map/ppermute | solution.py:406
  56.6 1.8 %collective-permute-start.14 = (bf16[64,2048]{1,0:T(8,128)(2,1)S(1)}, bf16[64,2048]{1,0:T(8,128)(2,1)S(1)}, u32[]{:S(2)}, u32[]{:S(2)}) collective-permute-start(bf16[64,2048]{1,0:T(8,128)(2,1)S(1)} %add_blocks.6), channel_id=1, source_target_pairs={{0,16},{1,17},{2,18},{3,19},{4,20},{5,21},{6,22},{7,23},{8,9},{9,8... | collective-permute-start | bytes 786440 | tf_op jit(solution)/shard_map/ppermute | solution.py:406
  59.6 2.2 %collective-permute-start.21 = (bf16[64,2048]{1,0:T(8,128)(2,1)S(1)}, bf16[64,2048]{1,0:T(8,128)(2,1)S(1)}, u32[]{:S(2)}, u32[]{:S(2)}) collective-permute-start(bf16[64,2048]{1,0:T(8,128)(2,1)S(1)} %add_blocks.8), channel_id=1, source_target_pairs={{0,2},{1,3},{2,0},{3,1},{4,6},{5,7},{6,4},{7,5},{8,24},{9,25},{10,... | collective-permute-start | bytes 786440 | tf_op jit(solution)/shard_map/ppermute | solution.py:406
  61.9 3.0 %collective-permute-done.22.refs_1_ = bf16[64,2048]{1,0:T(8,128)(2,1)S(1)} collective-permute-done((bf16[64,2048]{1,0:T(8,128)(2,1)S(1)}, bf16[64,2048]{1,0:T(8,128)(2,1)S(1)}, u32[]{:S(2)}, u32[]{:S(2)}) %collective-permute-start.22) | collective-permute-done | bytes 262176 | tf_op jit(solution)/shard_map/ppermute | solution.py:406
  65.0 3.0 %collective-permute-start.23 = (bf16[64,2048]{1,0:T(8,128)(2,1)S(1)}, bf16[64,2048]{1,0:T(8,128)(2,1)S(1)}, u32[]{:S(2)}, u32[]{:S(2)}) collective-permute-start(bf16[64,2048]{1,0:T(8,128)(2,1)S(1)} %add_blocks.9), channel_id=1, source_target_pairs={{0,18},{1,19},{2,16},{3,17},{4,22},{5,23},{6,20},{7,21},{8,25},{9,... | collective-permute-start | bytes 786440 | tf_op jit(solution)/shard_map/ppermute | solution.py:406
  67.9 5.8 %fetch.1.refs_4_ = bf16[4000,2048]{1,0:T(8,128)(2,1)S(1)} custom-call(bf16[4000,2048]{1,0:T(8,128)(2,1)} %bitcast.8, bf16[256,2048]{1,0:T(8,128)(2,1)S(1)} %get-tuple-element.63.after_ref), custom_call_target="tpu_custom_call" | custom-call | flops 1 | bytes 1 | tf_op jit(solution)/shard_map/fetch/pallas_call | solution.py:129
  73.8 1.5 %finish.1 = (bf16[64,2048]{1,0:T(8,128)(2,1)}, bf16[64,2048]{1,0:T(8,128)(2,1)S(1)}, f32[1,4]{1,0:T(1,128)}) custom-call(s32[1,4]{1,0:T(1,128)S(1)} %copy-done.2, bf16[64,2048]{1,0:T(8,128)(2,1)S(1)} %copy-done, f32[1,2048]{1,0:T(1,128)S(1)} %bitcast.7, bf16[64,2048]{1,0:T(8,128)(2,1)S(1)} %get-tuple-element.68.refs_0_, ...), custom_call_target="tpu_custom_call" | custom-call | tf_op jit(solution)/shard_map/finish/pallas_call | solution.py:303
  75.3 1.5 %collective-permute-start.26 = (bf16[64,2048]{1,0:T(8,128)(2,1)S(1)}, bf16[64,2048]{1,0:T(8,128)(2,1)S(1)}, u32[]{:S(2)}, u32[]{:S(2)}) collective-permute-start(bf16[64,2048]{1,0:T(8,128)(2,1)S(1)} %get-tuple-element.75.refs_0_), channel_id=1, source_target_pairs={{0,1},{1,0},{2,3},{3,2},{4,5},{5,4},{6,7},{7,6},{8,9},{9,8},{10,11... | collective-permute-start | bytes 786440 | tf_op jit(solution)/shard_map/ppermute | solution.py:406
  77.3 2.6 %collective-permute-start.24 = (bf16[64,2048]{1,0:T(8,128)(2,1)S(1)}, bf16[64,2048]{1,0:T(8,128)(2,1)S(1)}, u32[]{:S(2)}, u32[]{:S(2)}) collective-permute-start(bf16[64,2048]{1,0:T(8,128)(2,1)S(1)} %get-tuple-element.75.refs_0_), channel_id=1, source_target_pairs={{0,4},{1,5},{2,6},{3,7},{4,0},{5,1},{6,2},{7,3},{8,12},{9,13},{10,... | collective-permute-start | bytes 786440 | tf_op jit(solution)/shard_map/ppermute | solution.py:406
  79.8 1.8 %collective-permute-done.26.refs_2_ = bf16[64,2048]{1,0:T(8,128)(2,1)S(1)} collective-permute-done((bf16[64,2048]{1,0:T(8,128)(2,1)S(1)}, bf16[64,2048]{1,0:T(8,128)(2,1)S(1)}, u32[]{:S(2)}, u32[]{:S(2)}) %collective-permute-start.26) | collective-permute-done | bytes 262176 | tf_op jit(solution)/shard_map/ppermute | solution.py:406
  81.7 5.2 %collective-permute-done.25.refs_1_ = bf16[64,2048]{1,0:T(8,128)(2,1)S(1)} collective-permute-done((bf16[64,2048]{1,0:T(8,128)(2,1)S(1)}, bf16[64,2048]{1,0:T(8,128)(2,1)S(1)}, u32[]{:S(2)}, u32[]{:S(2)}) %collective-permute-start.25) | collective-permute-done | bytes 262176 | tf_op jit(solution)/shard_map/ppermute | solution.py:406
  86.9 1.3 %collective-permute-start.31 = (bf16[64,2048]{1,0:T(8,128)(2,1)S(1)}, bf16[64,2048]{1,0:T(8,128)(2,1)S(1)}, u32[]{:S(2)}, u32[]{:S(2)}) collective-permute-start(bf16[64,2048]{1,0:T(8,128)(2,1)S(1)} %collective-permute-done.24.refs_3_), channel_id=1, source_target_pairs={{0,1},{1,0},{2,3},{3,2},{4,5},{5,4},{6,7},{7,6},{8,10},{9,11},{10,... | collective-permute-start | bytes 786440 | tf_op jit(solution)/shard_map/ppermute | solution.py:406
  88.2 3.3 %collective-permute-start.32 = (bf16[64,2048]{1,0:T(8,128)(2,1)S(1)}, bf16[64,2048]{1,0:T(8,128)(2,1)S(1)}, u32[]{:S(2)}, u32[]{:S(2)}) collective-permute-start(bf16[64,2048]{1,0:T(8,128)(2,1)S(1)} %collective-permute-done.24.refs_3_), channel_id=1, source_target_pairs={{0,2},{1,3},{2,0},{3,1},{4,6},{5,7},{6,4},{7,5},{8,9},{9,8},{10,11... | collective-permute-start | bytes 786440 | tf_op jit(solution)/shard_map/ppermute | solution.py:406
  91.4 1.5 %collective-permute-start.30 = (bf16[64,2048]{1,0:T(8,128)(2,1)S(1)}, bf16[64,2048]{1,0:T(8,128)(2,1)S(1)}, u32[]{:S(2)}, u32[]{:S(2)}) collective-permute-start(bf16[64,2048]{1,0:T(8,128)(2,1)S(1)} %collective-permute-done.25.refs_1_), channel_id=1, source_target_pairs={{0,1},{1,0},{2,3},{3,2},{4,5},{5,4},{6,7},{7,6},{8,9},{9,8},{10,11... | collective-permute-start | bytes 786440 | tf_op jit(solution)/shard_map/ppermute | solution.py:406
  92.9 4.5 %peaks.2 = f32[4,64]{1,0:T(4,128)S(1)} custom-call(bf16[64,2048]{1,0:T(8,128)(2,1)S(1)} %get-tuple-element.75.refs_0_, bf16[64,2048]{1,0:T(8,128)(2,1)S(1)} %collective-permute-done.25.refs_1_, bf16[64,2048]{1,0:T(8,128)(2,1)S(1)} %collective-permute-done.26.refs_2_, bf16[64,2048]{1,0:T(8,128)(2,1)S(1)} %collective-permute-done.24.refs_3_, ...), custom_call_target="tpu_custom_call" | custom-call | flops 1 | bytes 1 | tf_op jit(solution)/shard_map/peaks/pallas_call | solution.py:371
  98.5 1.6 %collective-permute-start.29 = (f32[1,64]{1,0:T(1,128)S(1)}, f32[1,64]{1,0:T(1,128)S(1)}, u32[]{:S(2)}, u32[]{:S(2)}) collective-permute-start(f32[1,64]{1,0:T(1,128)S(1)} %get-tuple-element.85), channel_id=1, source_target_pairs={{0,4},{1,5},{2,6},{3,7},{4,0},{5,1},{6,2},{7,3},{8,12},{9,13},{10,... | collective-permute-start | bytes 776 | tf_op jit(solution)/shard_map/ppermute | solution.py:406
  102.2 1.7 %collective-permute-done.33.refs_3_ = bf16[64,2048]{1,0:T(8,128)(2,1)S(1)} collective-permute-done((bf16[64,2048]{1,0:T(8,128)(2,1)S(1)}, bf16[64,2048]{1,0:T(8,128)(2,1)S(1)}, u32[]{:S(2)}, u32[]{:S(2)}) %collective-permute-start.33) | collective-permute-done | bytes 262176 | tf_op jit(solution)/shard_map/ppermute | solution.py:406
  103.8 4.5 %peaks.3 = f32[4,64]{1,0:T(4,128)S(1)} custom-call(bf16[64,2048]{1,0:T(8,128)(2,1)S(1)} %collective-permute-done.30.refs_0_, bf16[64,2048]{1,0:T(8,128)(2,1)S(1)} %collective-permute-done.31.refs_1_, bf16[64,2048]{1,0:T(8,128)(2,1)S(1)} %collective-permute-done.32.refs_2_, bf16[64,2048]{1,0:T(8,128)(2,1)S(1)} %collective-permute-done.33.refs_3_, ...), custom_call_target="tpu_custom_call" | custom-call | flops 1 | bytes 1 | tf_op jit(solution)/shard_map/peaks/pallas_call | solution.py:371
  108.4 2.6 %collective-permute-start.37 = (f32[1,64]{1,0:T(1,128)S(1)}, f32[1,64]{1,0:T(1,128)S(1)}, u32[]{:S(2)}, u32[]{:S(2)}) collective-permute-start(f32[1,64]{1,0:T(1,128)S(1)} %get-tuple-element.81), channel_id=1, source_target_pairs={{0,7},{1,6},{2,5},{3,4},{4,3},{5,2},{6,1},{7,0},{8,15},{9,14},{10,... | collective-permute-start | bytes 776 | tf_op jit(solution)/shard_map/ppermute | solution.py:406
  113.0 3.2 %collective-permute-start.34 = (f32[1,64]{1,0:T(1,128)S(1)}, f32[1,64]{1,0:T(1,128)S(1)}, u32[]{:S(2)}, u32[]{:S(2)}) collective-permute-start(f32[1,64]{1,0:T(1,128)S(1)} %get-tuple-element.84), channel_id=1, source_target_pairs={{0,3},{1,2},{2,1},{3,0},{4,7},{5,6},{6,5},{7,4},{8,11},{9,10},{10,... | collective-permute-start | bytes 776 | tf_op jit(solution)/shard_map/ppermute | solution.py:406
  (65 shorter events, 14.3 us)
Async XLA Ops:
  1.9 7.5 %collective-permute-start.1 = (bf16[64,2176]{1,0:T(8,128)(2,1)S(1)}, bf16[64,2176]{1,0:T(8,128)(2,1)S(1)}, u32[]{:S(2)}, u32[]{:S(2)}) collective-permute-start(bf16[64,2176]{1,0:T(8,128)(2,1)S(1)} %prepare.1.refs_0_), channel_id=1, source_target_pairs={{0,16},{1,17},{2,18},{3,19},{4,20},{5,21},{6,22},{7,23},{8,9},{9,8... | collective-permute-start | bytes 835592 | tf_op jit(solution)/shard_map/ppermute | solution.py:406
  4.9 6.7 %collective-permute-start.3 = (bf16[64,2176]{1,0:T(8,128)(2,1)S(1)}, bf16[64,2176]{1,0:T(8,128)(2,1)S(1)}, u32[]{:S(2)}, u32[]{:S(2)}) collective-permute-start(bf16[64,2176]{1,0:T(8,128)(2,1)S(1)} %prepare.1.refs_0_), channel_id=1, source_target_pairs={{0,1},{1,0},{2,3},{3,2},{4,5},{5,4},{6,7},{7,6},{8,10},{9,11},{10,... | collective-permute-start | bytes 835592 | tf_op jit(solution)/shard_map/ppermute | solution.py:406
  9.5 6.6 %collective-permute-start.5 = (bf16[64,2176]{1,0:T(8,128)(2,1)S(1)}, bf16[64,2176]{1,0:T(8,128)(2,1)S(1)}, u32[]{:S(2)}, u32[]{:S(2)}) collective-permute-start(bf16[64,2176]{1,0:T(8,128)(2,1)S(1)} %collective-permute-done.1.refs_1_), channel_id=1, source_target_pairs={{0,1},{1,0},{2,3},{3,2},{4,5},{5,4},{6,7},{7,6},{8,10},{9,11},{10,... | collective-permute-start | bytes 835592 | tf_op jit(solution)/shard_map/ppermute | solution.py:406
  11.5 6.6 %collective-permute-start.7 = (bf16[64,2176]{1,0:T(8,128)(2,1)S(1)}, bf16[64,2176]{1,0:T(8,128)(2,1)S(1)}, u32[]{:S(2)}, u32[]{:S(2)}) collective-permute-start(bf16[64,2176]{1,0:T(8,128)(2,1)S(1)} %prepare.1.refs_0_), channel_id=1, source_target_pairs={{0,8},{1,9},{2,10},{3,11},{4,12},{5,13},{6,14},{7,15},{8,0},{9,1},... | collective-permute-start | bytes 835592 | tf_op jit(solution)/shard_map/ppermute | solution.py:406
  11.6 6.6 %collective-permute-start.9 = (bf16[64,2176]{1,0:T(8,128)(2,1)S(1)}, bf16[64,2176]{1,0:T(8,128)(2,1)S(1)}, u32[]{:S(2)}, u32[]{:S(2)}) collective-permute-start(bf16[64,2176]{1,0:T(8,128)(2,1)S(1)} %collective-permute-done.3.refs_2_), channel_id=1, source_target_pairs={{0,8},{1,9},{2,10},{3,11},{4,12},{5,13},{6,14},{7,15},{8,0},{9,1},... | collective-permute-start | bytes 835592 | tf_op jit(solution)/shard_map/ppermute | solution.py:406
  12.0 8.1 %collective-permute-start.8 = (bf16[64,2176]{1,0:T(8,128)(2,1)S(1)}, bf16[64,2176]{1,0:T(8,128)(2,1)S(1)}, u32[]{:S(2)}, u32[]{:S(2)}) collective-permute-start(bf16[64,2176]{1,0:T(8,128)(2,1)S(1)} %collective-permute-done.1.refs_1_), channel_id=1, source_target_pairs={{0,8},{1,9},{2,10},{3,11},{4,12},{5,13},{6,14},{7,15},{8,0},{9,1},... | collective-permute-start | bytes 835592 | tf_op jit(solution)/shard_map/ppermute | solution.py:406
  16.0 17.3 %collective-permute-start = (bf16[64,2176]{1,0:T(8,128)(2,1)S(1)}, bf16[64,2176]{1,0:T(8,128)(2,1)S(1)}, u32[]{:S(2)}, u32[]{:S(2)}) collective-permute-start(bf16[64,2176]{1,0:T(8,128)(2,1)S(1)} %prepare.1.refs_0_), channel_id=1, source_target_pairs={{0,2},{1,3},{2,0},{3,1},{4,6},{5,7},{6,4},{7,5},{8,24},{9,25},{10,... | collective-permute-start | bytes 835592 | tf_op jit(solution)/shard_map/ppermute | solution.py:406
  18.1 15.3 %collective-permute-start.4 = (bf16[64,2176]{1,0:T(8,128)(2,1)S(1)}, bf16[64,2176]{1,0:T(8,128)(2,1)S(1)}, u32[]{:S(2)}, u32[]{:S(2)}) collective-permute-start(bf16[64,2176]{1,0:T(8,128)(2,1)S(1)} %collective-permute-done.3.refs_2_), channel_id=1, source_target_pairs={{0,2},{1,3},{2,0},{3,1},{4,6},{5,7},{6,4},{7,5},{8,24},{9,25},{10,... | collective-permute-start | bytes 835592 | tf_op jit(solution)/shard_map/ppermute | solution.py:406
  18.2 15.2 %collective-permute-start.2 = (bf16[64,2176]{1,0:T(8,128)(2,1)S(1)}, bf16[64,2176]{1,0:T(8,128)(2,1)S(1)}, u32[]{:S(2)}, u32[]{:S(2)}) collective-permute-start(bf16[64,2176]{1,0:T(8,128)(2,1)S(1)} %collective-permute-done.1.refs_1_), channel_id=1, source_target_pairs={{0,2},{1,3},{2,0},{3,1},{4,6},{5,7},{6,4},{7,5},{8,24},{9,25},{10,... | collective-permute-start | bytes 835592 | tf_op jit(solution)/shard_map/ppermute | solution.py:406
  20.2 13.3 %collective-permute-start.6 = (bf16[64,2176]{1,0:T(8,128)(2,1)S(1)}, bf16[64,2176]{1,0:T(8,128)(2,1)S(1)}, u32[]{:S(2)}, u32[]{:S(2)}) collective-permute-start(bf16[64,2176]{1,0:T(8,128)(2,1)S(1)} %collective-permute-done.5.refs_3_), channel_id=1, source_target_pairs={{0,2},{1,3},{2,0},{3,1},{4,6},{5,7},{6,4},{7,5},{8,24},{9,25},{10,... | collective-permute-start | bytes 835592 | tf_op jit(solution)/shard_map/ppermute | solution.py:406
  34.5 15.3 %collective-permute-start.11 = (bf16[256,2048]{1,0:T(8,128)(2,1)S(1)}, bf16[256,2048]{1,0:T(8,128)(2,1)S(1)}, u32[]{:S(2)}, u32[]{:S(2)}) collective-permute-start(bf16[256,2048]{1,0:T(8,128)(2,1)S(1)} %get-tuple-element.50), channel_id=1, source_target_pairs={{0,8},{1,9},{2,10},{3,11},{4,12},{5,13},{6,14},{7,15},{8,0},{9,1},... | collective-permute-start | bytes 3145736 | tf_op jit(solution)/shard_map/ppermute | solution.py:406
  50.0 6.5 %collective-permute-start.13 = (bf16[64,2048]{1,0:T(8,128)(2,1)S(1)}, bf16[64,2048]{1,0:T(8,128)(2,1)S(1)}, u32[]{:S(2)}, u32[]{:S(2)}) collective-permute-start(bf16[64,2048]{1,0:T(8,128)(2,1)S(1)} %get-tuple-element.54), channel_id=1, source_target_pairs={{0,1},{1,0},{2,3},{3,2},{4,5},{5,4},{6,7},{7,6},{8,10},{9,11},{10,... | collective-permute-start | bytes 786440 | tf_op jit(solution)/shard_map/ppermute | solution.py:406
  52.6 7.0 %collective-permute-start.20 = (bf16[64,2048]{1,0:T(8,128)(2,1)S(1)}, bf16[64,2048]{1,0:T(8,128)(2,1)S(1)}, u32[]{:S(2)}, u32[]{:S(2)}) collective-permute-start(bf16[64,2048]{1,0:T(8,128)(2,1)S(1)} %get-tuple-element.65), channel_id=1, source_target_pairs={{0,1},{1,0},{2,3},{3,2},{4,5},{5,4},{6,7},{7,6},{8,10},{9,11},{10,... | collective-permute-start | bytes 786440 | tf_op jit(solution)/shard_map/ppermute | solution.py:406
  54.5 10.4 %collective-permute-start.22 = (bf16[64,2048]{1,0:T(8,128)(2,1)S(1)}, bf16[64,2048]{1,0:T(8,128)(2,1)S(1)}, u32[]{:S(2)}, u32[]{:S(2)}) collective-permute-start(bf16[64,2048]{1,0:T(8,128)(2,1)S(1)} %get-tuple-element.67), channel_id=1, source_target_pairs={{0,1},{1,0},{2,3},{3,2},{4,5},{5,4},{6,7},{7,6},{8,10},{9,11},{10,... | collective-permute-start | bytes 786440 | tf_op jit(solution)/shard_map/ppermute | solution.py:406
  54.6 19.1 %collective-permute-start.12 = (bf16[64,2048]{1,0:T(8,128)(2,1)S(1)}, bf16[64,2048]{1,0:T(8,128)(2,1)S(1)}, u32[]{:S(2)}, u32[]{:S(2)}) collective-permute-start(bf16[64,2048]{1,0:T(8,128)(2,1)S(1)} %get-tuple-element.52), channel_id=1, source_target_pairs={{0,1},{1,0},{2,3},{3,2},{4,5},{5,4},{6,7},{7,6},{8,10},{9,11},{10,... | collective-permute-start | bytes 786440 | tf_op jit(solution)/shard_map/ppermute | solution.py:406
  56.6 17.1 %collective-permute-start.14 = (bf16[64,2048]{1,0:T(8,128)(2,1)S(1)}, bf16[64,2048]{1,0:T(8,128)(2,1)S(1)}, u32[]{:S(2)}, u32[]{:S(2)}) collective-permute-start(bf16[64,2048]{1,0:T(8,128)(2,1)S(1)} %add_blocks.6), channel_id=1, source_target_pairs={{0,16},{1,17},{2,18},{3,19},{4,20},{5,21},{6,22},{7,23},{8,9},{9,8... | collective-permute-start | bytes 786440 | tf_op jit(solution)/shard_map/ppermute | solution.py:406
  59.6 14.1 %collective-permute-start.21 = (bf16[64,2048]{1,0:T(8,128)(2,1)S(1)}, bf16[64,2048]{1,0:T(8,128)(2,1)S(1)}, u32[]{:S(2)}, u32[]{:S(2)}) collective-permute-start(bf16[64,2048]{1,0:T(8,128)(2,1)S(1)} %add_blocks.8), channel_id=1, source_target_pairs={{0,2},{1,3},{2,0},{3,1},{4,6},{5,7},{6,4},{7,5},{8,24},{9,25},{10,... | collective-permute-start | bytes 786440 | tf_op jit(solution)/shard_map/ppermute | solution.py:406
  65.0 8.8 %collective-permute-start.23 = (bf16[64,2048]{1,0:T(8,128)(2,1)S(1)}, bf16[64,2048]{1,0:T(8,128)(2,1)S(1)}, u32[]{:S(2)}, u32[]{:S(2)}) collective-permute-start(bf16[64,2048]{1,0:T(8,128)(2,1)S(1)} %add_blocks.9), channel_id=1, source_target_pairs={{0,18},{1,19},{2,16},{3,17},{4,22},{5,23},{6,20},{7,21},{8,25},{9,... | collective-permute-start | bytes 786440 | tf_op jit(solution)/shard_map/ppermute | solution.py:406
  75.3 6.4 %collective-permute-start.26 = (bf16[64,2048]{1,0:T(8,128)(2,1)S(1)}, bf16[64,2048]{1,0:T(8,128)(2,1)S(1)}, u32[]{:S(2)}, u32[]{:S(2)}) collective-permute-start(bf16[64,2048]{1,0:T(8,128)(2,1)S(1)} %get-tuple-element.75.refs_0_), channel_id=1, source_target_pairs={{0,1},{1,0},{2,3},{3,2},{4,5},{5,4},{6,7},{7,6},{8,9},{9,8},{10,11... | collective-permute-start | bytes 786440 | tf_op jit(solution)/shard_map/ppermute | solution.py:406
  76.8 10.1 %collective-permute-start.25 = (bf16[64,2048]{1,0:T(8,128)(2,1)S(1)}, bf16[64,2048]{1,0:T(8,128)(2,1)S(1)}, u32[]{:S(2)}, u32[]{:S(2)}) collective-permute-start(bf16[64,2048]{1,0:T(8,128)(2,1)S(1)} %get-tuple-element.75.refs_0_), channel_id=1, source_target_pairs={{0,2},{1,3},{2,0},{3,1},{4,6},{5,7},{6,4},{7,5},{8,10},{9,11},{10,... | collective-permute-start | bytes 786440 | tf_op jit(solution)/shard_map/ppermute | solution.py:406
  77.3 9.6 %collective-permute-start.24 = (bf16[64,2048]{1,0:T(8,128)(2,1)S(1)}, bf16[64,2048]{1,0:T(8,128)(2,1)S(1)}, u32[]{:S(2)}, u32[]{:S(2)}) collective-permute-start(bf16[64,2048]{1,0:T(8,128)(2,1)S(1)} %get-tuple-element.75.refs_0_), channel_id=1, source_target_pairs={{0,4},{1,5},{2,6},{3,7},{4,0},{5,1},{6,2},{7,3},{8,12},{9,13},{10,... | collective-permute-start | bytes 786440 | tf_op jit(solution)/shard_map/ppermute | solution.py:406
  86.9 10.6 %collective-permute-start.31 = (bf16[64,2048]{1,0:T(8,128)(2,1)S(1)}, bf16[64,2048]{1,0:T(8,128)(2,1)S(1)}, u32[]{:S(2)}, u32[]{:S(2)}) collective-permute-start(bf16[64,2048]{1,0:T(8,128)(2,1)S(1)} %collective-permute-done.24.refs_3_), channel_id=1, source_target_pairs={{0,1},{1,0},{2,3},{3,2},{4,5},{5,4},{6,7},{7,6},{8,10},{9,11},{10,... | collective-permute-start | bytes 786440 | tf_op jit(solution)/shard_map/ppermute | solution.py:406
  88.2 13.0 %collective-permute-start.32 = (bf16[64,2048]{1,0:T(8,128)(2,1)S(1)}, bf16[64,2048]{1,0:T(8,128)(2,1)S(1)}, u32[]{:S(2)}, u32[]{:S(2)}) collective-permute-start(bf16[64,2048]{1,0:T(8,128)(2,1)S(1)} %collective-permute-done.24.refs_3_), channel_id=1, source_target_pairs={{0,2},{1,3},{2,0},{3,1},{4,6},{5,7},{6,4},{7,5},{8,9},{9,8},{10,11... | collective-permute-start | bytes 786440 | tf_op jit(solution)/shard_map/ppermute | solution.py:406
  91.4 10.7 %collective-permute-start.30 = (bf16[64,2048]{1,0:T(8,128)(2,1)S(1)}, bf16[64,2048]{1,0:T(8,128)(2,1)S(1)}, u32[]{:S(2)}, u32[]{:S(2)}) collective-permute-start(bf16[64,2048]{1,0:T(8,128)(2,1)S(1)} %collective-permute-done.25.refs_1_), channel_id=1, source_target_pairs={{0,1},{1,0},{2,3},{3,2},{4,5},{5,4},{6,7},{7,6},{8,9},{9,8},{10,11... | collective-permute-start | bytes 786440 | tf_op jit(solution)/shard_map/ppermute | solution.py:406
  97.5 6.4 %collective-permute-start.33 = (bf16[64,2048]{1,0:T(8,128)(2,1)S(1)}, bf16[64,2048]{1,0:T(8,128)(2,1)S(1)}, u32[]{:S(2)}, u32[]{:S(2)}) collective-permute-start(bf16[64,2048]{1,0:T(8,128)(2,1)S(1)} %collective-permute-done.31.refs_1_), channel_id=1, source_target_pairs={{0,2},{1,3},{2,0},{3,1},{4,6},{5,7},{6,4},{7,5},{8,9},{9,8},{10,11... | collective-permute-start | bytes 786440 | tf_op jit(solution)/shard_map/ppermute | solution.py:406
  98.5 13.7 %collective-permute-start.29 = (f32[1,64]{1,0:T(1,128)S(1)}, f32[1,64]{1,0:T(1,128)S(1)}, u32[]{:S(2)}, u32[]{:S(2)}) collective-permute-start(f32[1,64]{1,0:T(1,128)S(1)} %get-tuple-element.85), channel_id=1, source_target_pairs={{0,4},{1,5},{2,6},{3,7},{4,0},{5,1},{6,2},{7,3},{8,12},{9,13},{10,... | collective-permute-start | bytes 776 | tf_op jit(solution)/shard_map/ppermute | solution.py:406
  100.1 12.9 %collective-permute-start.28 = (f32[1,64]{1,0:T(1,128)S(1)}, f32[1,64]{1,0:T(1,128)S(1)}, u32[]{:S(2)}, u32[]{:S(2)}) collective-permute-start(f32[1,64]{1,0:T(1,128)S(1)} %get-tuple-element.86), channel_id=1, source_target_pairs={{0,1},{1,0},{2,3},{3,2},{4,5},{5,4},{6,7},{7,6},{8,9},{9,8},{10,11... | collective-permute-start | bytes 776 | tf_op jit(solution)/shard_map/ppermute | solution.py:406
  101.2 15.1 %collective-permute-start.27 = (f32[1,64]{1,0:T(1,128)S(1)}, f32[1,64]{1,0:T(1,128)S(1)}, u32[]{:S(2)}, u32[]{:S(2)}) collective-permute-start(f32[1,64]{1,0:T(1,128)S(1)} %get-tuple-element.87), channel_id=1, source_target_pairs={{0,2},{1,3},{2,0},{3,1},{4,6},{5,7},{6,4},{7,5},{8,10},{9,11},{10,... | collective-permute-start | bytes 776 | tf_op jit(solution)/shard_map/ppermute | solution.py:406
  108.4 7.9 %collective-permute-start.37 = (f32[1,64]{1,0:T(1,128)S(1)}, f32[1,64]{1,0:T(1,128)S(1)}, u32[]{:S(2)}, u32[]{:S(2)}) collective-permute-start(f32[1,64]{1,0:T(1,128)S(1)} %get-tuple-element.81), channel_id=1, source_target_pairs={{0,7},{1,6},{2,5},{3,4},{4,3},{5,2},{6,1},{7,0},{8,15},{9,14},{10,... | collective-permute-start | bytes 776 | tf_op jit(solution)/shard_map/ppermute | solution.py:406
  110.9 5.3 %collective-permute-start.36 = (f32[1,64]{1,0:T(1,128)S(1)}, f32[1,64]{1,0:T(1,128)S(1)}, u32[]{:S(2)}, u32[]{:S(2)}) collective-permute-start(f32[1,64]{1,0:T(1,128)S(1)} %get-tuple-element.82), channel_id=1, source_target_pairs={{0,6},{1,7},{2,4},{3,5},{4,2},{5,3},{6,0},{7,1},{8,13},{9,12},{10,... | collective-permute-start | bytes 776 | tf_op jit(solution)/shard_map/ppermute | solution.py:406
  112.2 5.3 %collective-permute-start.35 = (f32[1,64]{1,0:T(1,128)S(1)}, f32[1,64]{1,0:T(1,128)S(1)}, u32[]{:S(2)}, u32[]{:S(2)}) collective-permute-start(f32[1,64]{1,0:T(1,128)S(1)} %get-tuple-element.83), channel_id=1, source_target_pairs={{0,5},{1,4},{2,7},{3,6},{4,1},{5,0},{6,3},{7,2},{8,14},{9,15},{10,... | collective-permute-start | bytes 776 | tf_op jit(solution)/shard_map/ppermute | solution.py:406
  113.0 4.7 %collective-permute-start.34 = (f32[1,64]{1,0:T(1,128)S(1)}, f32[1,64]{1,0:T(1,128)S(1)}, u32[]{:S(2)}, u32[]{:S(2)}) collective-permute-start(f32[1,64]{1,0:T(1,128)S(1)} %get-tuple-element.84), channel_id=1, source_target_pairs={{0,3},{1,2},{2,1},{3,0},{4,7},{5,6},{6,5},{7,4},{8,11},{9,10},{10,... | collective-permute-start | bytes 776 | tf_op jit(solution)/shard_map/ppermute | solution.py:406
  (9 other events, 32.1 us)

commit v4 on v3

--- a/solution.py
+++ b/solution.py
@@ -9,7 +9,7 @@
 
 CAP = 24
 META = 128
-CUT = 768
+CUT = 512
 DOWN_CUT = 512
 SPREAD = 1024
 VMEM_LIMIT = 60 * 1024 * 1024
@@ -342,18 +342,18 @@
     )(lengths, *found)
 
 
-def peak_kernel(blocks, *refs):
+def peak_kernel(blocks, start, stop, *refs):
     block_refs = refs[:blocks]
-    head_ref, out_ref, table = refs[blocks:]
+    head_ref, *prior, out_ref, table = refs[blocks:]
     rows = block_refs[0].shape[0]
-    words = head_ref.shape[0]
     for i, ref in enumerate(block_refs):
         table[i * rows : (i + 1) * rows, :] = ref[...]
+    words = stop - start
     tile = max(t for t in range(16, 513, 16) if words % t == 0)
     best = None
-    for j in range(words // tile):
+    for at in range(start, stop, tile):
         logits = lax.dot_general(
-            head_ref[j * tile : (j + 1) * tile, :],
+            head_ref[at : at + tile, :],
             table[...],
             (((1,), (1,)), ((), ())),
             preferred_element_type=F32,
@@ -361,23 +361,25 @@
         peak = jnp.max(logits, axis=0, keepdims=True)
         best = peak if best is None else jnp.maximum(best, peak)
     for i in range(blocks):
-        out_ref[i : i + 1, :] = best[:, i * rows : (i + 1) * rows]
-
-
-def peaks(block_list, words_first):
+        line = best[:, i * rows : (i + 1) * rows]
+        if prior:
+            line = jnp.maximum(line, prior[0][i : i + 1, :])
+        out_ref[i : i + 1, :] = line
+
+
+def peaks(block_list, words_first, start, stop, prior=()):
     blocks = len(block_list)
     rows, width = block_list[0].shape
-    words = words_first.shape[0]
-    return pl.pallas_call(
-        functools.partial(peak_kernel, blocks),
-        in_specs=[LOCAL] * (blocks + 1),
+    return pl.pallas_call(
+        functools.partial(peak_kernel, blocks, start, stop),
+        in_specs=[LOCAL] * (blocks + 1 + len(prior)),
         out_specs=LOCAL,
         out_shape=jax.ShapeDtypeStruct((blocks, rows), F32),
         scratch_shapes=[pltpu.VMEM((blocks * rows, width), BF16)],
         compiler_params=params(12 * 1024 * 1024),
         cost_estimate=SHORT,
         name="peaks",
-    )(*map(near_core, block_list), near_core(words_first))
+    )(*map(near_core, block_list), near_core(words_first), *prior)
 
 
 def per_device(
@@ -455,8 +457,7 @@
             ways += [(a + [p], b + [q]) for a, b in ways]
         return ways
 
-    def peak_back(group):
-        peak = peaks([held[k] for k in group], words_first)
+    def give_back(group, peak):
         out = []
         for n, (side, i) in enumerate(group):
             p, q = trees[side][i]
@@ -466,9 +467,9 @@
             elif p:
                 one = send(one, p, q)
             out.append(one)
-        return out, peak
-
-    trees = tree(exp_dims[::-1], exp_dims[::-1]), tree(exp_dims, exp_dims[1:] + exp_dims[:1])
+        return out
+
+    trees = tree(exp_dims[::-1], exp_dims[::-1]), tree(exp_dims[1:] + exp_dims[:1], exp_dims)
     singles = [i for i, (p, _) in enumerate(trees[0]) if len(p) == 1]
     first = send(normed, [across])
     first, *near_singles = lax.optimization_barrier(
@@ -479,15 +480,21 @@
         held[0, i] = x
         held[1, i] = send(first, *trees[1][i])
     early = sorted(k for k in held if k == (1, 0) or k[0] == 0)
-    found, peak = peak_back(early)
+    words = head_weight.shape[1]
+    cut = words // 32 * 16
+    early_in = [held[k] for k in early]
+    peak = peaks(early_in, words_first, 0, cut)
     for i in singles:
         held[1, i], peak = lax.optimization_barrier((held[1, i], peak))
-    for side in (1, 0):
+    for side in (0, 1):
         for i, (p, q) in enumerate(trees[side]):
             if len(p) > 1:
                 before = trees[side].index((p[:-1], q[:-1]))
                 held[side, i] = send(held[side, before], p[-1:], q[-1:])
-    found += peak_back(sorted(k for k in held if k not in early))[0]
+    peak = peaks(early_in, words_first, cut, words, [peak])
+    late = sorted((k for k in held if k not in early), reverse=True)
+    found = give_back(early, peak)
+    found += give_back(late, peaks([held[k] for k in late], words_first, 0, words))
     request_max = request_peaks(lengths, found)
     return (hidden_out, request_norm[0], request_max[0])
 

time: 119 us -> 118 us (level)
  starting transfers between devices: 48.8 us -> 46.1 us
  waiting for transfers between devices: 23.4 us -> 24.8 us
    ppermute x38, starting transfers between devices: 48.8 us -> 46.1 us  [send(): return lax.ppermute(x, AXES, pairs)]
    ppermute x38, waiting for transfers between devices: 23.4 us -> 24.8 us  [send(): return lax.ppermute(x, AXES, pairs)]
    pallas_call x2 -> x3, Pallas kernels: 9.02 us -> 9.31 us  [peaks(): pl.pallas_call(functools.partial(peak_kernel, blocks, start, stop), in_sp...]
  transfers between devices with their start and end apart: 38 -> 38, of which waited for: 15 -> 15; matrix products, arithmetic and copies ran while one was open for 0% -> 0% of each run, Pallas kernels for 35% -> 36%
where the time goes in v4:
time: 118 us
  starting transfers between devices  46.1 us (39%)
  Pallas kernels  46 us (39%)
  waiting for transfers between devices  24.8 us (21%)
    ppermute x38, starting transfers between devices, send(): return lax.ppermute(x, AXES, pairs)  46.1 us
    pallas_call x2, Pallas kernels, run_expert(): pl.pallas_call(functools.partial(expert_kernel, blocks, slots), in_specs=...  26.3 us
    ppermute x38, waiting for transfers between devices, send(): return lax.ppermute(x, AXES, pairs)  24.8 us
    pallas_call x3, Pallas kernels, peaks(): pl.pallas_call(functools.partial(peak_kernel, blocks, start, stop), in_sp...  9.31 us
    pallas_call x1, Pallas kernels, fetch(): pl.pallas_call(functools.partial(fetch_kernel, parts), in_specs=[pl.Block...  5.8 us
  transfers between devices with their start and end apart: 38, of which 15 were waited for; matrix products, arithmetic and copies ran while one was open for 0% of the time, Pallas kernels for 36%

profile of v4, /device:TPU:0, one launch (start us, length us, event | category | flops | bytes accessed | tf_op | source)
XLA Modules:
  0.0 117.8 jit_solution(11848776971766832492)
XLA Ops:
  1.9 3.0 %collective-permute-start.1 = (bf16[64,2176]{1,0:T(8,128)(2,1)S(1)}, bf16[64,2176]{1,0:T(8,128)(2,1)S(1)}, u32[]{:S(2)}, u32[]{:S(2)}) collective-permute-start(bf16[64,2176]{1,0:T(8,128)(2,1)S(1)} %prepare.1.refs_0_), channel_id=1, source_target_pairs={{0,16},{1,17},{2,18},{3,19},{4,20},{5,21},{6,22},{7,23},{8,9},{9,8... | collective-permute-start | bytes 835592 | tf_op jit(solution)/shard_map/ppermute | solution.py:408
  4.9 1.5 %collective-permute-start.3 = (bf16[64,2176]{1,0:T(8,128)(2,1)S(1)}, bf16[64,2176]{1,0:T(8,128)(2,1)S(1)}, u32[]{:S(2)}, u32[]{:S(2)}) collective-permute-start(bf16[64,2176]{1,0:T(8,128)(2,1)S(1)} %prepare.1.refs_0_), channel_id=1, source_target_pairs={{0,1},{1,0},{2,3},{3,2},{4,5},{5,4},{6,7},{7,6},{8,10},{9,11},{10,... | collective-permute-start | bytes 835592 | tf_op jit(solution)/shard_map/ppermute | solution.py:408
  6.4 3.0 %collective-permute-done.1.refs_1_ = bf16[64,2176]{1,0:T(8,128)(2,1)S(1)} collective-permute-done((bf16[64,2176]{1,0:T(8,128)(2,1)S(1)}, bf16[64,2176]{1,0:T(8,128)(2,1)S(1)}, u32[]{:S(2)}, u32[]{:S(2)}) %collective-permute-start.1) | collective-permute-done | bytes 278560 | tf_op jit(solution)/shard_map/ppermute | solution.py:408
  9.5 2.0 %collective-permute-start.5 = (bf16[64,2176]{1,0:T(8,128)(2,1)S(1)}, bf16[64,2176]{1,0:T(8,128)(2,1)S(1)}, u32[]{:S(2)}, u32[]{:S(2)}) collective-permute-start(bf16[64,2176]{1,0:T(8,128)(2,1)S(1)} %collective-permute-done.1.refs_1_), channel_id=1, source_target_pairs={{0,1},{1,0},{2,3},{3,2},{4,5},{5,4},{6,7},{7,6},{8,10},{9,11},{10,... | collective-permute-start | bytes 835592 | tf_op jit(solution)/shard_map/ppermute | solution.py:408
  12.0 4.0 %collective-permute-done.5.refs_3_ = bf16[64,2176]{1,0:T(8,128)(2,1)S(1)} collective-permute-done((bf16[64,2176]{1,0:T(8,128)(2,1)S(1)}, bf16[64,2176]{1,0:T(8,128)(2,1)S(1)}, u32[]{:S(2)}, u32[]{:S(2)}) %collective-permute-start.5) | collective-permute-done | bytes 278560 | tf_op jit(solution)/shard_map/ppermute | solution.py:408
  16.0 2.1 %collective-permute-start = (bf16[64,2176]{1,0:T(8,128)(2,1)S(1)}, bf16[64,2176]{1,0:T(8,128)(2,1)S(1)}, u32[]{:S(2)}, u32[]{:S(2)}) collective-permute-start(bf16[64,2176]{1,0:T(8,128)(2,1)S(1)} %prepare.1.refs_0_), channel_id=1, source_target_pairs={{0,2},{1,3},{2,0},{3,1},{4,6},{5,7},{6,4},{7,5},{8,24},{9,25},{10,... | collective-permute-start | bytes 835592 | tf_op jit(solution)/shard_map/ppermute | solution.py:408
  18.2 2.0 %collective-permute-start.4 = (bf16[64,2176]{1,0:T(8,128)(2,1)S(1)}, bf16[64,2176]{1,0:T(8,128)(2,1)S(1)}, u32[]{:S(2)}, u32[]{:S(2)}) collective-permute-start(bf16[64,2176]{1,0:T(8,128)(2,1)S(1)} %collective-permute-done.3.refs_2_), channel_id=1, source_target_pairs={{0,2},{1,3},{2,0},{3,1},{4,6},{5,7},{6,4},{7,5},{8,24},{9,25},{10,... | collective-permute-start | bytes 835592 | tf_op jit(solution)/shard_map/ppermute | solution.py:408
  20.2 13.1 %expert.2 = (bf16[64,2048]{1,0:T(8,128)(2,1)S(1)}, bf16[64,2048]{1,0:T(8,128)(2,1)S(1)}, bf16[64,2048]{1,0:T(8,128)(2,1)S(1)}, bf16[64,2048]{1,0:T(8,128)(2,1)S(1)}, bf16[256,2048]{1,0:T(8,128)(2,1)S(1)}) custom-call(s32[1]{0:T(128)} %bitcast.3.expert_ref, bf16[64,2176]{1,0:T(8,128)(2,1)S(1)} %prepare.1.refs_0_, ...), custom_call_target="tpu_custom_call" | custom-call | flops 1 | bytes 1 | tf_op jit(solution)/shard_map/expert/pallas_call | solution.py:234
  36.1 13.3 %expert.3 = (bf16[64,2048]{1,0:T(8,128)(2,1)S(1)}, bf16[64,2048]{1,0:T(8,128)(2,1)S(1)}, bf16[64,2048]{1,0:T(8,128)(2,1)S(1)}, bf16[64,2048]{1,0:T(8,128)(2,1)S(1)}, bf16[256,2048]{1,0:T(8,128)(2,1)S(1)}) custom-call(s32[1]{0:T(128)} %bitcast.3.expert_ref, bf16[64,2176]{1,0:T(8,128)(2,1)S(1)} %collective-permute-done.refs_0_, ...), custom_call_target="tpu_custom_call" | custom-call | flops 1 | bytes 1 | tf_op jit(solution)/shard_map/expert/pallas_call | solution.py:234
  49.9 2.0 %collective-permute-start.13 = (bf16[64,2048]{1,0:T(8,128)(2,1)S(1)}, bf16[64,2048]{1,0:T(8,128)(2,1)S(1)}, u32[]{:S(2)}, u32[]{:S(2)}) collective-permute-start(bf16[64,2048]{1,0:T(8,128)(2,1)S(1)} %get-tuple-element.57), channel_id=1, source_target_pairs={{0,1},{1,0},{2,3},{3,2},{4,5},{5,4},{6,7},{7,6},{8,10},{9,11},{10,... | collective-permute-start | bytes 786440 | tf_op jit(solution)/shard_map/ppermute | solution.py:408
  52.4 2.0 %collective-permute-start.20 = (bf16[64,2048]{1,0:T(8,128)(2,1)S(1)}, bf16[64,2048]{1,0:T(8,128)(2,1)S(1)}, u32[]{:S(2)}, u32[]{:S(2)}) collective-permute-start(bf16[64,2048]{1,0:T(8,128)(2,1)S(1)} %get-tuple-element.68), channel_id=1, source_target_pairs={{0,1},{1,0},{2,3},{3,2},{4,5},{5,4},{6,7},{7,6},{8,10},{9,11},{10,... | collective-permute-start | bytes 786440 | tf_op jit(solution)/shard_map/ppermute | solution.py:408
  54.5 1.9 %collective-permute-start.12 = (bf16[64,2048]{1,0:T(8,128)(2,1)S(1)}, bf16[64,2048]{1,0:T(8,128)(2,1)S(1)}, u32[]{:S(2)}, u32[]{:S(2)}) collective-permute-start(bf16[64,2048]{1,0:T(8,128)(2,1)S(1)} %get-tuple-element.55), channel_id=1, source_target_pairs={{0,1},{1,0},{2,3},{3,2},{4,5},{5,4},{6,7},{7,6},{8,10},{9,11},{10,... | collective-permute-start | bytes 786440 | tf_op jit(solution)/shard_map/ppermute | solution.py:408
  56.5 1.8 %collective-permute-start.14 = (bf16[64,2048]{1,0:T(8,128)(2,1)S(1)}, bf16[64,2048]{1,0:T(8,128)(2,1)S(1)}, u32[]{:S(2)}, u32[]{:S(2)}) collective-permute-start(bf16[64,2048]{1,0:T(8,128)(2,1)S(1)} %add_blocks.6), channel_id=1, source_target_pairs={{0,16},{1,17},{2,18},{3,19},{4,20},{5,21},{6,22},{7,23},{8,9},{9,8... | collective-permute-start | bytes 786440 | tf_op jit(solution)/shard_map/ppermute | solution.py:408
  59.5 2.2 %collective-permute-start.21 = (bf16[64,2048]{1,0:T(8,128)(2,1)S(1)}, bf16[64,2048]{1,0:T(8,128)(2,1)S(1)}, u32[]{:S(2)}, u32[]{:S(2)}) collective-permute-start(bf16[64,2048]{1,0:T(8,128)(2,1)S(1)} %add_blocks.8), channel_id=1, source_target_pairs={{0,2},{1,3},{2,0},{3,1},{4,6},{5,7},{6,4},{7,5},{8,24},{9,25},{10,... | collective-permute-start | bytes 786440 | tf_op jit(solution)/shard_map/ppermute | solution.py:408
  61.7 3.0 %collective-permute-done.22.refs_1_ = bf16[64,2048]{1,0:T(8,128)(2,1)S(1)} collective-permute-done((bf16[64,2048]{1,0:T(8,128)(2,1)S(1)}, bf16[64,2048]{1,0:T(8,128)(2,1)S(1)}, u32[]{:S(2)}, u32[]{:S(2)}) %collective-permute-start.22) | collective-permute-done | bytes 262176 | tf_op jit(solution)/shard_map/ppermute | solution.py:408
  64.8 3.0 %collective-permute-start.23 = (bf16[64,2048]{1,0:T(8,128)(2,1)S(1)}, bf16[64,2048]{1,0:T(8,128)(2,1)S(1)}, u32[]{:S(2)}, u32[]{:S(2)}) collective-permute-start(bf16[64,2048]{1,0:T(8,128)(2,1)S(1)} %add_blocks.9), channel_id=1, source_target_pairs={{0,18},{1,19},{2,16},{3,17},{4,22},{5,23},{6,20},{7,21},{8,25},{9,... | collective-permute-start | bytes 786440 | tf_op jit(solution)/shard_map/ppermute | solution.py:408
  67.8 5.8 %fetch.1.refs_4_ = bf16[4000,2048]{1,0:T(8,128)(2,1)S(1)} custom-call(bf16[4000,2048]{1,0:T(8,128)(2,1)} %bitcast.8, bf16[256,2048]{1,0:T(8,128)(2,1)S(1)} %get-tuple-element.66.after_ref), custom_call_target="tpu_custom_call" | custom-call | flops 1 | bytes 1 | tf_op jit(solution)/shard_map/fetch/pallas_call | solution.py:129
  73.7 1.5 %finish.1 = (bf16[64,2048]{1,0:T(8,128)(2,1)}, bf16[64,2048]{1,0:T(8,128)(2,1)S(1)}, f32[1,4]{1,0:T(1,128)}) custom-call(s32[1,4]{1,0:T(1,128)S(1)} %copy-done.2, bf16[64,2048]{1,0:T(8,128)(2,1)S(1)} %copy-done, f32[1,2048]{1,0:T(1,128)S(1)} %bitcast.7, bf16[64,2048]{1,0:T(8,128)(2,1)S(1)} %get-tuple-element.71.refs_0_, ...), custom_call_target="tpu_custom_call" | custom-call | tf_op jit(solution)/shard_map/finish/pallas_call | solution.py:303
  75.2 2.6 %collective-permute-start.24 = (bf16[64,2048]{1,0:T(8,128)(2,1)S(1)}, bf16[64,2048]{1,0:T(8,128)(2,1)S(1)}, u32[]{:S(2)}, u32[]{:S(2)}) collective-permute-start(bf16[64,2048]{1,0:T(8,128)(2,1)S(1)} %get-tuple-element.78.refs_0_), channel_id=1, source_target_pairs={{0,4},{1,5},{2,6},{3,7},{4,0},{5,1},{6,2},{7,3},{8,12},{9,13},{10,... | collective-permute-start | bytes 786440 | tf_op jit(solution)/shard_map/ppermute | solution.py:408
  78.2 1.5 %collective-permute-start.26 = (bf16[64,2048]{1,0:T(8,128)(2,1)S(1)}, bf16[64,2048]{1,0:T(8,128)(2,1)S(1)}, u32[]{:S(2)}, u32[]{:S(2)}) collective-permute-start(bf16[64,2048]{1,0:T(8,128)(2,1)S(1)} %get-tuple-element.78.refs_0_), channel_id=1, source_target_pairs={{0,1},{1,0},{2,3},{3,2},{4,5},{5,4},{6,7},{7,6},{8,9},{9,8},{10,11... | collective-permute-start | bytes 786440 | tf_op jit(solution)/shard_map/ppermute | solution.py:408
  79.7 6.6 %collective-permute-done.24.refs_3_ = bf16[64,2048]{1,0:T(8,128)(2,1)S(1)} collective-permute-done((bf16[64,2048]{1,0:T(8,128)(2,1)S(1)}, bf16[64,2048]{1,0:T(8,128)(2,1)S(1)}, u32[]{:S(2)}, u32[]{:S(2)}) %collective-permute-start.24) | collective-permute-done | bytes 262176 | tf_op jit(solution)/shard_map/ppermute | solution.py:408
  88.5 1.5 %collective-permute-start.33 = (bf16[64,2048]{1,0:T(8,128)(2,1)S(1)}, bf16[64,2048]{1,0:T(8,128)(2,1)S(1)}, u32[]{:S(2)}, u32[]{:S(2)}) collective-permute-start(bf16[64,2048]{1,0:T(8,128)(2,1)S(1)} %collective-permute-done.25.refs_1_), channel_id=1, source_target_pairs={{0,1},{1,0},{2,3},{3,2},{4,5},{5,4},{6,7},{7,6},{8,9},{9,8},{10,11... | collective-permute-start | bytes 786440 | tf_op jit(solution)/shard_map/ppermute | solution.py:408
  90.0 2.4 %peaks.3.refs_5_ = f32[4,64]{1,0:T(4,128)S(1)} custom-call(bf16[64,2048]{1,0:T(8,128)(2,1)S(1)} %get-tuple-element.78.refs_0_, bf16[64,2048]{1,0:T(8,128)(2,1)S(1)} %collective-permute-done.25.refs_1_, bf16[64,2048]{1,0:T(8,128)(2,1)S(1)} %collective-permute-done.26.refs_2_, bf16[64,2048]{1,0:T(8,128)(2,1)S(1)} %collective-permute-done.24.refs_3_, ...), custom_call_target="tpu_custom_call" | custom-call | flops 1 | bytes 1 | tf_op jit(solution)/shard_map/peaks/pallas_call | solution.py:373
  92.5 2.0 %collective-permute-done.28.refs_2_ = bf16[64,2048]{1,0:T(8,128)(2,1)S(1)} collective-permute-done((bf16[64,2048]{1,0:T(8,128)(2,1)S(1)}, bf16[64,2048]{1,0:T(8,128)(2,1)S(1)}, u32[]{:S(2)}, u32[]{:S(2)}) %collective-permute-start.28) | collective-permute-done | bytes 262176 | tf_op jit(solution)/shard_map/ppermute | solution.py:408
  94.5 1.5 %collective-permute-start.32 = (bf16[64,2048]{1,0:T(8,128)(2,1)S(1)}, bf16[64,2048]{1,0:T(8,128)(2,1)S(1)}, u32[]{:S(2)}, u32[]{:S(2)}) collective-permute-start(bf16[64,2048]{1,0:T(8,128)(2,1)S(1)} %collective-permute-done.28.refs_2_), channel_id=1, source_target_pairs={{0,1},{1,0},{2,3},{3,2},{4,5},{5,4},{6,7},{7,6},{8,10},{9,11},{10,... | collective-permute-start | bytes 786440 | tf_op jit(solution)/shard_map/ppermute | solution.py:408
  96.0 2.4 %peaks.4 = f32[4,64]{1,0:T(4,128)S(1)} custom-call(bf16[64,2048]{1,0:T(8,128)(2,1)S(1)} %get-tuple-element.78.refs_0_, bf16[64,2048]{1,0:T(8,128)(2,1)S(1)} %collective-permute-done.25.refs_1_, bf16[64,2048]{1,0:T(8,128)(2,1)S(1)} %collective-permute-done.26.refs_2_, bf16[64,2048]{1,0:T(8,128)(2,1)S(1)} %collective-permute-done.24.refs_3_, ...), custom_call_target="tpu_custom_call" | custom-call | flops 1 | bytes 1 | tf_op jit(solution)/shard_map/peaks/pallas_call | solution.py:373
  98.4 1.8 %collective-permute-start.29 = (f32[1,64]{1,0:T(1,128)S(1)}, f32[1,64]{1,0:T(1,128)S(1)}, u32[]{:S(2)}, u32[]{:S(2)}) collective-permute-start(f32[1,64]{1,0:T(1,128)S(1)} %get-tuple-element.93), channel_id=1, source_target_pairs={{0,2},{1,3},{2,0},{3,1},{4,6},{5,7},{6,4},{7,5},{8,10},{9,11},{10,... | collective-permute-start | bytes 776 | tf_op jit(solution)/shard_map/ppermute | solution.py:408
  100.2 2.4 %collective-permute-start.31 = (f32[1,64]{1,0:T(1,128)S(1)}, f32[1,64]{1,0:T(1,128)S(1)}, u32[]{:S(2)}, u32[]{:S(2)}) collective-permute-start(f32[1,64]{1,0:T(1,128)S(1)} %get-tuple-element.91), channel_id=1, source_target_pairs={{0,4},{1,5},{2,6},{3,7},{4,0},{5,1},{6,2},{7,3},{8,12},{9,13},{10,... | collective-permute-start | bytes 776 | tf_op jit(solution)/shard_map/ppermute | solution.py:408
  102.6 4.5 %peaks.5 = f32[4,64]{1,0:T(4,128)S(1)} custom-call(bf16[64,2048]{1,0:T(8,128)(2,1)S(1)} %collective-permute-done.32.refs_0_, bf16[64,2048]{1,0:T(8,128)(2,1)S(1)} %collective-permute-done.27.refs_1_, bf16[64,2048]{1,0:T(8,128)(2,1)S(1)} %collective-permute-done.28.refs_2_, bf16[64,2048]{1,0:T(8,128)(2,1)S(1)} %collective-permute-done.33.refs_3_, ...), custom_call_target="tpu_custom_call" | custom-call | flops 1 | bytes 1 | tf_op jit(solution)/shard_map/peaks/pallas_call | solution.py:373
  107.1 2.8 %collective-permute-start.34 = (f32[1,64]{1,0:T(1,128)S(1)}, f32[1,64]{1,0:T(1,128)S(1)}, u32[]{:S(2)}, u32[]{:S(2)}) collective-permute-start(f32[1,64]{1,0:T(1,128)S(1)} %get-tuple-element.90), channel_id=1, source_target_pairs={{0,7},{1,6},{2,5},{3,4},{4,3},{5,2},{6,1},{7,0},{8,15},{9,14},{10,... | collective-permute-start | bytes 776 | tf_op jit(solution)/shard_map/ppermute | solution.py:408
  110.6 1.6 %collective-permute-start.36 = (f32[1,64]{1,0:T(1,128)S(1)}, f32[1,64]{1,0:T(1,128)S(1)}, u32[]{:S(2)}, u32[]{:S(2)}) collective-permute-start(f32[1,64]{1,0:T(1,128)S(1)} %get-tuple-element.88), channel_id=1, source_target_pairs={{0,6},{1,7},{2,4},{3,5},{4,2},{5,3},{6,0},{7,1},{8,13},{9,12},{10,... | collective-permute-start | bytes 776 | tf_op jit(solution)/shard_map/ppermute | solution.py:408
  112.2 2.1 %collective-permute-start.37 = (f32[1,64]{1,0:T(1,128)S(1)}, f32[1,64]{1,0:T(1,128)S(1)}, u32[]{:S(2)}, u32[]{:S(2)}) collective-permute-start(f32[1,64]{1,0:T(1,128)S(1)} %get-tuple-element.87), channel_id=1, source_target_pairs={{0,3},{1,2},{2,1},{3,0},{4,7},{5,6},{6,5},{7,4},{8,11},{9,10},{10,... | collective-permute-start | bytes 776 | tf_op jit(solution)/shard_map/ppermute | solution.py:408
  (66 shorter events, 14.0 us)
Async XLA Ops:
  1.9 7.5 %collective-permute-start.1 = (bf16[64,2176]{1,0:T(8,128)(2,1)S(1)}, bf16[64,2176]{1,0:T(8,128)(2,1)S(1)}, u32[]{:S(2)}, u32[]{:S(2)}) collective-permute-start(bf16[64,2176]{1,0:T(8,128)(2,1)S(1)} %prepare.1.refs_0_), channel_id=1, source_target_pairs={{0,16},{1,17},{2,18},{3,19},{4,20},{5,21},{6,22},{7,23},{8,9},{9,8... | collective-permute-start | bytes 835592 | tf_op jit(solution)/shard_map/ppermute | solution.py:408
  4.9 7.1 %collective-permute-start.3 = (bf16[64,2176]{1,0:T(8,128)(2,1)S(1)}, bf16[64,2176]{1,0:T(8,128)(2,1)S(1)}, u32[]{:S(2)}, u32[]{:S(2)}) collective-permute-start(bf16[64,2176]{1,0:T(8,128)(2,1)S(1)} %prepare.1.refs_0_), channel_id=1, source_target_pairs={{0,1},{1,0},{2,3},{3,2},{4,5},{5,4},{6,7},{7,6},{8,10},{9,11},{10,... | collective-permute-start | bytes 835592 | tf_op jit(solution)/shard_map/ppermute | solution.py:408
  9.5 6.6 %collective-permute-start.5 = (bf16[64,2176]{1,0:T(8,128)(2,1)S(1)}, bf16[64,2176]{1,0:T(8,128)(2,1)S(1)}, u32[]{:S(2)}, u32[]{:S(2)}) collective-permute-start(bf16[64,2176]{1,0:T(8,128)(2,1)S(1)} %collective-permute-done.1.refs_1_), channel_id=1, source_target_pairs={{0,1},{1,0},{2,3},{3,2},{4,5},{5,4},{6,7},{7,6},{8,10},{9,11},{10,... | collective-permute-start | bytes 835592 | tf_op jit(solution)/shard_map/ppermute | solution.py:408
  11.5 6.6 %collective-permute-start.7 = (bf16[64,2176]{1,0:T(8,128)(2,1)S(1)}, bf16[64,2176]{1,0:T(8,128)(2,1)S(1)}, u32[]{:S(2)}, u32[]{:S(2)}) collective-permute-start(bf16[64,2176]{1,0:T(8,128)(2,1)S(1)} %prepare.1.refs_0_), channel_id=1, source_target_pairs={{0,8},{1,9},{2,10},{3,11},{4,12},{5,13},{6,14},{7,15},{8,0},{9,1},... | collective-permute-start | bytes 835592 | tf_op jit(solution)/shard_map/ppermute | solution.py:408
  11.5 6.7 %collective-permute-start.8 = (bf16[64,2176]{1,0:T(8,128)(2,1)S(1)}, bf16[64,2176]{1,0:T(8,128)(2,1)S(1)}, u32[]{:S(2)}, u32[]{:S(2)}) collective-permute-start(bf16[64,2176]{1,0:T(8,128)(2,1)S(1)} %collective-permute-done.1.refs_1_), channel_id=1, source_target_pairs={{0,8},{1,9},{2,10},{3,11},{4,12},{5,13},{6,14},{7,15},{8,0},{9,1},... | collective-permute-start | bytes 835592 | tf_op jit(solution)/shard_map/ppermute | solution.py:408
  12.0 8.1 %collective-permute-start.9 = (bf16[64,2176]{1,0:T(8,128)(2,1)S(1)}, bf16[64,2176]{1,0:T(8,128)(2,1)S(1)}, u32[]{:S(2)}, u32[]{:S(2)}) collective-permute-start(bf16[64,2176]{1,0:T(8,128)(2,1)S(1)} %collective-permute-done.3.refs_2_), channel_id=1, source_target_pairs={{0,8},{1,9},{2,10},{3,11},{4,12},{5,13},{6,14},{7,15},{8,0},{9,1},... | collective-permute-start | bytes 835592 | tf_op jit(solution)/shard_map/ppermute | solution.py:408
  16.0 17.3 %collective-permute-start = (bf16[64,2176]{1,0:T(8,128)(2,1)S(1)}, bf16[64,2176]{1,0:T(8,128)(2,1)S(1)}, u32[]{:S(2)}, u32[]{:S(2)}) collective-permute-start(bf16[64,2176]{1,0:T(8,128)(2,1)S(1)} %prepare.1.refs_0_), channel_id=1, source_target_pairs={{0,2},{1,3},{2,0},{3,1},{4,6},{5,7},{6,4},{7,5},{8,24},{9,25},{10,... | collective-permute-start | bytes 835592 | tf_op jit(solution)/shard_map/ppermute | solution.py:408
  18.1 15.2 %collective-permute-start.2 = (bf16[64,2176]{1,0:T(8,128)(2,1)S(1)}, bf16[64,2176]{1,0:T(8,128)(2,1)S(1)}, u32[]{:S(2)}, u32[]{:S(2)}) collective-permute-start(bf16[64,2176]{1,0:T(8,128)(2,1)S(1)} %collective-permute-done.1.refs_1_), channel_id=1, source_target_pairs={{0,2},{1,3},{2,0},{3,1},{4,6},{5,7},{6,4},{7,5},{8,24},{9,25},{10,... | collective-permute-start | bytes 835592 | tf_op jit(solution)/shard_map/ppermute | solution.py:408
  18.2 15.1 %collective-permute-start.4 = (bf16[64,2176]{1,0:T(8,128)(2,1)S(1)}, bf16[64,2176]{1,0:T(8,128)(2,1)S(1)}, u32[]{:S(2)}, u32[]{:S(2)}) collective-permute-start(bf16[64,2176]{1,0:T(8,128)(2,1)S(1)} %collective-permute-done.3.refs_2_), channel_id=1, source_target_pairs={{0,2},{1,3},{2,0},{3,1},{4,6},{5,7},{6,4},{7,5},{8,24},{9,25},{10,... | collective-permute-start | bytes 835592 | tf_op jit(solution)/shard_map/ppermute | solution.py:408
  20.2 13.2 %collective-permute-start.6 = (bf16[64,2176]{1,0:T(8,128)(2,1)S(1)}, bf16[64,2176]{1,0:T(8,128)(2,1)S(1)}, u32[]{:S(2)}, u32[]{:S(2)}) collective-permute-start(bf16[64,2176]{1,0:T(8,128)(2,1)S(1)} %collective-permute-done.5.refs_3_), channel_id=1, source_target_pairs={{0,2},{1,3},{2,0},{3,1},{4,6},{5,7},{6,4},{7,5},{8,24},{9,25},{10,... | collective-permute-start | bytes 835592 | tf_op jit(solution)/shard_map/ppermute | solution.py:408
  34.4 15.2 %collective-permute-start.11 = (bf16[256,2048]{1,0:T(8,128)(2,1)S(1)}, bf16[256,2048]{1,0:T(8,128)(2,1)S(1)}, u32[]{:S(2)}, u32[]{:S(2)}) collective-permute-start(bf16[256,2048]{1,0:T(8,128)(2,1)S(1)} %get-tuple-element.53), channel_id=1, source_target_pairs={{0,8},{1,9},{2,10},{3,11},{4,12},{5,13},{6,14},{7,15},{8,0},{9,1},... | collective-permute-start | bytes 3145736 | tf_op jit(solution)/shard_map/ppermute | solution.py:408
  49.9 6.5 %collective-permute-start.13 = (bf16[64,2048]{1,0:T(8,128)(2,1)S(1)}, bf16[64,2048]{1,0:T(8,128)(2,1)S(1)}, u32[]{:S(2)}, u32[]{:S(2)}) collective-permute-start(bf16[64,2048]{1,0:T(8,128)(2,1)S(1)} %get-tuple-element.57), channel_id=1, source_target_pairs={{0,1},{1,0},{2,3},{3,2},{4,5},{5,4},{6,7},{7,6},{8,10},{9,11},{10,... | collective-permute-start | bytes 786440 | tf_op jit(solution)/shard_map/ppermute | solution.py:408
  52.4 7.0 %collective-permute-start.20 = (bf16[64,2048]{1,0:T(8,128)(2,1)S(1)}, bf16[64,2048]{1,0:T(8,128)(2,1)S(1)}, u32[]{:S(2)}, u32[]{:S(2)}) collective-permute-start(bf16[64,2048]{1,0:T(8,128)(2,1)S(1)} %get-tuple-element.68), channel_id=1, source_target_pairs={{0,1},{1,0},{2,3},{3,2},{4,5},{5,4},{6,7},{7,6},{8,10},{9,11},{10,... | collective-permute-start | bytes 786440 | tf_op jit(solution)/shard_map/ppermute | solution.py:408
  54.4 10.4 %collective-permute-start.22 = (bf16[64,2048]{1,0:T(8,128)(2,1)S(1)}, bf16[64,2048]{1,0:T(8,128)(2,1)S(1)}, u32[]{:S(2)}, u32[]{:S(2)}) collective-permute-start(bf16[64,2048]{1,0:T(8,128)(2,1)S(1)} %get-tuple-element.70), channel_id=1, source_target_pairs={{0,1},{1,0},{2,3},{3,2},{4,5},{5,4},{6,7},{7,6},{8,10},{9,11},{10,... | collective-permute-start | bytes 786440 | tf_op jit(solution)/shard_map/ppermute | solution.py:408
  54.5 19.1 %collective-permute-start.12 = (bf16[64,2048]{1,0:T(8,128)(2,1)S(1)}, bf16[64,2048]{1,0:T(8,128)(2,1)S(1)}, u32[]{:S(2)}, u32[]{:S(2)}) collective-permute-start(bf16[64,2048]{1,0:T(8,128)(2,1)S(1)} %get-tuple-element.55), channel_id=1, source_target_pairs={{0,1},{1,0},{2,3},{3,2},{4,5},{5,4},{6,7},{7,6},{8,10},{9,11},{10,... | collective-permute-start | bytes 786440 | tf_op jit(solution)/shard_map/ppermute | solution.py:408
  56.5 17.1 %collective-permute-start.14 = (bf16[64,2048]{1,0:T(8,128)(2,1)S(1)}, bf16[64,2048]{1,0:T(8,128)(2,1)S(1)}, u32[]{:S(2)}, u32[]{:S(2)}) collective-permute-start(bf16[64,2048]{1,0:T(8,128)(2,1)S(1)} %add_blocks.6), channel_id=1, source_target_pairs={{0,16},{1,17},{2,18},{3,19},{4,20},{5,21},{6,22},{7,23},{8,9},{9,8... | collective-permute-start | bytes 786440 | tf_op jit(solution)/shard_map/ppermute | solution.py:408
  59.5 14.1 %collective-permute-start.21 = (bf16[64,2048]{1,0:T(8,128)(2,1)S(1)}, bf16[64,2048]{1,0:T(8,128)(2,1)S(1)}, u32[]{:S(2)}, u32[]{:S(2)}) collective-permute-start(bf16[64,2048]{1,0:T(8,128)(2,1)S(1)} %add_blocks.8), channel_id=1, source_target_pairs={{0,2},{1,3},{2,0},{3,1},{4,6},{5,7},{6,4},{7,5},{8,24},{9,25},{10,... | collective-permute-start | bytes 786440 | tf_op jit(solution)/shard_map/ppermute | solution.py:408
  64.8 8.8 %collective-permute-start.23 = (bf16[64,2048]{1,0:T(8,128)(2,1)S(1)}, bf16[64,2048]{1,0:T(8,128)(2,1)S(1)}, u32[]{:S(2)}, u32[]{:S(2)}) collective-permute-start(bf16[64,2048]{1,0:T(8,128)(2,1)S(1)} %add_blocks.9), channel_id=1, source_target_pairs={{0,18},{1,19},{2,16},{3,17},{4,22},{5,23},{6,20},{7,21},{8,25},{9,... | collective-permute-start | bytes 786440 | tf_op jit(solution)/shard_map/ppermute | solution.py:408
  75.2 11.2 %collective-permute-start.24 = (bf16[64,2048]{1,0:T(8,128)(2,1)S(1)}, bf16[64,2048]{1,0:T(8,128)(2,1)S(1)}, u32[]{:S(2)}, u32[]{:S(2)}) collective-permute-start(bf16[64,2048]{1,0:T(8,128)(2,1)S(1)} %get-tuple-element.78.refs_0_), channel_id=1, source_target_pairs={{0,4},{1,5},{2,6},{3,7},{4,0},{5,1},{6,2},{7,3},{8,12},{9,13},{10,... | collective-permute-start | bytes 786440 | tf_op jit(solution)/shard_map/ppermute | solution.py:408
  77.7 9.4 %collective-permute-start.25 = (bf16[64,2048]{1,0:T(8,128)(2,1)S(1)}, bf16[64,2048]{1,0:T(8,128)(2,1)S(1)}, u32[]{:S(2)}, u32[]{:S(2)}) collective-permute-start(bf16[64,2048]{1,0:T(8,128)(2,1)S(1)} %get-tuple-element.78.refs_0_), channel_id=1, source_target_pairs={{0,2},{1,3},{2,0},{3,1},{4,6},{5,7},{6,4},{7,5},{8,10},{9,11},{10,... | collective-permute-start | bytes 786440 | tf_op jit(solution)/shard_map/ppermute | solution.py:408
  78.2 8.9 %collective-permute-start.26 = (bf16[64,2048]{1,0:T(8,128)(2,1)S(1)}, bf16[64,2048]{1,0:T(8,128)(2,1)S(1)}, u32[]{:S(2)}, u32[]{:S(2)}) collective-permute-start(bf16[64,2048]{1,0:T(8,128)(2,1)S(1)} %get-tuple-element.78.refs_0_), channel_id=1, source_target_pairs={{0,1},{1,0},{2,3},{3,2},{4,5},{5,4},{6,7},{7,6},{8,9},{9,8},{10,11... | collective-permute-start | bytes 786440 | tf_op jit(solution)/shard_map/ppermute | solution.py:408
  87.1 7.4 %collective-permute-start.28 = (bf16[64,2048]{1,0:T(8,128)(2,1)S(1)}, bf16[64,2048]{1,0:T(8,128)(2,1)S(1)}, u32[]{:S(2)}, u32[]{:S(2)}) collective-permute-start(bf16[64,2048]{1,0:T(8,128)(2,1)S(1)} %collective-permute-done.24.refs_3_), channel_id=1, source_target_pairs={{0,2},{1,3},{2,0},{3,1},{4,6},{5,7},{6,4},{7,5},{8,9},{9,8},{10,11... | collective-permute-start | bytes 786440 | tf_op jit(solution)/shard_map/ppermute | solution.py:408
  88.0 8.0 %collective-permute-start.27 = (bf16[64,2048]{1,0:T(8,128)(2,1)S(1)}, bf16[64,2048]{1,0:T(8,128)(2,1)S(1)}, u32[]{:S(2)}, u32[]{:S(2)}) collective-permute-start(bf16[64,2048]{1,0:T(8,128)(2,1)S(1)} %collective-permute-done.24.refs_3_), channel_id=1, source_target_pairs={{0,1},{1,0},{2,3},{3,2},{4,5},{5,4},{6,7},{7,6},{8,10},{9,11},{10,... | collective-permute-start | bytes 786440 | tf_op jit(solution)/shard_map/ppermute | solution.py:408
  88.5 14.0 %collective-permute-start.33 = (bf16[64,2048]{1,0:T(8,128)(2,1)S(1)}, bf16[64,2048]{1,0:T(8,128)(2,1)S(1)}, u32[]{:S(2)}, u32[]{:S(2)}) collective-permute-start(bf16[64,2048]{1,0:T(8,128)(2,1)S(1)} %collective-permute-done.25.refs_1_), channel_id=1, source_target_pairs={{0,1},{1,0},{2,3},{3,2},{4,5},{5,4},{6,7},{7,6},{8,9},{9,8},{10,11... | collective-permute-start | bytes 786440 | tf_op jit(solution)/shard_map/ppermute | solution.py:408
  94.5 8.1 %collective-permute-start.32 = (bf16[64,2048]{1,0:T(8,128)(2,1)S(1)}, bf16[64,2048]{1,0:T(8,128)(2,1)S(1)}, u32[]{:S(2)}, u32[]{:S(2)}) collective-permute-start(bf16[64,2048]{1,0:T(8,128)(2,1)S(1)} %collective-permute-done.28.refs_2_), channel_id=1, source_target_pairs={{0,1},{1,0},{2,3},{3,2},{4,5},{5,4},{6,7},{7,6},{8,10},{9,11},{10,... | collective-permute-start | bytes 786440 | tf_op jit(solution)/shard_map/ppermute | solution.py:408
  98.4 12.2 %collective-permute-start.29 = (f32[1,64]{1,0:T(1,128)S(1)}, f32[1,64]{1,0:T(1,128)S(1)}, u32[]{:S(2)}, u32[]{:S(2)}) collective-permute-start(f32[1,64]{1,0:T(1,128)S(1)} %get-tuple-element.93), channel_id=1, source_target_pairs={{0,2},{1,3},{2,0},{3,1},{4,6},{5,7},{6,4},{7,5},{8,10},{9,11},{10,... | collective-permute-start | bytes 776 | tf_op jit(solution)/shard_map/ppermute | solution.py:408
  100.2 12.0 %collective-permute-start.30 = (f32[1,64]{1,0:T(1,128)S(1)}, f32[1,64]{1,0:T(1,128)S(1)}, u32[]{:S(2)}, u32[]{:S(2)}) collective-permute-start(f32[1,64]{1,0:T(1,128)S(1)} %get-tuple-element.92), channel_id=1, source_target_pairs={{0,1},{1,0},{2,3},{3,2},{4,5},{5,4},{6,7},{7,6},{8,9},{9,8},{10,11... | collective-permute-start | bytes 776 | tf_op jit(solution)/shard_map/ppermute | solution.py:408
  100.2 14.1 %collective-permute-start.31 = (f32[1,64]{1,0:T(1,128)S(1)}, f32[1,64]{1,0:T(1,128)S(1)}, u32[]{:S(2)}, u32[]{:S(2)}) collective-permute-start(f32[1,64]{1,0:T(1,128)S(1)} %get-tuple-element.91), channel_id=1, source_target_pairs={{0,4},{1,5},{2,6},{3,7},{4,0},{5,1},{6,2},{7,3},{8,12},{9,13},{10,... | collective-permute-start | bytes 776 | tf_op jit(solution)/shard_map/ppermute | solution.py:408
  107.1 7.2 %collective-permute-start.34 = (f32[1,64]{1,0:T(1,128)S(1)}, f32[1,64]{1,0:T(1,128)S(1)}, u32[]{:S(2)}, u32[]{:S(2)}) collective-permute-start(f32[1,64]{1,0:T(1,128)S(1)} %get-tuple-element.90), channel_id=1, source_target_pairs={{0,7},{1,6},{2,5},{3,4},{4,3},{5,2},{6,1},{7,0},{8,15},{9,14},{10,... | collective-permute-start | bytes 776 | tf_op jit(solution)/shard_map/ppermute | solution.py:408
  109.9 5.3 %collective-permute-start.35 = (f32[1,64]{1,0:T(1,128)S(1)}, f32[1,64]{1,0:T(1,128)S(1)}, u32[]{:S(2)}, u32[]{:S(2)}) collective-permute-start(f32[1,64]{1,0:T(1,128)S(1)} %get-tuple-element.89), channel_id=1, source_target_pairs={{0,5},{1,4},{2,7},{3,6},{4,1},{5,0},{6,3},{7,2},{8,14},{9,15},{10,... | collective-permute-start | bytes 776 | tf_op jit(solution)/shard_map/ppermute | solution.py:408
  110.6 5.3 %collective-permute-start.36 = (f32[1,64]{1,0:T(1,128)S(1)}, f32[1,64]{1,0:T(1,128)S(1)}, u32[]{:S(2)}, u32[]{:S(2)}) collective-permute-start(f32[1,64]{1,0:T(1,128)S(1)} %get-tuple-element.88), channel_id=1, source_target_pairs={{0,6},{1,7},{2,4},{3,5},{4,2},{5,3},{6,0},{7,1},{8,13},{9,12},{10,... | collective-permute-start | bytes 776 | tf_op jit(solution)/shard_map/ppermute | solution.py:408
  112.2 4.4 %collective-permute-start.37 = (f32[1,64]{1,0:T(1,128)S(1)}, f32[1,64]{1,0:T(1,128)S(1)}, u32[]{:S(2)}, u32[]{:S(2)}) collective-permute-start(f32[1,64]{1,0:T(1,128)S(1)} %get-tuple-element.87), channel_id=1, source_target_pairs={{0,3},{1,2},{2,1},{3,0},{4,7},{5,6},{6,5},{7,4},{8,11},{9,10},{10,... | collective-permute-start | bytes 776 | tf_op jit(solution)/shard_map/ppermute | solution.py:408
  (9 other events, 32.1 us)

commit v5 on v4

--- a/solution.py
+++ b/solution.py
@@ -430,16 +430,16 @@
     far, near_out = lax.optimization_barrier((far, near_out))
     far += [send(b, core) for b in far]
     *far_out, far_other = run_expert(expert, far, weights, cap)
-    near_sum = add_blocks(near_out, [send(near_other, core)])
-    n3 = hop(near_sum[3], 1)
-    n2 = hop(near_sum[2], 1)
-    n1 = hop(add_blocks([near_sum[1]], [n3])[0], 0)
     words_first = fetch(head_weight.T, far_other)
     far_sum = add_blocks(far_out, [send(far_other, core)])
     f3 = hop(far_sum[3], 1)
     f2 = hop(far_sum[2], 1)
     f1 = hop(add_blocks([far_sum[1]], [f3])[0], 0, 2)
     f0 = hop(add_blocks([far_sum[0]], [f2])[0], 2)
+    near_sum = add_blocks(near_out, [send(near_other, core)])
+    n3 = hop(near_sum[3], 1)
+    n2 = hop(near_sum[2], 1)
+    n1 = hop(add_blocks([near_sum[1]], [n3])[0], 0)
     parts = [near_sum[0], n2, n1, f0, f1]
     for d in reversed(extra):
         merged = sum(p.astype(F32) for p in parts).astype(BF16)

time: 118 us -> 118 us (level)
  no operation moved by 1% of the time
where the time goes in v5:
time: 118 us
  starting transfers between devices  46.1 us (39%)
  Pallas kernels  46 us (39%)
  waiting for transfers between devices  24.8 us (21%)
    ppermute x38, starting transfers between devices, send(): return lax.ppermute(x, AXES, pairs)  46.1 us
    pallas_call x2, Pallas kernels, run_expert(): pl.pallas_call(functools.partial(expert_kernel, blocks, slots), in_specs=...  26.3 us
    ppermute x38, waiting for transfers between devices, send(): return lax.ppermute(x, AXES, pairs)  24.8 us
    pallas_call x3, Pallas kernels, peaks(): pl.pallas_call(functools.partial(peak_kernel, blocks, start, stop), in_sp...  9.31 us
    pallas_call x1, Pallas kernels, fetch(): pl.pallas_call(functools.partial(fetch_kernel, parts), in_specs=[pl.Block...  5.8 us
  transfers between devices with their start and end apart: 38, of which 15 were waited for; matrix products, arithmetic and copies ran while one was open for 0% of the time, Pallas kernels for 36%

profile of v5, /device:TPU:0, one launch (start us, length us, event | category | flops | bytes accessed | tf_op | source)
XLA Modules:
  0.0 117.8 jit_solution(11848776971766832492)
XLA Ops:
  1.9 3.0 %collective-permute-start.1 = (bf16[64,2176]{1,0:T(8,128)(2,1)S(1)}, bf16[64,2176]{1,0:T(8,128)(2,1)S(1)}, u32[]{:S(2)}, u32[]{:S(2)}) collective-permute-start(bf16[64,2176]{1,0:T(8,128)(2,1)S(1)} %prepare.1.refs_0_), channel_id=1, source_target_pairs={{0,16},{1,17},{2,18},{3,19},{4,20},{5,21},{6,22},{7,23},{8,9},{9,8... | collective-permute-start | bytes 835592 | tf_op jit(solution)/shard_map/ppermute | solution.py:408
  4.9 1.5 %collective-permute-start.3 = (bf16[64,2176]{1,0:T(8,128)(2,1)S(1)}, bf16[64,2176]{1,0:T(8,128)(2,1)S(1)}, u32[]{:S(2)}, u32[]{:S(2)}) collective-permute-start(bf16[64,2176]{1,0:T(8,128)(2,1)S(1)} %prepare.1.refs_0_), channel_id=1, source_target_pairs={{0,1},{1,0},{2,3},{3,2},{4,5},{5,4},{6,7},{7,6},{8,10},{9,11},{10,... | collective-permute-start | bytes 835592 | tf_op jit(solution)/shard_map/ppermute | solution.py:408
  6.4 3.0 %collective-permute-done.1.refs_1_ = bf16[64,2176]{1,0:T(8,128)(2,1)S(1)} collective-permute-done((bf16[64,2176]{1,0:T(8,128)(2,1)S(1)}, bf16[64,2176]{1,0:T(8,128)(2,1)S(1)}, u32[]{:S(2)}, u32[]{:S(2)}) %collective-permute-start.1) | collective-permute-done | bytes 278560 | tf_op jit(solution)/shard_map/ppermute | solution.py:408
  9.5 2.0 %collective-permute-start.5 = (bf16[64,2176]{1,0:T(8,128)(2,1)S(1)}, bf16[64,2176]{1,0:T(8,128)(2,1)S(1)}, u32[]{:S(2)}, u32[]{:S(2)}) collective-permute-start(bf16[64,2176]{1,0:T(8,128)(2,1)S(1)} %collective-permute-done.1.refs_1_), channel_id=1, source_target_pairs={{0,1},{1,0},{2,3},{3,2},{4,5},{5,4},{6,7},{7,6},{8,10},{9,11},{10,... | collective-permute-start | bytes 835592 | tf_op jit(solution)/shard_map/ppermute | solution.py:408
  12.0 4.0 %collective-permute-done.5.refs_3_ = bf16[64,2176]{1,0:T(8,128)(2,1)S(1)} collective-permute-done((bf16[64,2176]{1,0:T(8,128)(2,1)S(1)}, bf16[64,2176]{1,0:T(8,128)(2,1)S(1)}, u32[]{:S(2)}, u32[]{:S(2)}) %collective-permute-start.5) | collective-permute-done | bytes 278560 | tf_op jit(solution)/shard_map/ppermute | solution.py:408
  16.0 2.1 %collective-permute-start = (bf16[64,2176]{1,0:T(8,128)(2,1)S(1)}, bf16[64,2176]{1,0:T(8,128)(2,1)S(1)}, u32[]{:S(2)}, u32[]{:S(2)}) collective-permute-start(bf16[64,2176]{1,0:T(8,128)(2,1)S(1)} %prepare.1.refs_0_), channel_id=1, source_target_pairs={{0,2},{1,3},{2,0},{3,1},{4,6},{5,7},{6,4},{7,5},{8,24},{9,25},{10,... | collective-permute-start | bytes 835592 | tf_op jit(solution)/shard_map/ppermute | solution.py:408
  18.2 2.0 %collective-permute-start.4 = (bf16[64,2176]{1,0:T(8,128)(2,1)S(1)}, bf16[64,2176]{1,0:T(8,128)(2,1)S(1)}, u32[]{:S(2)}, u32[]{:S(2)}) collective-permute-start(bf16[64,2176]{1,0:T(8,128)(2,1)S(1)} %collective-permute-done.3.refs_2_), channel_id=1, source_target_pairs={{0,2},{1,3},{2,0},{3,1},{4,6},{5,7},{6,4},{7,5},{8,24},{9,25},{10,... | collective-permute-start | bytes 835592 | tf_op jit(solution)/shard_map/ppermute | solution.py:408
  20.2 13.1 %expert.2 = (bf16[64,2048]{1,0:T(8,128)(2,1)S(1)}, bf16[64,2048]{1,0:T(8,128)(2,1)S(1)}, bf16[64,2048]{1,0:T(8,128)(2,1)S(1)}, bf16[64,2048]{1,0:T(8,128)(2,1)S(1)}, bf16[256,2048]{1,0:T(8,128)(2,1)S(1)}) custom-call(s32[1]{0:T(128)} %bitcast.3.expert_ref, bf16[64,2176]{1,0:T(8,128)(2,1)S(1)} %prepare.1.refs_0_, ...), custom_call_target="tpu_custom_call" | custom-call | flops 1 | bytes 1 | tf_op jit(solution)/shard_map/expert/pallas_call | solution.py:234
  36.1 13.3 %expert.3 = (bf16[64,2048]{1,0:T(8,128)(2,1)S(1)}, bf16[64,2048]{1,0:T(8,128)(2,1)S(1)}, bf16[64,2048]{1,0:T(8,128)(2,1)S(1)}, bf16[64,2048]{1,0:T(8,128)(2,1)S(1)}, bf16[256,2048]{1,0:T(8,128)(2,1)S(1)}) custom-call(s32[1]{0:T(128)} %bitcast.3.expert_ref, bf16[64,2176]{1,0:T(8,128)(2,1)S(1)} %collective-permute-done.refs_0_, ...), custom_call_target="tpu_custom_call" | custom-call | flops 1 | bytes 1 | tf_op jit(solution)/shard_map/expert/pallas_call | solution.py:234
  49.9 2.0 %collective-permute-start.13 = (bf16[64,2048]{1,0:T(8,128)(2,1)S(1)}, bf16[64,2048]{1,0:T(8,128)(2,1)S(1)}, u32[]{:S(2)}, u32[]{:S(2)}) collective-permute-start(bf16[64,2048]{1,0:T(8,128)(2,1)S(1)} %get-tuple-element.57), channel_id=1, source_target_pairs={{0,1},{1,0},{2,3},{3,2},{4,5},{5,4},{6,7},{7,6},{8,10},{9,11},{10,... | collective-permute-start | bytes 786440 | tf_op jit(solution)/shard_map/ppermute | solution.py:408
  52.4 2.0 %collective-permute-start.20 = (bf16[64,2048]{1,0:T(8,128)(2,1)S(1)}, bf16[64,2048]{1,0:T(8,128)(2,1)S(1)}, u32[]{:S(2)}, u32[]{:S(2)}) collective-permute-start(bf16[64,2048]{1,0:T(8,128)(2,1)S(1)} %get-tuple-element.68), channel_id=1, source_target_pairs={{0,1},{1,0},{2,3},{3,2},{4,5},{5,4},{6,7},{7,6},{8,10},{9,11},{10,... | collective-permute-start | bytes 786440 | tf_op jit(solution)/shard_map/ppermute | solution.py:408
  54.5 1.9 %collective-permute-start.12 = (bf16[64,2048]{1,0:T(8,128)(2,1)S(1)}, bf16[64,2048]{1,0:T(8,128)(2,1)S(1)}, u32[]{:S(2)}, u32[]{:S(2)}) collective-permute-start(bf16[64,2048]{1,0:T(8,128)(2,1)S(1)} %get-tuple-element.55), channel_id=1, source_target_pairs={{0,1},{1,0},{2,3},{3,2},{4,5},{5,4},{6,7},{7,6},{8,10},{9,11},{10,... | collective-permute-start | bytes 786440 | tf_op jit(solution)/shard_map/ppermute | solution.py:408
  56.5 1.8 %collective-permute-start.14 = (bf16[64,2048]{1,0:T(8,128)(2,1)S(1)}, bf16[64,2048]{1,0:T(8,128)(2,1)S(1)}, u32[]{:S(2)}, u32[]{:S(2)}) collective-permute-start(bf16[64,2048]{1,0:T(8,128)(2,1)S(1)} %add_blocks.6), channel_id=1, source_target_pairs={{0,16},{1,17},{2,18},{3,19},{4,20},{5,21},{6,22},{7,23},{8,9},{9,8... | collective-permute-start | bytes 786440 | tf_op jit(solution)/shard_map/ppermute | solution.py:408
  59.5 2.2 %collective-permute-start.21 = (bf16[64,2048]{1,0:T(8,128)(2,1)S(1)}, bf16[64,2048]{1,0:T(8,128)(2,1)S(1)}, u32[]{:S(2)}, u32[]{:S(2)}) collective-permute-start(bf16[64,2048]{1,0:T(8,128)(2,1)S(1)} %add_blocks.8), channel_id=1, source_target_pairs={{0,2},{1,3},{2,0},{3,1},{4,6},{5,7},{6,4},{7,5},{8,24},{9,25},{10,... | collective-permute-start | bytes 786440 | tf_op jit(solution)/shard_map/ppermute | solution.py:408
  61.7 3.0 %collective-permute-done.22.refs_1_ = bf16[64,2048]{1,0:T(8,128)(2,1)S(1)} collective-permute-done((bf16[64,2048]{1,0:T(8,128)(2,1)S(1)}, bf16[64,2048]{1,0:T(8,128)(2,1)S(1)}, u32[]{:S(2)}, u32[]{:S(2)}) %collective-permute-start.22) | collective-permute-done | bytes 262176 | tf_op jit(solution)/shard_map/ppermute | solution.py:408
  64.8 3.0 %collective-permute-start.23 = (bf16[64,2048]{1,0:T(8,128)(2,1)S(1)}, bf16[64,2048]{1,0:T(8,128)(2,1)S(1)}, u32[]{:S(2)}, u32[]{:S(2)}) collective-permute-start(bf16[64,2048]{1,0:T(8,128)(2,1)S(1)} %add_blocks.9), channel_id=1, source_target_pairs={{0,18},{1,19},{2,16},{3,17},{4,22},{5,23},{6,20},{7,21},{8,25},{9,... | collective-permute-start | bytes 786440 | tf_op jit(solution)/shard_map/ppermute | solution.py:408
  67.8 5.8 %fetch.1.refs_4_ = bf16[4000,2048]{1,0:T(8,128)(2,1)S(1)} custom-call(bf16[4000,2048]{1,0:T(8,128)(2,1)} %bitcast.8, bf16[256,2048]{1,0:T(8,128)(2,1)S(1)} %get-tuple-element.66.after_ref), custom_call_target="tpu_custom_call" | custom-call | flops 1 | bytes 1 | tf_op jit(solution)/shard_map/fetch/pallas_call | solution.py:129
  73.7 1.5 %finish.1 = (bf16[64,2048]{1,0:T(8,128)(2,1)}, bf16[64,2048]{1,0:T(8,128)(2,1)S(1)}, f32[1,4]{1,0:T(1,128)}) custom-call(s32[1,4]{1,0:T(1,128)S(1)} %copy-done.2, bf16[64,2048]{1,0:T(8,128)(2,1)S(1)} %copy-done, f32[1,2048]{1,0:T(1,128)S(1)} %bitcast.7, bf16[64,2048]{1,0:T(8,128)(2,1)S(1)} %get-tuple-element.71.refs_0_, ...), custom_call_target="tpu_custom_call" | custom-call | tf_op jit(solution)/shard_map/finish/pallas_call | solution.py:303
  75.2 2.6 %collective-permute-start.24 = (bf16[64,2048]{1,0:T(8,128)(2,1)S(1)}, bf16[64,2048]{1,0:T(8,128)(2,1)S(1)}, u32[]{:S(2)}, u32[]{:S(2)}) collective-permute-start(bf16[64,2048]{1,0:T(8,128)(2,1)S(1)} %get-tuple-element.78.refs_0_), channel_id=1, source_target_pairs={{0,4},{1,5},{2,6},{3,7},{4,0},{5,1},{6,2},{7,3},{8,12},{9,13},{10,... | collective-permute-start | bytes 786440 | tf_op jit(solution)/shard_map/ppermute | solution.py:408
  78.2 1.5 %collective-permute-start.26 = (bf16[64,2048]{1,0:T(8,128)(2,1)S(1)}, bf16[64,2048]{1,0:T(8,128)(2,1)S(1)}, u32[]{:S(2)}, u32[]{:S(2)}) collective-permute-start(bf16[64,2048]{1,0:T(8,128)(2,1)S(1)} %get-tuple-element.78.refs_0_), channel_id=1, source_target_pairs={{0,1},{1,0},{2,3},{3,2},{4,5},{5,4},{6,7},{7,6},{8,9},{9,8},{10,11... | collective-permute-start | bytes 786440 | tf_op jit(solution)/shard_map/ppermute | solution.py:408
  79.7 6.6 %collective-permute-done.24.refs_3_ = bf16[64,2048]{1,0:T(8,128)(2,1)S(1)} collective-permute-done((bf16[64,2048]{1,0:T(8,128)(2,1)S(1)}, bf16[64,2048]{1,0:T(8,128)(2,1)S(1)}, u32[]{:S(2)}, u32[]{:S(2)}) %collective-permute-start.24) | collective-permute-done | bytes 262176 | tf_op jit(solution)/shard_map/ppermute | solution.py:408
  88.5 1.5 %collective-permute-start.33 = (bf16[64,2048]{1,0:T(8,128)(2,1)S(1)}, bf16[64,2048]{1,0:T(8,128)(2,1)S(1)}, u32[]{:S(2)}, u32[]{:S(2)}) collective-permute-start(bf16[64,2048]{1,0:T(8,128)(2,1)S(1)} %collective-permute-done.25.refs_1_), channel_id=1, source_target_pairs={{0,1},{1,0},{2,3},{3,2},{4,5},{5,4},{6,7},{7,6},{8,9},{9,8},{10,11... | collective-permute-start | bytes 786440 | tf_op jit(solution)/shard_map/ppermute | solution.py:408
  90.0 2.4 %peaks.3.refs_5_ = f32[4,64]{1,0:T(4,128)S(1)} custom-call(bf16[64,2048]{1,0:T(8,128)(2,1)S(1)} %get-tuple-element.78.refs_0_, bf16[64,2048]{1,0:T(8,128)(2,1)S(1)} %collective-permute-done.25.refs_1_, bf16[64,2048]{1,0:T(8,128)(2,1)S(1)} %collective-permute-done.26.refs_2_, bf16[64,2048]{1,0:T(8,128)(2,1)S(1)} %collective-permute-done.24.refs_3_, ...), custom_call_target="tpu_custom_call" | custom-call | flops 1 | bytes 1 | tf_op jit(solution)/shard_map/peaks/pallas_call | solution.py:373
  92.5 2.0 %collective-permute-done.28.refs_2_ = bf16[64,2048]{1,0:T(8,128)(2,1)S(1)} collective-permute-done((bf16[64,2048]{1,0:T(8,128)(2,1)S(1)}, bf16[64,2048]{1,0:T(8,128)(2,1)S(1)}, u32[]{:S(2)}, u32[]{:S(2)}) %collective-permute-start.28) | collective-permute-done | bytes 262176 | tf_op jit(solution)/shard_map/ppermute | solution.py:408
  94.5 1.5 %collective-permute-start.32 = (bf16[64,2048]{1,0:T(8,128)(2,1)S(1)}, bf16[64,2048]{1,0:T(8,128)(2,1)S(1)}, u32[]{:S(2)}, u32[]{:S(2)}) collective-permute-start(bf16[64,2048]{1,0:T(8,128)(2,1)S(1)} %collective-permute-done.28.refs_2_), channel_id=1, source_target_pairs={{0,1},{1,0},{2,3},{3,2},{4,5},{5,4},{6,7},{7,6},{8,10},{9,11},{10,... | collective-permute-start | bytes 786440 | tf_op jit(solution)/shard_map/ppermute | solution.py:408
  96.0 2.4 %peaks.4 = f32[4,64]{1,0:T(4,128)S(1)} custom-call(bf16[64,2048]{1,0:T(8,128)(2,1)S(1)} %get-tuple-element.78.refs_0_, bf16[64,2048]{1,0:T(8,128)(2,1)S(1)} %collective-permute-done.25.refs_1_, bf16[64,2048]{1,0:T(8,128)(2,1)S(1)} %collective-permute-done.26.refs_2_, bf16[64,2048]{1,0:T(8,128)(2,1)S(1)} %collective-permute-done.24.refs_3_, ...), custom_call_target="tpu_custom_call" | custom-call | flops 1 | bytes 1 | tf_op jit(solution)/shard_map/peaks/pallas_call | solution.py:373
  98.4 1.8 %collective-permute-start.29 = (f32[1,64]{1,0:T(1,128)S(1)}, f32[1,64]{1,0:T(1,128)S(1)}, u32[]{:S(2)}, u32[]{:S(2)}) collective-permute-start(f32[1,64]{1,0:T(1,128)S(1)} %get-tuple-element.93), channel_id=1, source_target_pairs={{0,2},{1,3},{2,0},{3,1},{4,6},{5,7},{6,4},{7,5},{8,10},{9,11},{10,... | collective-permute-start | bytes 776 | tf_op jit(solution)/shard_map/ppermute | solution.py:408
  100.2 2.4 %collective-permute-start.31 = (f32[1,64]{1,0:T(1,128)S(1)}, f32[1,64]{1,0:T(1,128)S(1)}, u32[]{:S(2)}, u32[]{:S(2)}) collective-permute-start(f32[1,64]{1,0:T(1,128)S(1)} %get-tuple-element.91), channel_id=1, source_target_pairs={{0,4},{1,5},{2,6},{3,7},{4,0},{5,1},{6,2},{7,3},{8,12},{9,13},{10,... | collective-permute-start | bytes 776 | tf_op jit(solution)/shard_map/ppermute | solution.py:408
  102.6 4.5 %peaks.5 = f32[4,64]{1,0:T(4,128)S(1)} custom-call(bf16[64,2048]{1,0:T(8,128)(2,1)S(1)} %collective-permute-done.32.refs_0_, bf16[64,2048]{1,0:T(8,128)(2,1)S(1)} %collective-permute-done.27.refs_1_, bf16[64,2048]{1,0:T(8,128)(2,1)S(1)} %collective-permute-done.28.refs_2_, bf16[64,2048]{1,0:T(8,128)(2,1)S(1)} %collective-permute-done.33.refs_3_, ...), custom_call_target="tpu_custom_call" | custom-call | flops 1 | bytes 1 | tf_op jit(solution)/shard_map/peaks/pallas_call | solution.py:373
  107.1 2.8 %collective-permute-start.34 = (f32[1,64]{1,0:T(1,128)S(1)}, f32[1,64]{1,0:T(1,128)S(1)}, u32[]{:S(2)}, u32[]{:S(2)}) collective-permute-start(f32[1,64]{1,0:T(1,128)S(1)} %get-tuple-element.90), channel_id=1, source_target_pairs={{0,7},{1,6},{2,5},{3,4},{4,3},{5,2},{6,1},{7,0},{8,15},{9,14},{10,... | collective-permute-start | bytes 776 | tf_op jit(solution)/shard_map/ppermute | solution.py:408
  110.6 1.6 %collective-permute-start.36 = (f32[1,64]{1,0:T(1,128)S(1)}, f32[1,64]{1,0:T(1,128)S(1)}, u32[]{:S(2)}, u32[]{:S(2)}) collective-permute-start(f32[1,64]{1,0:T(1,128)S(1)} %get-tuple-element.88), channel_id=1, source_target_pairs={{0,6},{1,7},{2,4},{3,5},{4,2},{5,3},{6,0},{7,1},{8,13},{9,12},{10,... | collective-permute-start | bytes 776 | tf_op jit(solution)/shard_map/ppermute | solution.py:408
  112.2 2.1 %collective-permute-start.37 = (f32[1,64]{1,0:T(1,128)S(1)}, f32[1,64]{1,0:T(1,128)S(1)}, u32[]{:S(2)}, u32[]{:S(2)}) collective-permute-start(f32[1,64]{1,0:T(1,128)S(1)} %get-tuple-element.87), channel_id=1, source_target_pairs={{0,3},{1,2},{2,1},{3,0},{4,7},{5,6},{6,5},{7,4},{8,11},{9,10},{10,... | collective-permute-start | bytes 776 | tf_op jit(solution)/shard_map/ppermute | solution.py:408
  (66 shorter events, 14.0 us)
Async XLA Ops:
  1.9 7.5 %collective-permute-start.1 = (bf16[64,2176]{1,0:T(8,128)(2,1)S(1)}, bf16[64,2176]{1,0:T(8,128)(2,1)S(1)}, u32[]{:S(2)}, u32[]{:S(2)}) collective-permute-start(bf16[64,2176]{1,0:T(8,128)(2,1)S(1)} %prepare.1.refs_0_), channel_id=1, source_target_pairs={{0,16},{1,17},{2,18},{3,19},{4,20},{5,21},{6,22},{7,23},{8,9},{9,8... | collective-permute-start | bytes 835592 | tf_op jit(solution)/shard_map/ppermute | solution.py:408
  4.9 7.1 %collective-permute-start.3 = (bf16[64,2176]{1,0:T(8,128)(2,1)S(1)}, bf16[64,2176]{1,0:T(8,128)(2,1)S(1)}, u32[]{:S(2)}, u32[]{:S(2)}) collective-permute-start(bf16[64,2176]{1,0:T(8,128)(2,1)S(1)} %prepare.1.refs_0_), channel_id=1, source_target_pairs={{0,1},{1,0},{2,3},{3,2},{4,5},{5,4},{6,7},{7,6},{8,10},{9,11},{10,... | collective-permute-start | bytes 835592 | tf_op jit(solution)/shard_map/ppermute | solution.py:408
  9.5 6.6 %collective-permute-start.5 = (bf16[64,2176]{1,0:T(8,128)(2,1)S(1)}, bf16[64,2176]{1,0:T(8,128)(2,1)S(1)}, u32[]{:S(2)}, u32[]{:S(2)}) collective-permute-start(bf16[64,2176]{1,0:T(8,128)(2,1)S(1)} %collective-permute-done.1.refs_1_), channel_id=1, source_target_pairs={{0,1},{1,0},{2,3},{3,2},{4,5},{5,4},{6,7},{7,6},{8,10},{9,11},{10,... | collective-permute-start | bytes 835592 | tf_op jit(solution)/shard_map/ppermute | solution.py:408
  11.5 6.6 %collective-permute-start.7 = (bf16[64,2176]{1,0:T(8,128)(2,1)S(1)}, bf16[64,2176]{1,0:T(8,128)(2,1)S(1)}, u32[]{:S(2)}, u32[]{:S(2)}) collective-permute-start(bf16[64,2176]{1,0:T(8,128)(2,1)S(1)} %prepare.1.refs_0_), channel_id=1, source_target_pairs={{0,8},{1,9},{2,10},{3,11},{4,12},{5,13},{6,14},{7,15},{8,0},{9,1},... | collective-permute-start | bytes 835592 | tf_op jit(solution)/shard_map/ppermute | solution.py:408
  11.5 6.7 %collective-permute-start.8 = (bf16[64,2176]{1,0:T(8,128)(2,1)S(1)}, bf16[64,2176]{1,0:T(8,128)(2,1)S(1)}, u32[]{:S(2)}, u32[]{:S(2)}) collective-permute-start(bf16[64,2176]{1,0:T(8,128)(2,1)S(1)} %collective-permute-done.1.refs_1_), channel_id=1, source_target_pairs={{0,8},{1,9},{2,10},{3,11},{4,12},{5,13},{6,14},{7,15},{8,0},{9,1},... | collective-permute-start | bytes 835592 | tf_op jit(solution)/shard_map/ppermute | solution.py:408
  12.0 8.1 %collective-permute-start.9 = (bf16[64,2176]{1,0:T(8,128)(2,1)S(1)}, bf16[64,2176]{1,0:T(8,128)(2,1)S(1)}, u32[]{:S(2)}, u32[]{:S(2)}) collective-permute-start(bf16[64,2176]{1,0:T(8,128)(2,1)S(1)} %collective-permute-done.3.refs_2_), channel_id=1, source_target_pairs={{0,8},{1,9},{2,10},{3,11},{4,12},{5,13},{6,14},{7,15},{8,0},{9,1},... | collective-permute-start | bytes 835592 | tf_op jit(solution)/shard_map/ppermute | solution.py:408
  16.0 17.3 %collective-permute-start = (bf16[64,2176]{1,0:T(8,128)(2,1)S(1)}, bf16[64,2176]{1,0:T(8,128)(2,1)S(1)}, u32[]{:S(2)}, u32[]{:S(2)}) collective-permute-start(bf16[64,2176]{1,0:T(8,128)(2,1)S(1)} %prepare.1.refs_0_), channel_id=1, source_target_pairs={{0,2},{1,3},{2,0},{3,1},{4,6},{5,7},{6,4},{7,5},{8,24},{9,25},{10,... | collective-permute-start | bytes 835592 | tf_op jit(solution)/shard_map/ppermute | solution.py:408
  18.1 15.2 %collective-permute-start.2 = (bf16[64,2176]{1,0:T(8,128)(2,1)S(1)}, bf16[64,2176]{1,0:T(8,128)(2,1)S(1)}, u32[]{:S(2)}, u32[]{:S(2)}) collective-permute-start(bf16[64,2176]{1,0:T(8,128)(2,1)S(1)} %collective-permute-done.1.refs_1_), channel_id=1, source_target_pairs={{0,2},{1,3},{2,0},{3,1},{4,6},{5,7},{6,4},{7,5},{8,24},{9,25},{10,... | collective-permute-start | bytes 835592 | tf_op jit(solution)/shard_map/ppermute | solution.py:408
  18.2 15.1 %collective-permute-start.4 = (bf16[64,2176]{1,0:T(8,128)(2,1)S(1)}, bf16[64,2176]{1,0:T(8,128)(2,1)S(1)}, u32[]{:S(2)}, u32[]{:S(2)}) collective-permute-start(bf16[64,2176]{1,0:T(8,128)(2,1)S(1)} %collective-permute-done.3.refs_2_), channel_id=1, source_target_pairs={{0,2},{1,3},{2,0},{3,1},{4,6},{5,7},{6,4},{7,5},{8,24},{9,25},{10,... | collective-permute-start | bytes 835592 | tf_op jit(solution)/shard_map/ppermute | solution.py:408
  20.2 13.2 %collective-permute-start.6 = (bf16[64,2176]{1,0:T(8,128)(2,1)S(1)}, bf16[64,2176]{1,0:T(8,128)(2,1)S(1)}, u32[]{:S(2)}, u32[]{:S(2)}) collective-permute-start(bf16[64,2176]{1,0:T(8,128)(2,1)S(1)} %collective-permute-done.5.refs_3_), channel_id=1, source_target_pairs={{0,2},{1,3},{2,0},{3,1},{4,6},{5,7},{6,4},{7,5},{8,24},{9,25},{10,... | collective-permute-start | bytes 835592 | tf_op jit(solution)/shard_map/ppermute | solution.py:408
  34.4 15.2 %collective-permute-start.11 = (bf16[256,2048]{1,0:T(8,128)(2,1)S(1)}, bf16[256,2048]{1,0:T(8,128)(2,1)S(1)}, u32[]{:S(2)}, u32[]{:S(2)}) collective-permute-start(bf16[256,2048]{1,0:T(8,128)(2,1)S(1)} %get-tuple-element.53), channel_id=1, source_target_pairs={{0,8},{1,9},{2,10},{3,11},{4,12},{5,13},{6,14},{7,15},{8,0},{9,1},... | collective-permute-start | bytes 3145736 | tf_op jit(solution)/shard_map/ppermute | solution.py:408
  49.9 6.5 %collective-permute-start.13 = (bf16[64,2048]{1,0:T(8,128)(2,1)S(1)}, bf16[64,2048]{1,0:T(8,128)(2,1)S(1)}, u32[]{:S(2)}, u32[]{:S(2)}) collective-permute-start(bf16[64,2048]{1,0:T(8,128)(2,1)S(1)} %get-tuple-element.57), channel_id=1, source_target_pairs={{0,1},{1,0},{2,3},{3,2},{4,5},{5,4},{6,7},{7,6},{8,10},{9,11},{10,... | collective-permute-start | bytes 786440 | tf_op jit(solution)/shard_map/ppermute | solution.py:408
  52.4 7.0 %collective-permute-start.20 = (bf16[64,2048]{1,0:T(8,128)(2,1)S(1)}, bf16[64,2048]{1,0:T(8,128)(2,1)S(1)}, u32[]{:S(2)}, u32[]{:S(2)}) collective-permute-start(bf16[64,2048]{1,0:T(8,128)(2,1)S(1)} %get-tuple-element.68), channel_id=1, source_target_pairs={{0,1},{1,0},{2,3},{3,2},{4,5},{5,4},{6,7},{7,6},{8,10},{9,11},{10,... | collective-permute-start | bytes 786440 | tf_op jit(solution)/shard_map/ppermute | solution.py:408
  54.4 10.4 %collective-permute-start.22 = (bf16[64,2048]{1,0:T(8,128)(2,1)S(1)}, bf16[64,2048]{1,0:T(8,128)(2,1)S(1)}, u32[]{:S(2)}, u32[]{:S(2)}) collective-permute-start(bf16[64,2048]{1,0:T(8,128)(2,1)S(1)} %get-tuple-element.70), channel_id=1, source_target_pairs={{0,1},{1,0},{2,3},{3,2},{4,5},{5,4},{6,7},{7,6},{8,10},{9,11},{10,... | collective-permute-start | bytes 786440 | tf_op jit(solution)/shard_map/ppermute | solution.py:408
  54.5 19.1 %collective-permute-start.12 = (bf16[64,2048]{1,0:T(8,128)(2,1)S(1)}, bf16[64,2048]{1,0:T(8,128)(2,1)S(1)}, u32[]{:S(2)}, u32[]{:S(2)}) collective-permute-start(bf16[64,2048]{1,0:T(8,128)(2,1)S(1)} %get-tuple-element.55), channel_id=1, source_target_pairs={{0,1},{1,0},{2,3},{3,2},{4,5},{5,4},{6,7},{7,6},{8,10},{9,11},{10,... | collective-permute-start | bytes 786440 | tf_op jit(solution)/shard_map/ppermute | solution.py:408
  56.5 17.1 %collective-permute-start.14 = (bf16[64,2048]{1,0:T(8,128)(2,1)S(1)}, bf16[64,2048]{1,0:T(8,128)(2,1)S(1)}, u32[]{:S(2)}, u32[]{:S(2)}) collective-permute-start(bf16[64,2048]{1,0:T(8,128)(2,1)S(1)} %add_blocks.6), channel_id=1, source_target_pairs={{0,16},{1,17},{2,18},{3,19},{4,20},{5,21},{6,22},{7,23},{8,9},{9,8... | collective-permute-start | bytes 786440 | tf_op jit(solution)/shard_map/ppermute | solution.py:408
  59.5 14.1 %collective-permute-start.21 = (bf16[64,2048]{1,0:T(8,128)(2,1)S(1)}, bf16[64,2048]{1,0:T(8,128)(2,1)S(1)}, u32[]{:S(2)}, u32[]{:S(2)}) collective-permute-start(bf16[64,2048]{1,0:T(8,128)(2,1)S(1)} %add_blocks.8), channel_id=1, source_target_pairs={{0,2},{1,3},{2,0},{3,1},{4,6},{5,7},{6,4},{7,5},{8,24},{9,25},{10,... | collective-permute-start | bytes 786440 | tf_op jit(solution)/shard_map/ppermute | solution.py:408
  64.8 8.8 %collective-permute-start.23 = (bf16[64,2048]{1,0:T(8,128)(2,1)S(1)}, bf16[64,2048]{1,0:T(8,128)(2,1)S(1)}, u32[]{:S(2)}, u32[]{:S(2)}) collective-permute-start(bf16[64,2048]{1,0:T(8,128)(2,1)S(1)} %add_blocks.9), channel_id=1, source_target_pairs={{0,18},{1,19},{2,16},{3,17},{4,22},{5,23},{6,20},{7,21},{8,25},{9,... | collective-permute-start | bytes 786440 | tf_op jit(solution)/shard_map/ppermute | solution.py:408
  75.2 11.2 %collective-permute-start.24 = (bf16[64,2048]{1,0:T(8,128)(2,1)S(1)}, bf16[64,2048]{1,0:T(8,128)(2,1)S(1)}, u32[]{:S(2)}, u32[]{:S(2)}) collective-permute-start(bf16[64,2048]{1,0:T(8,128)(2,1)S(1)} %get-tuple-element.78.refs_0_), channel_id=1, source_target_pairs={{0,4},{1,5},{2,6},{3,7},{4,0},{5,1},{6,2},{7,3},{8,12},{9,13},{10,... | collective-permute-start | bytes 786440 | tf_op jit(solution)/shard_map/ppermute | solution.py:408
  77.7 9.4 %collective-permute-start.25 = (bf16[64,2048]{1,0:T(8,128)(2,1)S(1)}, bf16[64,2048]{1,0:T(8,128)(2,1)S(1)}, u32[]{:S(2)}, u32[]{:S(2)}) collective-permute-start(bf16[64,2048]{1,0:T(8,128)(2,1)S(1)} %get-tuple-element.78.refs_0_), channel_id=1, source_target_pairs={{0,2},{1,3},{2,0},{3,1},{4,6},{5,7},{6,4},{7,5},{8,10},{9,11},{10,... | collective-permute-start | bytes 786440 | tf_op jit(solution)/shard_map/ppermute | solution.py:408
  78.2 8.9 %collective-permute-start.26 = (bf16[64,2048]{1,0:T(8,128)(2,1)S(1)}, bf16[64,2048]{1,0:T(8,128)(2,1)S(1)}, u32[]{:S(2)}, u32[]{:S(2)}) collective-permute-start(bf16[64,2048]{1,0:T(8,128)(2,1)S(1)} %get-tuple-element.78.refs_0_), channel_id=1, source_target_pairs={{0,1},{1,0},{2,3},{3,2},{4,5},{5,4},{6,7},{7,6},{8,9},{9,8},{10,11... | collective-permute-start | bytes 786440 | tf_op jit(solution)/shard_map/ppermute | solution.py:408
  87.1 7.4 %collective-permute-start.28 = (bf16[64,2048]{1,0:T(8,128)(2,1)S(1)}, bf16[64,2048]{1,0:T(8,128)(2,1)S(1)}, u32[]{:S(2)}, u32[]{:S(2)}) collective-permute-start(bf16[64,2048]{1,0:T(8,128)(2,1)S(1)} %collective-permute-done.24.refs_3_), channel_id=1, source_target_pairs={{0,2},{1,3},{2,0},{3,1},{4,6},{5,7},{6,4},{7,5},{8,9},{9,8},{10,11... | collective-permute-start | bytes 786440 | tf_op jit(solution)/shard_map/ppermute | solution.py:408
  88.0 8.0 %collective-permute-start.27 = (bf16[64,2048]{1,0:T(8,128)(2,1)S(1)}, bf16[64,2048]{1,0:T(8,128)(2,1)S(1)}, u32[]{:S(2)}, u32[]{:S(2)}) collective-permute-start(bf16[64,2048]{1,0:T(8,128)(2,1)S(1)} %collective-permute-done.24.refs_3_), channel_id=1, source_target_pairs={{0,1},{1,0},{2,3},{3,2},{4,5},{5,4},{6,7},{7,6},{8,10},{9,11},{10,... | collective-permute-start | bytes 786440 | tf_op jit(solution)/shard_map/ppermute | solution.py:408
  88.5 14.0 %collective-permute-start.33 = (bf16[64,2048]{1,0:T(8,128)(2,1)S(1)}, bf16[64,2048]{1,0:T(8,128)(2,1)S(1)}, u32[]{:S(2)}, u32[]{:S(2)}) collective-permute-start(bf16[64,2048]{1,0:T(8,128)(2,1)S(1)} %collective-permute-done.25.refs_1_), channel_id=1, source_target_pairs={{0,1},{1,0},{2,3},{3,2},{4,5},{5,4},{6,7},{7,6},{8,9},{9,8},{10,11... | collective-permute-start | bytes 786440 | tf_op jit(solution)/shard_map/ppermute | solution.py:408
  94.5 8.1 %collective-permute-start.32 = (bf16[64,2048]{1,0:T(8,128)(2,1)S(1)}, bf16[64,2048]{1,0:T(8,128)(2,1)S(1)}, u32[]{:S(2)}, u32[]{:S(2)}) collective-permute-start(bf16[64,2048]{1,0:T(8,128)(2,1)S(1)} %collective-permute-done.28.refs_2_), channel_id=1, source_target_pairs={{0,1},{1,0},{2,3},{3,2},{4,5},{5,4},{6,7},{7,6},{8,10},{9,11},{10,... | collective-permute-start | bytes 786440 | tf_op jit(solution)/shard_map/ppermute | solution.py:408
  98.4 12.2 %collective-permute-start.29 = (f32[1,64]{1,0:T(1,128)S(1)}, f32[1,64]{1,0:T(1,128)S(1)}, u32[]{:S(2)}, u32[]{:S(2)}) collective-permute-start(f32[1,64]{1,0:T(1,128)S(1)} %get-tuple-element.93), channel_id=1, source_target_pairs={{0,2},{1,3},{2,0},{3,1},{4,6},{5,7},{6,4},{7,5},{8,10},{9,11},{10,... | collective-permute-start | bytes 776 | tf_op jit(solution)/shard_map/ppermute | solution.py:408
  100.2 12.0 %collective-permute-start.30 = (f32[1,64]{1,0:T(1,128)S(1)}, f32[1,64]{1,0:T(1,128)S(1)}, u32[]{:S(2)}, u32[]{:S(2)}) collective-permute-start(f32[1,64]{1,0:T(1,128)S(1)} %get-tuple-element.92), channel_id=1, source_target_pairs={{0,1},{1,0},{2,3},{3,2},{4,5},{5,4},{6,7},{7,6},{8,9},{9,8},{10,11... | collective-permute-start | bytes 776 | tf_op jit(solution)/shard_map/ppermute | solution.py:408
  100.2 14.1 %collective-permute-start.31 = (f32[1,64]{1,0:T(1,128)S(1)}, f32[1,64]{1,0:T(1,128)S(1)}, u32[]{:S(2)}, u32[]{:S(2)}) collective-permute-start(f32[1,64]{1,0:T(1,128)S(1)} %get-tuple-element.91), channel_id=1, source_target_pairs={{0,4},{1,5},{2,6},{3,7},{4,0},{5,1},{6,2},{7,3},{8,12},{9,13},{10,... | collective-permute-start | bytes 776 | tf_op jit(solution)/shard_map/ppermute | solution.py:408
  107.1 7.2 %collective-permute-start.34 = (f32[1,64]{1,0:T(1,128)S(1)}, f32[1,64]{1,0:T(1,128)S(1)}, u32[]{:S(2)}, u32[]{:S(2)}) collective-permute-start(f32[1,64]{1,0:T(1,128)S(1)} %get-tuple-element.90), channel_id=1, source_target_pairs={{0,7},{1,6},{2,5},{3,4},{4,3},{5,2},{6,1},{7,0},{8,15},{9,14},{10,... | collective-permute-start | bytes 776 | tf_op jit(solution)/shard_map/ppermute | solution.py:408
  109.9 5.3 %collective-permute-start.35 = (f32[1,64]{1,0:T(1,128)S(1)}, f32[1,64]{1,0:T(1,128)S(1)}, u32[]{:S(2)}, u32[]{:S(2)}) collective-permute-start(f32[1,64]{1,0:T(1,128)S(1)} %get-tuple-element.89), channel_id=1, source_target_pairs={{0,5},{1,4},{2,7},{3,6},{4,1},{5,0},{6,3},{7,2},{8,14},{9,15},{10,... | collective-permute-start | bytes 776 | tf_op jit(solution)/shard_map/ppermute | solution.py:408
  110.6 5.3 %collective-permute-start.36 = (f32[1,64]{1,0:T(1,128)S(1)}, f32[1,64]{1,0:T(1,128)S(1)}, u32[]{:S(2)}, u32[]{:S(2)}) collective-permute-start(f32[1,64]{1,0:T(1,128)S(1)} %get-tuple-element.88), channel_id=1, source_target_pairs={{0,6},{1,7},{2,4},{3,5},{4,2},{5,3},{6,0},{7,1},{8,13},{9,12},{10,... | collective-permute-start | bytes 776 | tf_op jit(solution)/shard_map/ppermute | solution.py:408
  112.2 4.4 %collective-permute-start.37 = (f32[1,64]{1,0:T(1,128)S(1)}, f32[1,64]{1,0:T(1,128)S(1)}, u32[]{:S(2)}, u32[]{:S(2)}) collective-permute-start(f32[1,64]{1,0:T(1,128)S(1)} %get-tuple-element.87), channel_id=1, source_target_pairs={{0,3},{1,2},{2,1},{3,0},{4,7},{5,6},{6,5},{7,4},{8,11},{9,10},{10,... | collective-permute-start | bytes 776 | tf_op jit(solution)/shard_map/ppermute | solution.py:408
  (9 other events, 32.1 us)
